TPU v7x, 32 devices: a whole 2x2x4 slice. The times are simulated.
32 devices in a mesh: dp: 8 (over z, y), mp: 4 (over x, core).
Axes of the slice: x: 2, y: 2, z: 4, core: 2. Of those that a mesh axis runs over, the one named last changes fastest.
Arguments:
- pixels: bfloat16 [32, 588, 1536], P('dp'), may hold values from -6 to 6
- visible: int32 [32, 147], P('dp'), may hold values from 0 to 587, as said below
- valid: int32 [32, 588, 256], P('dp'), may hold values 0 or 1
- row_dest: int32 [32, 147], P('dp'), may hold values from 0 to 592, as said below
- encoder_in: float32 [768, 7, 768], P('dp', None, 'mp'), may hold values from -0.21875 to 0.21875
- encoder_in_moment: float32 [768, 7, 768], P('dp', None, 'mp'), may hold values from -3.7252903e-08 to 3.7252903e-08
- encoder_in_second: float32 [768, 7, 768], P('dp', None, 'mp'), may hold values from 1.6837284e-16 to 6.671377e-16
- encoder_out: float32 [5, 768, 768], P(None, 'mp', 'dp'), may hold values from -0.15625 to 0.15625
- encoder_out_moment: float32 [5, 768, 768], P(None, 'mp', 'dp'), may hold values from -3.7252903e-08 to 3.7252903e-08
- encoder_out_second: float32 [5, 768, 768], P(None, 'mp', 'dp'), may hold values from 1.6837284e-16 to 6.671377e-16
- decoder_in: float32 [512, 7, 512], P('dp', None, 'mp'), may hold values from -0.25 to 0.25
- decoder_in_moment: float32 [512, 7, 512], P('dp', None, 'mp'), may hold values from -3.7252903e-08 to 3.7252903e-08
- decoder_in_second: float32 [512, 7, 512], P('dp', None, 'mp'), may hold values from 1.6837284e-16 to 6.671377e-16
- decoder_out: float32 [5, 512, 512], P(None, 'mp', 'dp'), may hold values from -0.1875 to 0.1875
- decoder_out_moment: float32 [5, 512, 512], P(None, 'mp', 'dp'), may hold values from -3.7252903e-08 to 3.7252903e-08
- decoder_out_second: float32 [5, 512, 512], P(None, 'mp', 'dp'), may hold values from 1.6837284e-16 to 6.671377e-16
- patch_embed: float32 [1536, 768], P('dp'), may hold values from -0.15625 to 0.15625
- patch_embed_moment: float32 [1536, 768], P('dp'), may hold values from -7.450581e-09 to 7.450581e-09
- patch_embed_second: float32 [1536, 768], P('dp'), may hold values from 6.671377e-18 to 2.6685508e-17
- decoder_embed: float32 [768, 512], P('dp'), may hold values from -0.21875 to 0.21875
- decoder_embed_moment: float32 [768, 512], P('dp'), may hold values from -3.7252903e-08 to 3.7252903e-08
- decoder_embed_second: float32 [768, 512], P('dp'), may hold values from 1.6837284e-16 to 6.671377e-16
- pixel_head: float32 [512, 1536], P('dp', 'mp'), may hold values from -0.25 to 0.25
- pixel_head_moment: float32 [512, 1536], P('dp', 'mp'), may hold values from -3.7252903e-08 to 3.7252903e-08
- pixel_head_second: float32 [512, 1536], P('dp', 'mp'), may hold values from 1.6837284e-16 to 6.671377e-16
- norm_params: float32 [8192], P('dp'), may hold values from -3 to 3
- norm_params_moment: float32 [8192], P('dp'), may hold values from -3.5762787e-07 to 3.5762787e-07
- norm_params_second: float32 [8192], P('dp'), may hold values from 1.2707385e-14 to 5.082954e-14
Outputs:
- loss_sum: float32 [], replicated
- valid_count: float32 [], replicated
- grad_norm: float32 [], replicated
- new_encoder_in: float32 [768, 7, 768], P('dp', None, 'mp')
- new_encoder_in_moment: float32 [768, 7, 768], P('dp', None, 'mp')
- new_encoder_in_second: float32 [768, 7, 768], P('dp', None, 'mp')
- new_encoder_out: float32 [5, 768, 768], P(None, 'mp', 'dp')
- new_encoder_out_moment: float32 [5, 768, 768], P(None, 'mp', 'dp')
- new_encoder_out_second: float32 [5, 768, 768], P(None, 'mp', 'dp')
- new_decoder_in: float32 [512, 7, 512], P('dp', None, 'mp')
- new_decoder_in_moment: float32 [512, 7, 512], P('dp', None, 'mp')
- new_decoder_in_second: float32 [512, 7, 512], P('dp', None, 'mp')
- new_decoder_out: float32 [5, 512, 512], P(None, 'mp', 'dp')
- new_decoder_out_moment: float32 [5, 512, 512], P(None, 'mp', 'dp')
- new_decoder_out_second: float32 [5, 512, 512], P(None, 'mp', 'dp')
- new_patch_embed: float32 [1536, 768], P('dp')
- new_patch_embed_moment: float32 [1536, 768], P('dp')
- new_patch_embed_second: float32 [1536, 768], P('dp')
- new_decoder_embed: float32 [768, 512], P('dp')
- new_decoder_embed_moment: float32 [768, 512], P('dp')
- new_decoder_embed_second: float32 [768, 512], P('dp')
- new_pixel_head: float32 [512, 1536], P('dp', 'mp')
- new_pixel_head_moment: float32 [512, 1536], P('dp', 'mp')
- new_pixel_head_second: float32 [512, 1536], P('dp', 'mp')
- new_norm_params: float32 [8192], P('dp')
- new_norm_params_moment: float32 [8192], P('dp')
- new_norm_params_second: float32 [8192], P('dp')
Inputs may be any that keep to these rules, and one draw needn't show every extreme that they name: `visible`: each row holds 147 different token numbers in rising order. `row_dest`: let N be the number of dp indices, 74 = ceil(4 * 147 / N) and 592 = N * 74. All entries of an item slot equal 592 when the slot is empty, and a device's live slots come first. The live slots of a device and of the device half the dp axis away number 4 together. A live entry is owner * 74 + k: owner is the dp index of the device that processes this visible row, k counts the earlier rows of the same device sent to that owner. Entries of one device differ; each owner receives exactly 294 = 294 rows; some device sends 74 rows to one owner and some device has no live slot.
All inputs are finite; a program needn't handle non-finite values. No bound on the sum of `valid` on one device may be relied on, other than what follows from the above.
Results may differ from a plain program's by a relative error of at most 0.0075.
Values may be sent and summed in bfloat16 or wider, within the bound.
No kernel may reach another device: no remote copies, remote signals or barrier semaphores. Data moves between devices by JAX's collectives and lax.ppermute only.
A program may use at most 256 MiB of HBM per device.

v0:
```python
import jax
import jax.numpy as jnp
from jax import lax
from jax.sharding import PartitionSpec as P

HEADS_ENC = 12
HEADS_DEC = 16
STEP = 10


EPS_NORM = 1e-05
EPS_PIX = 1e-06
CLIP = 0.0002
LR_MATRIX = 0.03
LR_NORM = 0.5
BETA_ONE = 0.9
BETA_TWO = 0.95
ADAM_EPS = 1e-10
DECAY = 0.05
FLOAT_TYPE = jnp.float32
NARROW_TYPE = jnp.bfloat16


def matmul(left, right):
    return jnp.dot(left, right, preferred_element_type=FLOAT_TYPE)


def rows_of(tensor):
    return tensor.reshape(-1, tensor.shape[-1])


def exact_gelu(values):
    return jax.nn.gelu(values, approximate=False)


def sincos(count_rows, features):
    places = jnp.arange(count_rows, dtype=FLOAT_TYPE)[:, None]
    half_width = features // 2
    freqs = jnp.exp(-jnp.log(10000.0) * jnp.arange(half_width, dtype=FLOAT_TYPE) / half_width)
    angles = places * freqs[None, :]
    return jnp.concatenate([jnp.sin(angles), jnp.cos(angles)], axis=1)


def norm_fwd(stream, gain_row, shift_row):
    centred = stream - jnp.mean(stream, -1, keepdims=True)
    inverse = lax.rsqrt(jnp.mean(centred * centred, -1, keepdims=True) + EPS_NORM)
    scaled = centred * inverse
    return (scaled * gain_row + shift_row, (scaled, inverse))


def norm_back(upstream, kept_state, gain_row):
    scaled, inverse = kept_state
    weighted = upstream * gain_row
    input_grad = inverse * (
        weighted
        - jnp.mean(weighted, -1, keepdims=True)
        - scaled * jnp.mean(weighted * scaled, -1, keepdims=True)
    )
    leading = tuple(range(upstream.ndim - 1))
    return (input_grad, jnp.sum(upstream * scaled, leading), jnp.sum(upstream, leading))


def block_parts(w_in, w_out):
    features = w_in.shape[0]
    return (
        w_in[:, :3],
        w_in[:, 3:].reshape(features, -1),
        w_out[0],
        w_out[1:].reshape(-1, w_out.shape[2]),
    )


def block_grads(qkv_grad, up_grad, proj_grad, down_grad):
    features = qkv_grad.shape[0]
    local_width = qkv_grad.shape[2]
    in_grad = jnp.concatenate([qkv_grad, up_grad.reshape(features, -1, local_width)], axis=1)
    out_grad = jnp.concatenate(
        [proj_grad[None], down_grad.reshape(-1, local_width, features)], axis=0
    )
    return (in_grad, out_grad)


def attn_fwd(stream, w_qkv, w_proj, gain_row, shift_row, head_count):
    normed, norm_kept = norm_fwd(stream, gain_row, shift_row)
    normed_low = normed.astype(NARROW_TYPE)
    batches, length, features = stream.shape
    local_width = w_qkv.shape[2]
    head_size = local_width // head_count
    triple = jnp.einsum(
        "bld,dtc->tblc", normed_low, w_qkv, preferred_element_type=FLOAT_TYPE
    ).astype(NARROW_TYPE)
    split_heads = triple.reshape(3, batches, length, head_count, head_size)
    scores = jnp.einsum(
        "bqhd,bkhd->bhqk", split_heads[0], split_heads[1], preferred_element_type=FLOAT_TYPE
    ) * head_size ** (-0.5)
    log_total = jax.nn.logsumexp(scores, axis=-1, keepdims=True)
    attend_low = jnp.exp(scores - log_total).astype(NARROW_TYPE)
    mixture = jnp.einsum(
        "bhqk,bkhd->bqhd", attend_low, split_heads[2], preferred_element_type=FLOAT_TYPE
    )
    mixture = mixture.astype(NARROW_TYPE).reshape(batches, length, local_width)
    partial_value = jnp.einsum("blc,cd->bld", mixture, w_proj, preferred_element_type=FLOAT_TYPE)
    branch = lax.psum(partial_value, "mp")
    return (stream + branch, (normed_low, norm_kept, split_heads, mixture, log_total))


def attn_back(upstream, kept_state, w_qkv, w_proj, gain_row, head_count):
    normed_low, norm_kept, split_heads, mixture, log_total = kept_state
    batches, length, local_width = mixture.shape
    head_size = local_width // head_count
    factor = head_size ** (-0.5)
    upstream_low = upstream.astype(NARROW_TYPE)
    proj_grad = jnp.einsum("blc,bld->cd", mixture, upstream_low, preferred_element_type=FLOAT_TYPE)
    mix_grad = jnp.einsum("bld,cd->blc", upstream_low, w_proj, preferred_element_type=FLOAT_TYPE)
    mix_grad = mix_grad.astype(NARROW_TYPE).reshape(batches, length, head_count, head_size)
    scores = (
        jnp.einsum(
            "bqhd,bkhd->bhqk", split_heads[0], split_heads[1], preferred_element_type=FLOAT_TYPE
        )
        * factor
    )
    attend_full = jnp.exp(scores - log_total)
    value_grad = jnp.einsum(
        "bhqk,bqhd->bkhd",
        attend_full.astype(NARROW_TYPE),
        mix_grad,
        preferred_element_type=FLOAT_TYPE,
    ).astype(NARROW_TYPE)
    attend_grad = jnp.einsum(
        "bqhd,bkhd->bhqk", mix_grad, split_heads[2], preferred_element_type=FLOAT_TYPE
    )
    score_grad = attend_full * (attend_grad - jnp.sum(attend_full * attend_grad, -1, keepdims=True))
    score_grad = score_grad.astype(NARROW_TYPE)
    query_grad = (
        jnp.einsum("bhqk,bkhd->bqhd", score_grad, split_heads[1], preferred_element_type=FLOAT_TYPE)
        * factor
    ).astype(NARROW_TYPE)
    key_grad = (
        jnp.einsum("bhqk,bqhd->bkhd", score_grad, split_heads[0], preferred_element_type=FLOAT_TYPE)
        * factor
    ).astype(NARROW_TYPE)
    triple_grad = jnp.stack([query_grad, key_grad, value_grad]).reshape(
        3, batches, length, local_width
    )
    qkv_grad = jnp.einsum(
        "bld,tblc->dtc", normed_low, triple_grad, preferred_element_type=FLOAT_TYPE
    )
    normed_grad = lax.psum(
        jnp.einsum("tblc,dtc->bld", triple_grad, w_qkv, preferred_element_type=FLOAT_TYPE).astype(
            jnp.bfloat16
        ),
        "mp",
    ).astype(jnp.float32)
    input_grad, gain_grad, shift_grad = norm_back(normed_grad, norm_kept, gain_row)
    return (upstream + input_grad, qkv_grad, proj_grad, gain_grad, shift_grad)


def mlp_fwd(stream, w_up, w_down, gain_row, shift_row):
    normed, norm_kept = norm_fwd(stream, gain_row, shift_row)
    normed_low = rows_of(normed).astype(NARROW_TYPE)
    upward = matmul(normed_low, w_up)
    hidden = exact_gelu(upward).astype(NARROW_TYPE)
    branch = lax.psum(matmul(hidden, w_down), "mp")
    return (stream + branch.reshape(stream.shape), (normed_low, norm_kept, upward, hidden))


def mlp_back(upstream, kept_state, w_up, w_down, gain_row):
    normed_low, norm_kept, upward, hidden = kept_state
    upstream_low = rows_of(upstream).astype(NARROW_TYPE)
    down_grad = matmul(hidden.T, upstream_low)
    hidden_grad = matmul(upstream_low, w_down.T)
    upward_grad = jax.vjp(exact_gelu, upward)[1](hidden_grad)[0].astype(NARROW_TYPE)
    up_grad = matmul(normed_low.T, upward_grad)
    normed_grad = (
        lax.psum(matmul(upward_grad, w_up.T).astype(jnp.bfloat16), "mp")
        .astype(jnp.float32)
        .reshape(upstream.shape)
    )
    input_grad, gain_grad, shift_grad = norm_back(normed_grad, norm_kept, gain_row)
    return (upstream + input_grad, up_grad, down_grad, gain_grad, shift_grad)


def tail_fwd(rows, w_up, w_down, gains, w_embed):
    stream, mlp_kept = mlp_fwd(rows, w_up, w_down, gains[2], gains[3])
    normed, norm_kept = norm_fwd(stream, gains[4], gains[5])
    normed_low = normed.astype(NARROW_TYPE)
    return (matmul(normed_low, w_embed), (mlp_kept, norm_kept, normed_low))


def tail_back(grad_low, kept_state, w_up, w_down, gains, w_embed):
    mlp_kept, norm_kept, normed_low = kept_state
    embed_grad = matmul(normed_low.T, grad_low)
    normed_grad = matmul(grad_low, w_embed.T)
    stream_grad, gain_five, shift_five = norm_back(normed_grad, norm_kept, gains[4])
    input_grad, up_grad, down_grad, gain_two, shift_two = mlp_back(
        stream_grad, mlp_kept, w_up, w_down, gains[2]
    )
    return (
        input_grad,
        (up_grad, down_grad, embed_grad, gain_two, shift_two, gain_five, shift_five),
    )


def adam_update(weight, moment, second, gradient, step_rate, decay_rate):
    moment = BETA_ONE * moment + (1.0 - BETA_ONE) * gradient
    second = BETA_TWO * second + (1.0 - BETA_TWO) * gradient * gradient
    fixed_one = moment / (1.0 - BETA_ONE**STEP)
    fixed_two = second / (1.0 - BETA_TWO**STEP)
    weight = weight - step_rate * (
        fixed_one / (jnp.sqrt(fixed_two) + ADAM_EPS) + decay_rate * weight
    )
    return [weight, moment, second]


def on_device(
    pixels,
    visible,
    valid,
    row_dest,
    encoder_in,
    encoder_in_moment,
    encoder_in_second,
    encoder_out,
    encoder_out_moment,
    encoder_out_second,
    decoder_in,
    decoder_in_moment,
    decoder_in_second,
    decoder_out,
    decoder_out_moment,
    decoder_out_second,
    patch_embed,
    patch_embed_moment,
    patch_embed_second,
    decoder_embed,
    decoder_embed_moment,
    decoder_embed_second,
    pixel_head,
    pixel_head_moment,
    pixel_head_second,
    norm_params,
    norm_params_moment,
    norm_params_second,
):
    masters = [
        encoder_in,
        encoder_out,
        decoder_in,
        decoder_out,
        patch_embed,
        decoder_embed,
        pixel_head,
        norm_params,
    ]
    moments = [
        encoder_in_moment,
        encoder_out_moment,
        decoder_in_moment,
        decoder_out_moment,
        patch_embed_moment,
        decoder_embed_moment,
        pixel_head_moment,
        norm_params_moment,
    ]
    seconds = [
        encoder_in_second,
        encoder_out_second,
        decoder_in_second,
        decoder_out_second,
        patch_embed_second,
        decoder_embed_second,
        pixel_head_second,
        norm_params_second,
    ]
    model_size = lax.axis_size("mp")
    data_size = lax.axis_size("dp")
    gathered = (
        lax.all_gather(encoder_in.astype(NARROW_TYPE), "dp", axis=0, tiled=True),
        lax.all_gather(encoder_out.astype(NARROW_TYPE), "dp", axis=2, tiled=True),
        lax.all_gather(decoder_in.astype(NARROW_TYPE), "dp", axis=0, tiled=True),
        lax.all_gather(decoder_out.astype(NARROW_TYPE), "dp", axis=2, tiled=True),
        lax.all_gather(patch_embed.astype(NARROW_TYPE), "dp", axis=0, tiled=True),
        lax.all_gather(decoder_embed.astype(NARROW_TYPE), "dp", axis=0, tiled=True),
        lax.all_gather(pixel_head.astype(NARROW_TYPE), "dp", axis=0, tiled=True),
        lax.all_gather(norm_params.astype(NARROW_TYPE), "dp", axis=0, tiled=True),
    )
    full_patch = gathered[4]
    full_embed = gathered[5]
    full_head = gathered[6]
    width_enc = full_patch.shape[1]
    width_dec = full_embed.shape[1]
    norm_full = gathered[7].astype(FLOAT_TYPE)
    enc_gains = norm_full[: 6 * width_enc].reshape(6, width_enc)
    dec_gains = norm_full[6 * width_enc : 6 * width_enc + 6 * width_dec].reshape(6, width_dec)
    mask_token = norm_full[6 * width_enc + 6 * width_dec : 6 * width_enc + 7 * width_dec]
    enc_qkv, enc_up, enc_proj, enc_down = block_parts(gathered[0], gathered[1])
    dec_qkv, dec_up, dec_proj, dec_down = block_parts(gathered[2], gathered[3])
    enc_heads = HEADS_ENC // model_size
    dec_heads = HEADS_DEC // model_size
    slot_total = pixels.shape[0]
    vis_count = visible.shape[1]
    buf_rows = data_size * -(-(slot_total * vis_count) // data_size)
    slot_alive = row_dest[:, 0] < buf_rows
    alive_slot = slot_alive.astype(FLOAT_TYPE)
    slot_count, tokens, pix_width = pixels.shape
    pixel_float = pixels.astype(FLOAT_TYPE)
    centred = pixel_float - jnp.mean(pixel_float, -1, keepdims=True)
    target = centred * lax.rsqrt(jnp.mean(centred * centred, -1, keepdims=True) + EPS_PIX)
    slot_rows = jnp.arange(slot_count)[:, None]
    shown_mask = jnp.zeros((slot_count, tokens), FLOAT_TYPE).at[slot_rows, visible].set(1.0)
    seen_rows = rows_of(jnp.take_along_axis(pixels, visible[:, :, None], axis=1))
    stream = matmul(seen_rows, full_patch).reshape(slot_count, vis_count, width_enc)
    stream = stream + sincos(tokens, width_enc)[visible]
    stream, enc_attn_kept = attn_fwd(
        stream, enc_qkv, enc_proj, enc_gains[0], enc_gains[1], enc_heads
    )
    flat_rows = rows_of(stream)
    decoded_rows, tail_kept = tail_fwd(flat_rows, enc_up, enc_down, enc_gains, full_embed)
    placed = (
        jnp.zeros((slot_count, tokens, width_dec), FLOAT_TYPE)
        .at[slot_rows, visible]
        .set(decoded_rows.reshape(slot_count, vis_count, width_dec))
    )
    stream = placed + (1.0 - shown_mask)[:, :, None] * mask_token + sincos(tokens, width_dec)
    stream, dec_attn_kept = attn_fwd(
        stream, dec_qkv, dec_proj, dec_gains[0], dec_gains[1], dec_heads
    )
    stream, dec_mlp_kept = mlp_fwd(stream, dec_up, dec_down, dec_gains[2], dec_gains[3])
    normed, head_norm_kept = norm_fwd(stream, dec_gains[4], dec_gains[5])
    normed_low = normed.astype(NARROW_TYPE)
    predicted = jnp.einsum("btd,dp->btp", normed_low, full_head, preferred_element_type=FLOAT_TYPE)
    column_count = full_head.shape[1]
    column_start = lax.axis_index("mp") * column_count
    goal_cols = lax.dynamic_slice_in_dim(target, column_start, column_count, 2)
    valid_tiled = jnp.tile(valid.astype(FLOAT_TYPE), (1, 1, pix_width // valid.shape[2]))
    valid_cols = lax.dynamic_slice_in_dim(valid_tiled, column_start, column_count, 2)
    loss_weights = (1.0 - shown_mask)[:, :, None] * valid_cols * alive_slot[:, None, None]
    errors = predicted - goal_cols
    loss_sum, valid_count = lax.psum(
        (jnp.sum(loss_weights * errors * errors), jnp.sum(loss_weights)), ("dp", "mp")
    )
    pred_grad = (loss_weights * (2.0 * errors) * (1.0 / valid_count)).astype(NARROW_TYPE)
    head_grad = jnp.einsum("btd,btp->dp", normed_low, pred_grad, preferred_element_type=FLOAT_TYPE)
    normed_grad = lax.psum(
        jnp.einsum("btp,dp->btd", pred_grad, full_head, preferred_element_type=FLOAT_TYPE).astype(
            jnp.bfloat16
        ),
        "mp",
    ).astype(jnp.float32)
    stream_grad, dec_gain_five, dec_shift_five = norm_back(
        normed_grad, head_norm_kept, dec_gains[4]
    )
    stream_grad, dec_up_grad, dec_down_grad, dec_gain_three, dec_shift_three = mlp_back(
        stream_grad, dec_mlp_kept, dec_up, dec_down, dec_gains[2]
    )
    stream_grad, dec_qkv_grad, dec_proj_grad, dec_gain_one, dec_shift_one = attn_back(
        stream_grad, dec_attn_kept, dec_qkv, dec_proj, dec_gains[0], dec_heads
    )
    mask_grad = jnp.sum((1.0 - shown_mask)[:, :, None] * stream_grad, axis=(0, 1))
    decoded_grad = rows_of(jnp.take_along_axis(stream_grad, visible[:, :, None], axis=1)).astype(
        NARROW_TYPE
    )
    flat_grad, tail_grads = tail_back(
        decoded_grad, tail_kept, enc_up, enc_down, enc_gains, full_embed
    )
    stream_grad = flat_grad.reshape(slot_count, vis_count, width_enc)
    stream_grad, enc_qkv_grad, enc_proj_grad, enc_gain_one, enc_shift_one = attn_back(
        stream_grad, enc_attn_kept, enc_qkv, enc_proj, enc_gains[0], enc_heads
    )
    patch_grad = matmul(seen_rows.T, rows_of(stream_grad).astype(NARROW_TYPE))
    enc_in_grad, enc_out_grad = block_grads(
        enc_qkv_grad, tail_grads[0], enc_proj_grad, tail_grads[1]
    )
    dec_in_grad, dec_out_grad = block_grads(dec_qkv_grad, dec_up_grad, dec_proj_grad, dec_down_grad)
    norm_pieces = jnp.concatenate(
        [
            enc_gain_one,
            enc_shift_one,
            tail_grads[3],
            tail_grads[4],
            tail_grads[5],
            tail_grads[6],
            dec_gain_one,
            dec_shift_one,
            dec_gain_three,
            dec_shift_three,
            dec_gain_five,
            dec_shift_five,
            mask_grad,
        ]
    )
    norm_total = norm_params.shape[0] * data_size
    norm_grad = jnp.concatenate(
        [norm_pieces, jnp.zeros((norm_total - norm_pieces.shape[0],), FLOAT_TYPE)]
    )
    reduced = (
        lax.psum_scatter(enc_in_grad, "dp", scatter_dimension=0, tiled=True),
        lax.psum_scatter(enc_out_grad, "dp", scatter_dimension=2, tiled=True),
        lax.psum_scatter(dec_in_grad, "dp", scatter_dimension=0, tiled=True),
        lax.psum_scatter(dec_out_grad, "dp", scatter_dimension=2, tiled=True),
        lax.psum_scatter(patch_grad, "dp", scatter_dimension=0, tiled=True),
        lax.psum_scatter(tail_grads[2], "dp", scatter_dimension=0, tiled=True),
        lax.psum_scatter(head_grad, "dp", scatter_dimension=0, tiled=True),
        lax.psum_scatter(norm_grad, "dp", scatter_dimension=0, tiled=True),
    )
    split_squares = sum((jnp.sum(reduced[number] * reduced[number]) for number in (0, 1, 2, 3, 6)))
    shared_squares = sum((jnp.sum(reduced[number] * reduced[number]) for number in (4, 5, 7)))
    grad_norm = jnp.sqrt(lax.psum(split_squares + shared_squares / model_size, ("dp", "mp")))
    clip_scale = CLIP / jnp.maximum(grad_norm, CLIP)
    updated = []
    for number in range(8):
        step_rate = LR_NORM if number == 7 else LR_MATRIX
        decay_rate = 0.0 if number == 7 else DECAY
        updated.extend(
            adam_update(
                masters[number],
                moments[number],
                seconds[number],
                reduced[number] * clip_scale,
                step_rate,
                decay_rate,
            )
        )
    return (
        loss_sum,
        valid_count,
        grad_norm,
        updated[0],
        updated[1],
        updated[2],
        updated[3],
        updated[4],
        updated[5],
        updated[6],
        updated[7],
        updated[8],
        updated[9],
        updated[10],
        updated[11],
        updated[12],
        updated[13],
        updated[14],
        updated[15],
        updated[16],
        updated[17],
        updated[18],
        updated[19],
        updated[20],
        updated[21],
        updated[22],
        updated[23],
    )


def solution(mesh):
    return jax.shard_map(
        on_device,
        mesh=mesh,
        in_specs=(
            P("dp", None, None),
            P("dp", None),
            P("dp", None, None),
            P("dp", None),
            P("dp", None, "mp"),
            P("dp", None, "mp"),
            P("dp", None, "mp"),
            P(None, "mp", "dp"),
            P(None, "mp", "dp"),
            P(None, "mp", "dp"),
            P("dp", None, "mp"),
            P("dp", None, "mp"),
            P("dp", None, "mp"),
            P(None, "mp", "dp"),
            P(None, "mp", "dp"),
            P(None, "mp", "dp"),
            P("dp", None),
            P("dp", None),
            P("dp", None),
            P("dp", None),
            P("dp", None),
            P("dp", None),
            P("dp", "mp"),
            P("dp", "mp"),
            P("dp", "mp"),
            P("dp"),
            P("dp"),
            P("dp"),
        ),
        out_specs=(
            P(),
            P(),
            P(),
            P("dp", None, "mp"),
            P("dp", None, "mp"),
            P("dp", None, "mp"),
            P(None, "mp", "dp"),
            P(None, "mp", "dp"),
            P(None, "mp", "dp"),
            P("dp", None, "mp"),
            P("dp", None, "mp"),
            P("dp", None, "mp"),
            P(None, "mp", "dp"),
            P(None, "mp", "dp"),
            P(None, "mp", "dp"),
            P("dp", None),
            P("dp", None),
            P("dp", None),
            P("dp", None),
            P("dp", None),
            P("dp", None),
            P("dp", "mp"),
            P("dp", "mp"),
            P("dp", "mp"),
            P("dp"),
            P("dp"),
            P("dp"),
        ),
        check_vma=False,
    )
```

profile of v0, /device:TPU:0, one launch (start us, length us, event | category | flops | bytes accessed | tf_op | source)
XLA Modules:
  0.0 1806.0 jit_solution(9612343188999287847)
XLA Ops:
  39.2 28.4 %all_gather.25 = bf16[8192]{0:T(1024)(128)(2,1)S(1)} all-gather(bf16[1024]{0:T(1024)(128)(2,1)S(1)} %convert_element_type.234), channel_id=1, replica_groups=mesh['dp'=8,'mp'=4] {'dp'}, dimensions={0}, use_global_device_ids=true | all-gather | bytes 18432 | tf_op jit(solution)/shard_map/all_gather | solution.py:285
  78.3 57.9 %all-gather.6.cloned.1.call-done = bf16[768,7,192]{2,1,0:T(8,128)(2,1)} async-done(((bf16[96,7,192]{2,1,0:T(8,128)(2,1)}), bf16[768,7,192]{2,1,0:T(8,128)(2,1)}) %all-gather.6.cloned.1.call-update) | async-done | bytes 2064400 | tf_op jit(solution)/shard_map/all_gather | solution.py:278
  140.6 49.1 %all-gather.4.cloned.1.call-done = bf16[1536,768]{1,0:T(8,128)(2,1)} async-done(((bf16[192,768]{1,0:T(8,128)(2,1)}), bf16[1536,768]{1,0:T(8,128)(2,1)}) %all-gather.4.cloned.1.call-update) | async-done | bytes 2359312 | tf_op jit(solution)/shard_map/all_gather | solution.py:282
  201.2 30.1 %scatter_fusion = f32[4,588]{1,0:T(4,128)S(1)} fusion(f32[4,588]{1,0:T(4,128)S(1)} %broadcast_in_dim.34, s32[588]{0:T(1024)S(1)} %reshape.498, f32[588]{0:T(1024)S(1)} %broadcast.998), kind=kCustom, calls=%fused_computation.3 | custom fusion | bytes 11760 | tf_op jit(solution)/shard_map/scatter | solution.py:310
  234.5 34.3 %all_gather.30 = bf16[5,128,512]{1,2,0:T(8,128)(2,1)} all-gather(bf16[5,128,64]{1,2,0:T(8,128)(2,1)S(1)} %convert_element_type.256), channel_id=1, replica_groups=mesh['dp'=8,'mp'=4] {'dp'}, dimensions={2}, use_global_device_ids=true | all-gather | bytes 737280 | tf_op jit(solution)/shard_map/all_gather | solution.py:281
  296.3 34.3 %all_gather.28 = bf16[768,512]{1,0:T(8,128)(2,1)} all-gather(bf16[96,512]{1,0:T(8,128)(2,1)S(1)} %convert_element_type.248), channel_id=1, replica_groups=mesh['dp'=8,'mp'=4] {'dp'}, dimensions={0}, use_global_device_ids=true | all-gather | bytes 884736 | tf_op jit(solution)/shard_map/all_gather | solution.py:283
  330.6 34.3 %all_gather.29 = bf16[512,7,128]{2,0,1:T(8,128)(2,1)} all-gather(bf16[64,7,128]{2,0,1:T(8,128)(2,1)S(1)} %convert_element_type.250), channel_id=1, replica_groups=mesh['dp'=8,'mp'=4] {'dp'}, dimensions={0}, use_global_device_ids=true | all-gather | bytes 1032192 | tf_op jit(solution)/shard_map/all_gather | solution.py:280
  374.6 72.0 %scatter_fusion.1 = f32[4,588,512]{2,0,1:T(4,128)} fusion(f32[4,588,512]{2,0,1:T(4,128)} %broadcast_in_dim.38, s32[588]{0:T(1024)S(1)} %reshape.498, f32[588,512]{1,0:T(8,128)S(1)} %fusion.221), kind=kCustom, calls=%fused_computation.4 | custom fusion | bytes 3617376 | tf_op jit(solution)/shard_map/scatter | solution.py:322
  493.7 91.7 %all-reduce.16.cloned.1.call-done = f32[4,588,512]{2,1,0:T(8,128)} async-done(((f32[4,588,512]{2,1,0:T(8,128)}), f32[4,588,512]{2,1,0:T(8,128)}) %all-reduce.16.cloned.1.call-update) | async-done | bytes 4816912 | tf_op jit(solution)/shard_map/psum | solution.py:103
  640.3 33.6 %all_gather.31 = bf16[512,384]{1,0:T(8,128)(2,1)} all-gather(bf16[64,384]{1,0:T(8,128)(2,1)} %convert_element_type.261), channel_id=1, replica_groups=mesh['dp'=8,'mp'=4] {'dp'}, dimensions={0}, use_global_device_ids=true | all-gather | bytes 442368 | tf_op jit(solution)/shard_map/all_gather | solution.py:284
  686.1 31.6 %all-reduce.18.cloned.1.call-done = f32[4,588,512]{2,1,0:T(8,128)} async-done(((f32[4,588,512]{2,1,0:T(8,128)}), f32[4,588,512]{2,1,0:T(8,128)}) %all-reduce.18.cloned.1.call-update) | async-done | bytes 4816912 | tf_op jit(solution)/shard_map/psum | solution.py:163
  732.3 39.7 %psum.89 = f32[]{:T(128)} all-reduce(f32[]{:T(128)} %get-tuple-element.168), channel_id=1, replica_groups=mesh['dp'=8,'mp'=4] {'dp','mp'}, use_global_device_ids=true, to_apply=%region_27.28 | all-reduce | flops 1 | bytes 8 | tf_op jit(solution)/shard_map/psum | solution.py:339
  780.8 57.5 %all-reduce.20.cloned.1.call-done = bf16[4,588,512]{2,1,0:T(8,128)(2,1)} async-done(((bf16[4,588,512]{2,1,0:T(8,128)(2,1)}), bf16[4,588,512]{2,1,0:T(8,128)(2,1)}) %all-reduce.20.cloned.1.call-update) | async-done | bytes 2408464 | tf_op jit(solution)/shard_map/psum | solution.py:344
  863.1 56.4 %all-reduce.22.cloned.1.call-done = bf16[2352,512]{1,0:T(8,128)(2,1)} async-done(((bf16[2352,512]{1,0:T(8,128)(2,1)}), bf16[2352,512]{1,0:T(8,128)(2,1)}) %all-reduce.22.cloned.1.call-update) | async-done | bytes 2408464 | tf_op jit(solution)/shard_map/psum | solution.py:175
  998.8 56.3 %all-reduce.24.cloned.1.call-done = bf16[4,588,512]{2,1,0:T(8,128)(2,1)} async-done(((bf16[4,588,512]{2,1,0:T(8,128)(2,1)}), bf16[4,588,512]{2,1,0:T(8,128)(2,1)}) %all-reduce.24.cloned.1.call-update) | async-done | bytes 2408464 | tf_op jit(solution)/shard_map/psum | solution.py:148
  1100.9 35.1 %all-reduce.26.cloned.1.call-done = bf16[588,768]{1,0:T(8,128)(2,1)} async-done(((bf16[588,768]{1,0:T(8,128)(2,1)}), bf16[588,768]{1,0:T(8,128)(2,1)}) %all-reduce.26.cloned.1.call-update) | async-done | bytes 903184 | tf_op jit(solution)/shard_map/psum | solution.py:175
  1262.2 35.4 %all-reduce = f32[8192]{0:T(1024)S(1)} all-reduce(f32[8192]{0:T(1024)S(1)} %constant_dynamic-update-slice_fusion), channel_id=9, replica_groups=mesh['dp'=8,'mp'=4] {'dp'}, use_global_device_ids=true, to_apply=%region_74.75.clone | all-reduce | flops 8192 | bytes 65536
  1298.2 32.6 %reduce-scatter.14.cloned.1.call-done = f32[5,128,64]{1,0,2:T(8,128)} async-done(((f32[5,128,512]{1,0,2:T(8,128)}), f32[5,128,64]{1,0,2:T(8,128)}) %reduce-scatter.14.cloned.1.call-update) | async-done | bytes 163856 | tf_op jit(solution)/shard_map/reduce_scatter | solution.py:400
  1332.5 67.6 %reduce-scatter.12.cloned.1.call-done = f32[64,7,128]{2,0,1:T(8,128)} async-done(((f32[512,7,128]{2,0,1:T(8,128)}), f32[64,7,128]{2,0,1:T(8,128)}) %reduce-scatter.12.cloned.1.call-update) | async-done | bytes 229392 | tf_op jit(solution)/shard_map/reduce_scatter | solution.py:399
  1401.7 65.4 %reduce-scatter.20.cloned.1.call-done = f32[96,512]{1,0:T(8,128)} async-done(((f32[768,512]{1,0:T(8,128)}), f32[96,512]{1,0:T(8,128)}) %reduce-scatter.20.cloned.1.call-update) | async-done | bytes 196624 | tf_op jit(solution)/shard_map/reduce_scatter | solution.py:402
  1468.7 75.8 %reduce-scatter.24.cloned.1.call-done = f32[96,960]{1,0:T(8,128)} async-done(((f32[768,960]{1,0:T(8,128)}), f32[96,960]{1,0:T(8,128)}) %reduce-scatter.24.cloned.1.call-update) | async-done | bytes 368656
  1546.8 90.6 %reduce-scatter.22.cloned.1.call-done = f32[96,1344]{1,0:T(8,128)} async-done(((f32[768,1344]{1,0:T(8,128)}), f32[96,1344]{1,0:T(8,128)}) %reduce-scatter.22.cloned.1.call-update) | async-done | bytes 516112
  1642.7 93.3 %reduce-scatter.18.cloned.1.call-done = f32[192,768]{1,0:T(8,128)} async-done(((f32[1536,768]{1,0:T(8,128)}), f32[192,768]{1,0:T(8,128)}) %reduce-scatter.18.cloned.1.call-update) | async-done | bytes 589840 | tf_op jit(solution)/shard_map/reduce_scatter | solution.py:401
  1739.8 40.7 %all-reduce.1 = (f32[]{:T(128)}, f32[]{:T(128)}) all-reduce(f32[]{:T(128)} %get-tuple-element.169, f32[]{:T(128)S(6)} %add.412), channel_id=1, replica_groups=mesh['dp'=8,'mp'=4] {'dp','mp'}, use_global_device_ids=true, to_apply=%region_25.26 | all-reduce | flops 2 | bytes 16 | tf_op jit(solution)/shard_map/psum | solution.py:339
  (692 shorter events, 536.9 us)
Async XLA Ops:
  7.2 67.0 %all-gather.8.cloned.1.call-start = ((), (), s32[]{:S(2)}) async-start(), calls=%async_computation.9 | async-start | bytes 3538944 | tf_op jit(solution)/shard_map/all_gather | solution.py:279
  9.5 126.7 %all-gather.6.cloned.1.call-start = ((), (), s32[]{:S(2)}) async-start(), calls=%async_computation.8 | async-start | bytes 3538944 | tf_op jit(solution)/shard_map/all_gather | solution.py:278
  11.7 178.0 %all-gather.4.cloned.1.call-start = ((), (), s32[]{:S(2)}) async-start(), calls=%async_computation.7 | async-start | bytes 2654208 | tf_op jit(solution)/shard_map/all_gather | solution.py:282
  12.5 266.3 %all-reduce.12.cloned.1.call-start = ((), (), s32[]{:S(2)}) async-start(), calls=%async_computation.10 | async-start | bytes 3735552 | tf_op jit(solution)/shard_map/psum | solution.py:103
  68.2 213.3 %copy-start.136 = (f32[768]{0:T(1024)}, f32[768]{0:T(1024)S(1)}, u32[]{:S(2)}) copy-start(f32[768]{0:T(1024)S(1)} %get-tuple-element.247) | copy-start | bytes 9220
  201.0 165.3 %all-reduce.14.cloned.1.call-start = ((), (), s32[]{:S(2)}) async-start(), calls=%async_computation.11 | async-start | bytes 3637248 | tf_op jit(solution)/shard_map/psum | solution.py:163
  231.3 222.9 %copy-start.83 = (f32[4,588]{1,0:T(4,128)}, f32[4,588]{1,0:T(4,128)S(1)}, u32[]{:S(2)}) copy-start(f32[4,588]{1,0:T(4,128)S(1)} %broadcast_subtract_fusion) | copy-start | bytes 28228
  294.1 291.2 %all-reduce.16.cloned.1.call-start = ((), (), s32[]{:S(2)}) async-start(), calls=%async_computation.12 | async-start | bytes 9699328 | tf_op jit(solution)/shard_map/psum | solution.py:103
  294.8 159.5 %copy-start.133 = (f32[512]{0:T(512)}, f32[512]{0:T(512)S(1)}, u32[]{:S(2)}) copy-start(f32[512]{0:T(512)S(1)} %get-tuple-element.242) | copy-start | bytes 6148
  294.8 159.5 %copy-start.156 = (f32[512]{0:T(512)}, f32[512]{0:T(512)S(1)}, u32[]{:S(2)}) copy-start(f32[512]{0:T(512)S(1)} %get-tuple-element.243) | copy-start | bytes 6148
  296.2 289.1 %copy-start.10 = (f32[588,512]{1,0:T(8,128)}, f32[588,512]{1,0:T(8,128)S(1)}, u32[]{:S(2)}) copy-start(f32[588,512]{1,0:T(8,128)S(1)} %pad_maximum_fusion.6) | copy-start | bytes 3612676
  491.3 226.5 %all-reduce.18.cloned.1.call-start = ((), (), s32[]{:S(2)}) async-start(), calls=%async_computation.13 | async-start | bytes 9699328 | tf_op jit(solution)/shard_map/psum | solution.py:163
  621.3 217.0 %all-reduce.20.cloned.1.call-start = ((), (), s32[]{:S(2)}) async-start(), calls=%async_computation.14 | async-start | bytes 4849664 | tf_op jit(solution)/shard_map/psum | solution.py:344
  780.7 138.7 %all-reduce.22.cloned.1.call-start = ((), (), s32[]{:S(2)}) async-start(), calls=%async_computation.15 | async-start | bytes 4816896 | tf_op jit(solution)/shard_map/psum | solution.py:175
  862.6 192.4 %all-reduce.24.cloned.1.call-start = ((), (), s32[]{:S(2)}) async-start(), calls=%async_computation.16 | async-start | bytes 4849664 | tf_op jit(solution)/shard_map/psum | solution.py:148
  998.2 137.8 %all-reduce.26.cloned.1.call-start = ((), (), s32[]{:S(2)}) async-start(), calls=%async_computation.17 | async-start | bytes 1818624 | tf_op jit(solution)/shard_map/psum | solution.py:175
  1100.6 138.5 %all-reduce.28.cloned.1.call-start = ((), (), s32[]{:S(2)}) async-start(), calls=%async_computation.21 | async-start | bytes 1867776 | tf_op jit(solution)/shard_map/psum | solution.py:148
  1158.4 102.0 %reduce-scatter.16.cloned.1.call-start = ((), (), s32[]{:S(2)}) async-start(), calls=%async_computation.20 | async-start | bytes 884736 | tf_op jit(solution)/shard_map/reduce_scatter | solution.py:403
  1164.1 166.7 %reduce-scatter.14.cloned.1.call-start = ((), (), s32[]{:S(2)}) async-start(), calls=%async_computation.19 | async-start | bytes 2359296 | tf_op jit(solution)/shard_map/reduce_scatter | solution.py:400
  1189.2 210.9 %reduce-scatter.12.cloned.1.call-start = ((), (), s32[]{:S(2)}) async-start(), calls=%async_computation.18 | async-start | bytes 2064384 | tf_op jit(solution)/shard_map/reduce_scatter | solution.py:399
  1204.9 262.3 %reduce-scatter.20.cloned.1.call-start = ((), (), s32[]{:S(2)}) async-start(), calls=%async_computation.23 | async-start | bytes 1769472 | tf_op jit(solution)/shard_map/reduce_scatter | solution.py:402
  1207.5 337.0 %reduce-scatter.24.cloned.1.call-start = ((), (), s32[]{:S(2)}) async-start(), calls=%async_computation.25 | async-start | bytes 3538944
  1221.3 416.1 %reduce-scatter.22.cloned.1.call-start = ((), (), s32[]{:S(2)}) async-start(), calls=%async_computation.24 | async-start | bytes 4866048
  1236.1 499.9 %reduce-scatter.18.cloned.1.call-start = ((), (), s32[]{:S(2)}) async-start(), calls=%async_computation.22 | async-start | bytes 5308416 | tf_op jit(solution)/shard_map/reduce_scatter | solution.py:401
  (199 other events, 2522.3 us)
Sparse Core Ops, SparseCore 0:
  10.8 63.4 all-gather.7
  77.0 59.1 all-gather.5
  139.0 50.6 all-gather.3
  201.1 46.1 all-reduce.11
  294.2 45.3 all-reduce.13
  491.4 93.9 all-reduce.15
  621.4 96.2 all-reduce.17
  780.8 57.3 all-reduce.19
  862.7 56.6 all-reduce.21
  998.3 56.7 all-reduce.23
  1100.8 35.1 all-reduce.25
  1158.5 35.6 all-reduce.27
  1197.5 62.9 reduce-scatter.15
  1264.2 66.5 reduce-scatter.13
  1334.6 65.4 reduce-scatter.11
  1403.4 63.6 reduce-scatter.19
  1471.0 73.5 reduce-scatter.23
  1548.4 88.9 reduce-scatter.21
  1641.0 94.9 reduce-scatter.17
where the time goes:
time: 1820 us; the launch traced here: 1810 us
  waiting for transfers between devices  875 us (48%)
  local copies, waits for them, and re-layouts  283 us (16%)
  blocking collectives  281 us (15%)
  matrix products  175 us (10%)
  other arithmetic  167 us (9%)
  between operations  25.4 us (1%)
    unnamed x21, waiting for transfers between devices  167 us
    reduce_scatter x1, waiting for transfers between devices, on_device(): lax.psum_scatter(patch_grad, 'dp', scatter_dimension=0, tiled=True)  93.3 us
    psum x2, waiting for transfers between devices, attn_fwd(): branch = lax.psum(partial_value, 'mp')  91.7 us
    psum x2, waiting for transfers between devices, mlp_back(): lax.psum(matmul(upward_grad, w_up.T).astype(jnp.bfloat16), 'mp')  91.5 us
    psum x2, blocking collectives, on_device(): lax.psum((jnp.sum(loss_weights * errors * errors), jnp.sum(loss_weights))...  80.4 us
    dot_general x17, matrix products, matmul(): return jnp.dot(left, right, preferred_element_type=FLOAT_TYPE)  77.5 us
    unnamed x437, local copies, waits for them, and re-layouts  74.6 us
    scatter x1, local copies, waits for them, and re-layouts, on_device(): placed = jnp.zeros((slot_count, tokens, width_dec), FLOAT_TYPE).at[slot_r...  72 us
  transfers between devices with their start and end apart: 19, of which 16 were waited for; matrix products, arithmetic and copies ran while one was open for 12% of the time, Pallas kernels for 0%

commit v1 on v0

v1 whole, which is shorter than its diff:
```python
import math

import jax
import jax.numpy as jnp
from jax import lax
from jax.sharding import Mesh
from jax.sharding import PartitionSpec as P

HEADS_ENC = 12
HEADS_DEC = 16
STEP = 10


EPS_NORM = 1e-05
EPS_PIX = 1e-06
CLIP = 0.0002
LR_MATRIX = 0.03
LR_NORM = 0.5
BETA_ONE = 0.9
BETA_TWO = 0.95
ADAM_EPS = 1e-10
DECAY = 0.05
FLOAT_TYPE = jnp.float32
NARROW_TYPE = jnp.bfloat16
SWAP = [(0, 1), (1, 0)]
LANES = 128
DATA = ("z", "y")


def product(spec, left, right):
    return jnp.einsum(spec, left, right, preferred_element_type=FLOAT_TYPE)


def low(values):
    return values.astype(NARROW_TYPE)


def swap(values, axis="c"):
    return lax.ppermute(values, axis, SWAP)


def join(partial):
    return partial + swap(partial)


def join_low(partial):
    mine = low(partial)
    other = swap(mine)
    return mine.astype(FLOAT_TYPE) + other.astype(FLOAT_TYPE)


def shift(values, axis, step):
    size = lax.axis_size(axis)
    return lax.ppermute(values, axis, [(i, (i + step) % size) for i in range(size)])


def total_over(values, axes):
    for axis in axes:
        size = lax.axis_size(axis)
        if size & (size - 1):
            values = lax.psum(values, axis)
            continue
        step = 1
        while step < size:
            values = values + lax.ppermute(values, axis, [(i, i ^ step) for i in range(size)])
            step *= 2
    return values


def spread(blob):
    sizes = tuple(lax.axis_size(axis) for axis in ("x", "z", "y"))
    if sizes != (2, 4, 2):
        return lax.all_gather(blob, ("x", "z", "y")).reshape(sizes + blob.shape)
    x, z, y = (lax.axis_index(axis) for axis in ("x", "z", "y"))
    column = jnp.zeros((4,) + blob.shape, blob.dtype)
    moving = blob
    for step in range(4):
        column = lax.dynamic_update_index_in_dim(column, moving, (z - step) % 4, 0)
        if step < 3:
            moving = shift(moving, "z", 1)
    from_x = swap(column, "x")
    from_y = swap(column, "y")
    corner = jnp.concatenate([swap(from_x[:2], "y"), swap(from_y[2:], "x")])
    whole = jnp.zeros((2, 4, 2) + blob.shape, blob.dtype)
    for part, at_x, at_y in (
        (column, x, y),
        (from_x, 1 - x, y),
        (from_y, x, 1 - y),
        (corner, 1 - x, 1 - y),
    ):
        whole = lax.dynamic_update_slice(whole, part[None, :, None], (at_x, 0, at_y, 0, 0))
    return whole


def collect(grads):
    sizes = tuple(lax.axis_size(axis) for axis in ("x", "z", "y"))
    shape = grads.shape[3:]
    if sizes != (2, 4, 2):
        flat = grads.reshape((-1,) + shape)
        return lax.psum_scatter(flat, ("x", "z", "y"), scatter_dimension=0).astype(FLOAT_TYPE)
    x, z, y = (lax.axis_index(axis) for axis in ("x", "z", "y"))

    def part(at_x, at_y):
        cut = lax.dynamic_slice(grads, (at_x, 0, at_y, 0, 0), (1, 4, 1) + shape)
        return cut.reshape((4,) + shape)

    def add(*terms):
        return sum(term.astype(FLOAT_TYPE) for term in terms)

    corner = part(1 - x, 1 - y)
    by_x = swap(corner[:2], "x")
    by_y = swap(corner[2:], "y")
    to_y = part(x, 1 - y)
    to_x = part(1 - x, y)
    to_y = jnp.concatenate([low(add(to_y[:2], by_x)), to_y[2:]])
    to_x = jnp.concatenate([to_x[:2], low(add(to_x[2:], by_y))])
    column = low(add(part(x, y), swap(to_y, "y"), swap(to_x, "x")))

    def at(index):
        return lax.dynamic_index_in_dim(column, index % 4, 0, keepdims=False)

    moving = at(z - 1)
    for step in range(1, 4):
        moving = add(shift(moving, "z", 1), at(z - 1 - step))
        if step < 3:
            moving = low(moving)
    return moving


def exact_gelu(values):
    return jax.nn.gelu(values, approximate=False)


def angles_of(places, features):
    half_width = features // 2
    freqs = jnp.exp(-jnp.log(10000.0) * jnp.arange(half_width, dtype=FLOAT_TYPE) / half_width)
    angles = places.astype(FLOAT_TYPE)[:, None] * freqs[None, :]
    return jnp.concatenate([jnp.sin(angles), jnp.cos(angles)], axis=1)


def norm_fwd(stream, gain_row, shift_row):
    centred = stream - jnp.mean(stream, -1, keepdims=True)
    inverse = lax.rsqrt(jnp.mean(centred * centred, -1, keepdims=True) + EPS_NORM)
    scaled = centred * inverse
    return (scaled * gain_row + shift_row, (scaled, inverse))


def norm_back(upstream, kept_state, gain_row):
    scaled, inverse = kept_state
    weighted = upstream * gain_row
    input_grad = inverse * (
        weighted
        - jnp.mean(weighted, -1, keepdims=True)
        - scaled * jnp.mean(weighted * scaled, -1, keepdims=True)
    )
    return (input_grad, jnp.sum(upstream * scaled, 0), jnp.sum(upstream, 0))


def attn_fwd(stream, w_qkv, w_proj, gain_row, shift_row, head_count):
    normed, norm_kept = norm_fwd(stream, gain_row, shift_row)
    normed_low = low(normed)
    length = stream.shape[0]
    width = w_proj.shape[2]
    head_size = width // head_count
    triple = low(product("ld,xdc->xlc", normed_low, w_qkv))
    split_heads = triple.reshape(2, length, 3, head_count, head_size).transpose(2, 0, 3, 1, 4)
    scores = product("xhqe,xhke->xhqk", split_heads[0], split_heads[1]) * head_size ** (-0.5)
    log_total = jax.nn.logsumexp(scores, axis=-1, keepdims=True)
    attend_low = low(jnp.exp(scores - log_total))
    mixture = low(product("xhqk,xhke->xqhe", attend_low, split_heads[2]))
    mixture = mixture.reshape(2, length, width)
    partial = product("lc,dc->ld", mixture[0], w_proj[0]) + product("lc,dc->ld", mixture[1], w_proj[1])
    return (stream + join(partial), (normed_low, norm_kept, split_heads, mixture, log_total))


def attn_back(upstream, kept_state, w_qkv, w_proj, gain_row, head_count):
    normed_low, norm_kept, split_heads, mixture, log_total = kept_state
    _, length, width = mixture.shape
    head_size = width // head_count
    factor = head_size ** (-0.5)
    upstream_low = low(upstream)
    proj_grad = low(product("ld,xlc->xdc", upstream_low, mixture))
    mix_grad = low(product("ld,xdc->xlc", upstream_low, w_proj))
    mix_grad = mix_grad.reshape(2, length, head_count, head_size).transpose(0, 2, 1, 3)
    scores = product("xhqe,xhke->xhqk", split_heads[0], split_heads[1]) * factor
    attend_full = jnp.exp(scores - log_total)
    value_grad = low(product("xhqk,xhqe->xkhe", low(attend_full), mix_grad))
    attend_grad = product("xhqe,xhke->xhqk", mix_grad, split_heads[2])
    score_grad = attend_full * (attend_grad - jnp.sum(attend_full * attend_grad, -1, keepdims=True))
    score_grad = low(score_grad)
    query_grad = low(product("xhqk,xhke->xqhe", score_grad, split_heads[1]) * factor)
    key_grad = low(product("xhqk,xhqe->xkhe", score_grad, split_heads[0]) * factor)
    triple_grad = jnp.stack([query_grad, key_grad, value_grad], axis=2).reshape(2, length, 3 * width)
    qkv_grad = low(product("ld,xlc->xdc", normed_low, triple_grad))
    normed_grad = join_low(
        product("lc,dc->ld", triple_grad[0], w_qkv[0]) + product("lc,dc->ld", triple_grad[1], w_qkv[1])
    )
    input_grad, gain_grad, shift_grad = norm_back(normed_grad, norm_kept, gain_row)
    return (upstream + input_grad, qkv_grad, proj_grad, gain_grad, shift_grad)


def mlp_fwd(stream, w_up, w_down, gain_row, shift_row):
    normed, norm_kept = norm_fwd(stream, gain_row, shift_row)
    normed_low = low(normed)
    upward = product("ld,xdc->xlc", normed_low, w_up)
    hidden = low(exact_gelu(upward))
    partial = product("lc,dc->ld", hidden[0], w_down[0]) + product("lc,dc->ld", hidden[1], w_down[1])
    return (stream + join(partial), (normed_low, norm_kept, upward, hidden))


def mlp_back(upstream, kept_state, w_up, w_down, gain_row):
    normed_low, norm_kept, upward, hidden = kept_state
    upstream_low = low(upstream)
    down_grad = low(product("ld,xlc->xdc", upstream_low, hidden))
    hidden_grad = product("ld,xdc->xlc", upstream_low, w_down)
    upward_grad = low(jax.vjp(exact_gelu, upward)[1](hidden_grad)[0])
    up_grad = low(product("ld,xlc->xdc", normed_low, upward_grad))
    normed_grad = join_low(
        product("lc,dc->ld", upward_grad[0], w_up[0]) + product("lc,dc->ld", upward_grad[1], w_up[1])
    )
    input_grad, gain_grad, shift_grad = norm_back(normed_grad, norm_kept, gain_row)
    return (upstream + input_grad, up_grad, down_grad, gain_grad, shift_grad)


def adam_update(weight, moment, second, gradient, step_rate, decay_rate):
    moment = BETA_ONE * moment + (1.0 - BETA_ONE) * gradient
    second = BETA_TWO * second + (1.0 - BETA_TWO) * gradient * gradient
    fixed_one = moment / (1.0 - BETA_ONE**STEP)
    fixed_two = second / (1.0 - BETA_TWO**STEP)
    weight = weight - step_rate * (
        fixed_one / (jnp.sqrt(fixed_two) + ADAM_EPS) + decay_rate * weight
    )
    return [weight, moment, second]


def one_hot(visible_row, tokens):
    return visible_row[:, None] == jnp.arange(tokens)[None, :]


def pick(array, index, axis=0):
    return lax.dynamic_index_in_dim(array, index, axis, keepdims=False)


def columns_of(blob, widths):
    pieces, start = [], 0
    for width in widths:
        pieces.append(blob[..., start : start + width])
        start += width
    return pieces


def on_device(
    pixels,
    visible,
    valid,
    row_dest,
    encoder_in,
    encoder_in_moment,
    encoder_in_second,
    encoder_out,
    encoder_out_moment,
    encoder_out_second,
    decoder_in,
    decoder_in_moment,
    decoder_in_second,
    decoder_out,
    decoder_out_moment,
    decoder_out_second,
    patch_embed,
    patch_embed_moment,
    patch_embed_second,
    decoder_embed,
    decoder_embed_moment,
    decoder_embed_second,
    pixel_head,
    pixel_head_moment,
    pixel_head_second,
    norm_params,
    norm_params_moment,
    norm_params_second,
):
    masters = [
        encoder_in,
        encoder_out,
        decoder_in,
        decoder_out,
        patch_embed,
        decoder_embed,
        pixel_head,
        norm_params,
    ]
    moments = [
        encoder_in_moment,
        encoder_out_moment,
        decoder_in_moment,
        decoder_out_moment,
        patch_embed_moment,
        decoder_embed_moment,
        pixel_head_moment,
        norm_params_moment,
    ]
    seconds = [
        encoder_in_second,
        encoder_out_second,
        decoder_in_second,
        decoder_out_second,
        patch_embed_second,
        decoder_embed_second,
        pixel_head_second,
        norm_params_second,
    ]
    x, c = lax.axis_index("x"), lax.axis_index("c")
    data_size = lax.axis_size("z") * lax.axis_size("y")
    slot_total, tokens, pix_width = pixels.shape
    vis_count = visible.shape[1]
    patch_positions = valid.shape[2]
    rows_enc, _, part_enc = encoder_in.shape
    rows_dec, _, part_dec = decoder_in.shape
    width_enc, width_dec = patch_embed.shape[1], decoder_embed.shape[1]
    enc_heads = HEADS_ENC // 4
    dec_heads = HEADS_DEC // 4

    patch_rows = patch_embed.shape[0] // 2
    half_enc, quarter_dec = width_enc // 2, width_dec // 4
    patch_piece = lax.dynamic_slice(
        low(patch_embed), (c * patch_rows, x * half_enc), (patch_rows, half_enc)
    ).reshape(rows_enc, -1)
    embed_piece = lax.dynamic_slice(
        low(decoder_embed), (0, (2 * x + c) * quarter_dec), (rows_enc, quarter_dec)
    )
    norm_share, norm_room = norm_params.shape[0], rows_enc * LANES
    norm_piece = jnp.pad(low(norm_params), (0, norm_room - norm_share)).reshape(rows_enc, LANES)
    enc_in_low = low(encoder_in).reshape(rows_enc, -1)
    enc_out_low = low(encoder_out).transpose(2, 0, 1).reshape(rows_enc, -1)
    dec_in_low = low(decoder_in).reshape(rows_dec, -1)
    dec_out_low = low(decoder_out).transpose(2, 0, 1).reshape(rows_dec, -1)
    head_low = low(pixel_head)
    first_widths = (3 * part_enc, part_enc, patch_piece.shape[1], LANES)
    second_widths = (4 * part_enc, 4 * part_enc, quarter_dec)
    third_widths = (7 * part_dec, 5 * part_dec, head_low.shape[1])
    first_blob = jnp.concatenate(
        [enc_in_low[:, : 3 * part_enc], enc_out_low[:, :part_enc], patch_piece, norm_piece], 1
    )
    second_blob = jnp.concatenate(
        [enc_in_low[:, 3 * part_enc :], enc_out_low[:, part_enc:], embed_piece], 1
    )
    third_blob = jnp.concatenate([dec_in_low, dec_out_low, head_low], 1)
    first_all = spread(first_blob)
    second_all = spread(second_blob)
    third_all = spread(third_blob)

    def flat(array):
        return array.reshape(2, -1, array.shape[-1])

    enc_qkv, enc_proj, patch_all, norm_all = columns_of(flat(first_all), first_widths)
    enc_up, enc_down, embed_all = columns_of(flat(second_all), second_widths)
    dec_in_all, dec_out_all, head_all = columns_of(flat(third_all), third_widths)
    dec_qkv, dec_up = dec_in_all[..., : 3 * part_dec], dec_in_all[..., 3 * part_dec :]
    dec_proj, dec_down = dec_out_all[..., :part_dec], dec_out_all[..., part_dec:]
    patch_all = patch_all.reshape(2, -1, half_enc)
    embed_other = swap(embed_all)
    embed_even = jnp.where(c == 0, embed_all, embed_other)
    embed_odd = jnp.where(c == 0, embed_other, embed_all)
    full_embed = jnp.concatenate([embed_even[0], embed_odd[0], embed_even[1], embed_odd[1]], 1)
    norm_full = norm_all[0].reshape(data_size, norm_room)[:, :norm_share].reshape(-1)
    norm_full = norm_full.astype(FLOAT_TYPE)
    enc_gains = norm_full[: 6 * width_enc].reshape(6, width_enc)
    dec_gains = norm_full[6 * width_enc : 6 * width_enc + 6 * width_dec].reshape(6, width_dec)
    mask_token = norm_full[6 * width_enc + 6 * width_dec : 6 * width_enc + 7 * width_dec]

    buf_rows = data_size * -(-(slot_total * vis_count) // data_size)
    alive = row_dest[:, 0] < buf_rows
    use_own = pick(alive, x)
    half_step = lax.axis_size("z") // 2

    def shown_of(visible_row):
        return jnp.any(one_hot(visible_row, tokens), axis=0).astype(FLOAT_TYPE)

    shown_slots = jnp.stack([shown_of(visible[slot]) for slot in range(slot_total)])
    per_token = jnp.sum(valid, -1).astype(FLOAT_TYPE)
    valid_count = jnp.sum((1.0 - shown_slots) * alive.astype(FLOAT_TYPE)[:, None] * per_token)
    valid_count = total_over(valid_count * (pix_width // patch_positions), DATA)

    def seen_of(slot):
        chosen = low(one_hot(pick(visible, slot), tokens))
        rows = low(product("vt,tp->vp", chosen, pick(pixels, slot)))
        rows = rows.reshape(vis_count, data_size, 2, patch_rows)
        return pick(rows, c, 2).reshape(vis_count, data_size * patch_rows)

    def pixels_of(slot):
        rows = pick(pixels, slot).reshape(tokens, 2, 2, pix_width // 4)
        rows = pick(rows, c, 2).reshape(tokens, pix_width // 2)
        return jnp.concatenate([rows, low(pick(valid, slot))], 1)

    away = slot_total - 1 - x
    visible_row = jnp.where(use_own, pick(visible, x), shift(pick(visible, away), "z", half_step))
    seen_rows = jnp.where(use_own, seen_of(x), shift(seen_of(away), "z", half_step))
    chosen = low(one_hot(visible_row, tokens))
    hidden_row = 1.0 - shown_of(visible_row)

    stream = product("lp,xpd->xld", seen_rows, patch_all)
    stream = join(jnp.concatenate([stream[0], stream[1]], 1)) + angles_of(visible_row, width_enc)
    stream, enc_attn_kept = attn_fwd(
        stream, enc_qkv, enc_proj, enc_gains[0], enc_gains[1], enc_heads
    )
    stream, enc_mlp_kept = mlp_fwd(stream, enc_up, enc_down, enc_gains[2], enc_gains[3])
    normed, enc_norm_kept = norm_fwd(stream, enc_gains[4], enc_gains[5])
    enc_normed_low = low(normed)
    embedded = product("ld,dc->lc", enc_normed_low, full_embed)

    own_pixels = pixels_of(x)
    sent_pixels, embedded = lax.optimization_barrier((pixels_of(away), embedded))
    pixel_pack = jnp.where(use_own, own_pixels, shift(sent_pixels, "z", half_step))

    embedded_high = low(embedded)
    embedded_rest = low(embedded - embedded_high.astype(FLOAT_TYPE))
    placed = product("vt,vc->tc", chosen, jnp.concatenate([embedded_high, embedded_rest], 1))
    placed = placed[:, :width_dec] + placed[:, width_dec:]
    stream = placed + hidden_row[:, None] * mask_token + angles_of(jnp.arange(tokens), width_dec)
    stream, dec_attn_kept = attn_fwd(
        stream, dec_qkv, dec_proj, dec_gains[0], dec_gains[1], dec_heads
    )
    stream, dec_mlp_kept = mlp_fwd(stream, dec_up, dec_down, dec_gains[2], dec_gains[3])
    normed, dec_norm_kept = norm_fwd(stream, dec_gains[4], dec_gains[5])
    dec_normed_low = low(normed)
    predicted = product("ld,xdp->xlp", dec_normed_low, head_all)

    pixel_cols = pixel_pack[:, : pix_width // 2].astype(FLOAT_TYPE)
    valid_cols = pixel_pack[:, pix_width // 2 :].astype(FLOAT_TYPE)
    half_mean = jnp.mean(pixel_cols, -1, keepdims=True)
    half_square = jnp.sum((pixel_cols - half_mean) ** 2, -1, keepdims=True)
    half_both = jnp.concatenate([half_mean, half_square], 1)
    other_both = swap(half_both)
    mean = 0.5 * (half_both[:, :1] + other_both[:, :1])
    gap = half_both[:, :1] - other_both[:, :1]
    variance = (half_both[:, 1:] + other_both[:, 1:]) / pix_width + 0.25 * gap * gap
    target = (pixel_cols - mean) * lax.rsqrt(variance + EPS_PIX)
    half_positions = patch_positions // 2
    front = jnp.where(c == 0, valid_cols[:, :half_positions], valid_cols[:, half_positions:])
    back = jnp.where(c == 0, valid_cols[:, half_positions:], valid_cols[:, :half_positions])
    part_mask = jnp.concatenate([front, back, front], 1) * hidden_row[:, None]
    loss_weights = part_mask[None]
    goal = jnp.stack([target[:, : pix_width // 4], target[:, pix_width // 4 :]])
    errors = predicted - goal
    loss_part = jnp.sum(loss_weights * errors * errors)
    pred_grad = low(loss_weights * (2.0 * errors) * (1.0 / valid_count))
    head_grad = low(product("ld,xlp->xdp", dec_normed_low, pred_grad))
    normed_grad = join_low(
        product("lp,dp->ld", pred_grad[0], head_all[0]) + product("lp,dp->ld", pred_grad[1], head_all[1])
    )
    stream_grad, dec_gain_five, dec_shift_five = norm_back(
        normed_grad, dec_norm_kept, dec_gains[4]
    )
    stream_grad, dec_up_grad, dec_down_grad, dec_gain_three, dec_shift_three = mlp_back(
        stream_grad, dec_mlp_kept, dec_up, dec_down, dec_gains[2]
    )
    stream_grad, dec_qkv_grad, dec_proj_grad, dec_gain_one, dec_shift_one = attn_back(
        stream_grad, dec_attn_kept, dec_qkv, dec_proj, dec_gains[0], dec_heads
    )
    third_grads = jnp.concatenate(
        [dec_qkv_grad, dec_up_grad, dec_proj_grad, dec_down_grad, head_grad], 2
    )
    third_sum = collect(third_grads.reshape(third_all.shape))
    mask_grad = jnp.sum(hidden_row[:, None] * stream_grad, axis=0)
    embedded_grad = low(product("vt,tc->vc", chosen, low(stream_grad)))
    embed_mine = jnp.stack(
        [pick(embedded_grad.reshape(vis_count, 4, quarter_dec), 2 * part + c, 1) for part in (0, 1)]
    )
    embed_grad = low(product("ld,xlc->xdc", enc_normed_low, embed_mine))
    normed_grad = product("lc,dc->ld", embedded_grad, full_embed)
    stream_grad, enc_gain_five, enc_shift_five = norm_back(
        normed_grad, enc_norm_kept, enc_gains[4]
    )
    stream_grad, enc_up_grad, enc_down_grad, enc_gain_three, enc_shift_three = mlp_back(
        stream_grad, enc_mlp_kept, enc_up, enc_down, enc_gains[2]
    )
    second_grads = jnp.concatenate([enc_up_grad, enc_down_grad, embed_grad], 2)
    second_sum = collect(second_grads.reshape(second_all.shape))
    stream_grad, enc_qkv_grad, enc_proj_grad, enc_gain_one, enc_shift_one = attn_back(
        stream_grad, enc_attn_kept, enc_qkv, enc_proj, enc_gains[0], enc_heads
    )
    stream_low = low(stream_grad)
    patch_grad = low(
        product("lp,xld->xpd", seen_rows, jnp.stack([stream_low[:, :half_enc], stream_low[:, half_enc:]]))
    )
    norm_pieces = jnp.concatenate(
        [
            enc_gain_one,
            enc_shift_one,
            enc_gain_three,
            enc_shift_three,
            enc_gain_five,
            enc_shift_five,
            dec_gain_one,
            dec_shift_one,
            dec_gain_three,
            dec_shift_three,
            dec_gain_five,
            dec_shift_five,
            mask_grad,
        ]
    )
    norm_total = norm_params.shape[0] * data_size
    norm_grad = jnp.concatenate(
        [norm_pieces, jnp.zeros((norm_total - norm_pieces.shape[0],), FLOAT_TYPE)]
    )
    norm_half = norm_share // 2
    norm_grads = low(norm_grad).reshape(data_size, 2, norm_half).transpose(1, 0, 2)
    norm_grads = jnp.pad(norm_grads, ((0, 0), (0, 0), (0, norm_room - norm_half)))
    first_grads = jnp.concatenate(
        [
            enc_qkv_grad,
            enc_proj_grad,
            patch_grad.reshape(2, width_enc, -1),
            norm_grads.reshape(2, width_enc, LANES),
        ],
        2,
    )
    first_sum = collect(first_grads.reshape(first_all.shape))

    qkv_sum, proj_sum, patch_sum, norm_sum = columns_of(first_sum, first_widths)
    up_sum, down_sum, embed_sum = columns_of(second_sum, second_widths)
    dec_in_sum, dec_out_sum, head_sum = columns_of(third_sum, third_widths)
    norm_sum = low(norm_sum.reshape(-1)[:norm_half])
    patch_sum, embed_sum = low(patch_sum), low(embed_sum)
    shared_square = sum(
        jnp.sum(jnp.square(piece.astype(FLOAT_TYPE))) for piece in (patch_sum, embed_sum)
    ) + 0.5 * jnp.sum(jnp.square(norm_sum.astype(FLOAT_TYPE)))
    own_square = sum(
        jnp.sum(jnp.square(piece))
        for piece in (qkv_sum, proj_sum, up_sum, down_sum, third_sum)
    )
    totals = total_over(
        jnp.stack([loss_part, own_square + shared_square]), ("c", "x", "y", "z")
    )
    loss_sum, grad_norm = totals[0], jnp.sqrt(totals[1])

    def both(piece, axis, place, dimension):
        other = swap(piece, axis)
        return jnp.where(
            place == 0,
            jnp.concatenate([piece, other], dimension),
            jnp.concatenate([other, piece], dimension),
        )

    patch_sum = patch_sum.reshape(patch_rows, half_enc)
    patch_sum = both(both(patch_sum, "c", c, 0), "x", x, 1)
    embed_sum = both(both(embed_sum, "c", c, 1), "x", x, 1)
    norm_sum = both(norm_sum, "x", x, 0)
    reduced = (
        jnp.concatenate([qkv_sum, up_sum], 1).reshape(encoder_in.shape),
        jnp.concatenate([proj_sum, down_sum], 1).reshape(rows_enc, -1, part_enc).transpose(1, 2, 0),
        dec_in_sum.reshape(decoder_in.shape),
        dec_out_sum.reshape(rows_dec, -1, part_dec).transpose(1, 2, 0),
        patch_sum.astype(FLOAT_TYPE),
        embed_sum.astype(FLOAT_TYPE),
        head_sum,
        norm_sum.astype(FLOAT_TYPE),
    )
    clip_scale = CLIP / jnp.maximum(grad_norm, CLIP)
    updated = []
    for number in range(8):
        step_rate = LR_NORM if number == 7 else LR_MATRIX
        decay_rate = 0.0 if number == 7 else DECAY
        updated.extend(
            adam_update(
                masters[number],
                moments[number],
                seconds[number],
                reduced[number] * clip_scale,
                step_rate,
                decay_rate,
            )
        )
    return (loss_sum, valid_count, grad_norm, *updated)


def solution(mesh):
    data, model = mesh.shape["dp"], mesh.shape["mp"]
    inner = Mesh(mesh.devices.reshape(data // 2, 2, model // 2, 2), ("z", "y", "x", "c"))
    data_axes, model_axes = ("z", "y"), ("x", "c")
    rows = P(data_axes)
    into = P(data_axes, None, model_axes)
    out_of = P(None, model_axes, data_axes)
    head = P(data_axes, model_axes)
    weights = (into, out_of, into, out_of, rows, rows, head, rows)
    triples = tuple(spec for spec in weights for _ in range(3))
    return jax.shard_map(
        on_device,
        mesh=inner,
        in_specs=(rows, rows, rows, rows) + triples,
        out_specs=(P(), P(), P()) + triples,
        check_vma=False,
    )
```

time: 1820 us -> 643 us (0.35)
  waiting for transfers between devices: 875 us -> 218 us
  blocking collectives: 281 us -> 0 us
  local copies, waits for them, and re-layouts: 283 us -> 139 us
  matrix products: 175 us -> 91.9 us
  starting transfers between devices: 1.2 us -> 76.9 us
  other arithmetic: 167 us -> 94.6 us
    psum x9 -> x0, waiting for transfers between devices: 329 us -> none  [the longest x2 91.7 us: attn_fwd(): branch = lax.psum(partial_value, 'mp')]
    reduce_scatter x5 -> x0, waiting for transfers between devices: 267 us -> none  [the longest x1 93.3 us: on_device(): lax.psum_scatter(patch_grad, 'dp', scatter_dimension=0, tiled=True)]
    ppermute x0 -> x70, waiting for transfers between devices: none -> 218 us  [the longest x41 120 us: swap(): return lax.ppermute(values, axis, SWAP)]
    unnamed x21 -> x0, waiting for transfers between devices: 167 us -> none
    all_gather x5 -> x0, blocking collectives: 165 us -> none  [the longest x1 34.3 us: on_device(): lax.all_gather(decoder_embed.astype(NARROW_TYPE), 'dp', axis=0, tiled=True)]
    all_gather x3 -> x0, waiting for transfers between devices: 113 us -> none  [the longest x1 57.9 us: on_device(): lax.all_gather(encoder_in.astype(NARROW_TYPE), 'dp', axis=0, tiled=True)]
    scatter x2 -> x0, local copies, waits for them, and re-layouts: 102 us -> none  [the longest x1 72 us: on_device(): placed = jnp.zeros((slot_count, tokens, width_dec), FLOAT_TYPE).at[slot_r...]
    dot_general x44 -> x57, matrix products: 175 us -> 91.9 us  [product(): return jnp.einsum(spec, left, right, preferred_element_type=FLOAT_TYPE)]
  transfers between devices with their start and end apart: 19 -> 70, of which waited for: 16 -> 38; matrix products, arithmetic and copies ran while one was open for 12% -> 38% of each run, Pallas kernels for 0% -> 0%
where the time goes in v1:
time: 643 us; the launch traced here: 635 us
  waiting for transfers between devices  218 us (34%)
  local copies, waits for them, and re-layouts  139 us (22%)
  other arithmetic  94.6 us (15%)
  matrix products  91.9 us (14%)
  starting transfers between devices  76.9 us (12%)
  between operations  14.4 us (2%)
    ppermute x41, waiting for transfers between devices, swap(): return lax.ppermute(values, axis, SWAP)  120 us
    dot_general x57, matrix products, product(): return jnp.einsum(spec, left, right, preferred_element_type=FLOAT_TYPE)  91.9 us
    ppermute x21, waiting for transfers between devices, shift(): lax.ppermute(values, axis, [(i, (i + step) % size) for i in range(size)])  57.2 us
    ppermute x8, waiting for transfers between devices, total_over(): lax.ppermute(values, axis, [(i, i ^ step) for i in range(size)])  40.5 us
    ppermute x41, starting transfers between devices, swap(): return lax.ppermute(values, axis, SWAP)  39.6 us
    dynamic_slice x8, local copies, waits for them, and re-layouts, pick(): return lax.dynamic_index_in_dim(array, index, axis, keepdims=False)  34.5 us
    unnamed x291, local copies, waits for them, and re-layouts  27.8 us
    ppermute x8, starting transfers between devices, total_over(): lax.ppermute(values, axis, [(i, i ^ step) for i in range(size)])  19.1 us
  transfers between devices with their start and end apart: 70, of which 38 were waited for; matrix products, arithmetic and copies ran while one was open for 38% of the time, Pallas kernels for 0%

profile of v1, /device:TPU:0, one launch (start us, length us, event | category | flops | bytes accessed | tf_op | source)
XLA Modules:
  0.0 635.2 jit_solution(18304369862533010326)
XLA Ops:
  12.4 10.6 %constant_dynamic-slice_fusion.7 = (bf16[1,588,1536]{2,0,1:T(2,128)(2,1)}, bf16[1,588,1536]{2,0,1:T(2,128)(2,1)S(1)}) fusion(bf16[4,588,1536]{2,0,1:T(4,128)(2,1)} %param.28, s32[]{:T(128)S(6)} %select_n.311, s32[]{:T(128)S(6)} %select_n.314), kind=kLoop, calls=%fused_computation.549 | loop fusion | bytes 7225352 | tf_op jit(solution)/shard_map/jit(dynamic_index_in_dim)/dynamic_slice | solution.py:241
  40.2 10.7 %reduce_sum.503 = s32[4,588]{0,1:T(8,128)} reduce(s32[4,588,256]{2,0,1:T(4,128)S(1)} %copy-done.28, s32[]{:T(128)} %constant.424.clone.1), dimensions={2}, to_apply=%region_24.25 | reduce | flops 599760 | bytes 2417860 | tf_op jit(solution)/shard_map/reduce_sum | solution.py:380
  65.4 6.3 dynamic-slice_reduce_fusion
  99.6 5.1 collective-permute-done.22
  105.6 6.0 collective-permute-done.12
  129.6 12.9 %collective-permute-done.3 = bf16[4,96,1280]{2,1,0:T(8,128)(2,1)S(1)} collective-permute-done((bf16[4,96,1280]{2,1,0:T(8,128)(2,1)}, bf16[4,96,1280]{2,1,0:T(8,128)(2,1)S(1)}, u32[]{:S(2)}, u32[]{:S(2)}) %collective-permute-start.3) | collective-permute-done | bytes 983072 | tf_op jit(solution)/shard_map/ppermute | solution.py:39
  148.4 15.1 %collective-permute-done.24 = bf16[4,64,1920]{2,1,0:T(8,128)(2,1)S(1)} collective-permute-done((bf16[4,64,1920]{2,1,0:T(8,128)(2,1)S(1)}, bf16[4,64,1920]{2,1,0:T(8,128)(2,1)S(1)}, u32[]{:S(2)}, u32[]{:S(2)}) %collective-permute-start.24) | collective-permute-done | bytes 983072 | tf_op jit(solution)/shard_map/ppermute | solution.py:39
  170.6 6.9 %collective-permute-done.5 = bf16[2,96,1280]{2,1,0:T(8,128)(2,1)S(1)} collective-permute-done((bf16[2,96,1280]{2,1,0:T(8,128)(2,1)S(1)}, bf16[2,96,1280]{2,1,0:T(8,128)(2,1)S(1)}, u32[]{:S(2)}, u32[]{:S(2)}) %collective-permute-start.5) | collective-permute-done | bytes 491552 | tf_op jit(solution)/shard_map/ppermute | solution.py:39
  179.2 16.0 %collective-permute-done.6 = bf16[2,96,1280]{2,1,0:T(8,128)(2,1)S(1)} collective-permute-done((bf16[2,96,1280]{2,1,0:T(8,128)(2,1)S(1)}, bf16[2,96,1280]{2,1,0:T(8,128)(2,1)S(1)}, u32[]{:S(2)}, u32[]{:S(2)}) %collective-permute-start.6) | collective-permute-done | bytes 491552 | tf_op jit(solution)/shard_map/ppermute | solution.py:39
  203.7 6.3 collective-permute-done.26
  258.8 6.5 %dynamic-slice_reduce_fusion.1 = bf16[588,2,384]{2,1,0:T(2,128)(2,1)S(1)} fusion(bf16[588,2,2,384]{3,2,1,0:T(2,128)(2,1)S(1)} %copy-done.26, s32[]{:T(128)S(6)} %select_n.313), kind=kLoop, calls=%fused_computation.70 | loop fusion | bytes 1806340 | tf_op jit(solution)/shard_map/jit(dynamic_index_in_dim)/dynamic_slice | solution.py:241
  267.6 11.1 %collective-permute-start.32 = (f32[]{:T(128)}, f32[]{:T(128)}, u32[]{:S(2)}, u32[]{:S(2)}) collective-permute-start(f32[]{:T(128)} %add.705), channel_id=1, source_target_pairs={{0,16},{8,24},{16,0},{24,8},{1,17},{9,25},{17,1},{25,9},{2,18},{10... | collective-permute-start | bytes 20 | tf_op jit(solution)/shard_map/ppermute | solution.py:65
  278.7 27.6 %collective-permute-done.32 = f32[]{:T(128)} collective-permute-done((f32[]{:T(128)}, f32[]{:T(128)}, u32[]{:S(2)}, u32[]{:S(2)}) %collective-permute-start.32) | collective-permute-done | bytes 36 | tf_op jit(solution)/shard_map/ppermute | solution.py:65
  316.8 7.0 %fusion.12 = (bf16[2,588,512]{2,1,0:T(8,128)(2,1)S(1)}, f32[2,588,512]{2,1,0:T(8,128)S(1)}, f32[2,512,588]{1,2,0:T(8,128)S(1)}) fusion(f32[588,512]{1,0:T(8,128)S(1)} %get-tuple-element.287, f32[512]{0:T(512)S(1)} %get-tuple-element.357, f32[512]{0:T(512)S(1)} %get-tuple-element.358, f32[588]{0:T(1024)S(1)} %add_rsqrt_fusion.1, ...), kind=kOutput, calls=%fused_computation.33 | convolution fusion | flops 657205248 | bytes 8282720 | tf_op jit(solution)/shard_map/ld,xdc->xlc/dot_general | solution.py:31
  354.7 7.7 %multiply_reduce_fusion = (f32[2,4,588]{2,1,0:T(4,128)S(1)}, f32[2,4,588,588]{2,3,1,0:T(8,128)S(1)}) fusion(f32[2,4,588,588]{2,3,1,0:T(8,128)} %copy-done, f32[2,4,588]{2,1,0:T(4,128)S(1)} %log_add_fusion, bf16[2,4,588,32]{2,3,1,0:T(8,128)(2,1)S(1)} %bitcast.826, bf16[3,2,4,588,32]{3,4,2,1,0:T(8,128)(2,1)S(1)} %bitcast.808), kind=kOutput, calls=%fused_computation.1 | convolution fusion | flops 188080032 | bytes 22822272 | tf_op jit(solution)/shard_map/xhqe,xhke->xhqk/dot_general | solution.py:31
  382.9 6.7 %copy.675 = bf16[2,512,1920]{2,1,0:T(8,128)(2,1)} copy(bf16[2,512,1920]{1,2,0:T(8,128)(2,1)} %fusion.56) | data formatting | bytes 7864320 | tf_op jit(solution)/shard_map/concatenate | solution.py:460
  395.7 8.9 %collective-permute-done.53 = bf16[2,64,1920]{2,1,0:T(8,128)(2,1)S(1)} collective-permute-done((bf16[2,64,1920]{2,1,0:T(8,128)(2,1)S(1)}, bf16[2,64,1920]{2,1,0:T(8,128)(2,1)S(1)}, u32[]{:S(2)}, u32[]{:S(2)}) %collective-permute-start.53) | collective-permute-done | bytes 491552 | tf_op jit(solution)/shard_map/ppermute | solution.py:39
  421.7 7.8 %copy.667 = bf16[2,768,1664]{2,1,0:T(8,128)(2,1)} copy(bf16[2,768,1664]{1,2,0:T(8,128)(2,1)} %pad_maximum_fusion) | data formatting | bytes 10223616 | tf_op jit(solution)/shard_map/concatenate | solution.py:477
  469.0 6.4 %concatenate.145 = bf16[2,4,2,96,1280]{4,3,2,1,0:T(8,128)(2,1)} concatenate(bf16[2,4,2,96,576]{4,3,2,1,0:T(8,128)(2,1)S(1)} %bitcast.811, bf16[2,4,2,96,192]{4,3,2,1,0:T(8,128)(2,1)S(1)} %bitcast.823, bf16[2,4,2,96,384]{4,3,2,1,0:T(8,128)(2,1)} %bitcast.817, bf16[2,4,2,96,128]{4,3,2,1,0:T(8,128)(2,1)S(1)} %copy-done.55), dimensions={4} | concatenate | bytes 7864320 | tf_op jit(solution)/shard_map/concatenate | solution.py:510
  499.3 5.2 collective-permute-done.58
  513.3 27.3 %collective-permute-done.40 = bf16[4,96,1280]{2,1,0:T(8,128)(2,1)} collective-permute-done((bf16[4,96,1280]{2,1,0:T(8,128)(2,1)}, bf16[4,96,1280]{2,1,0:T(8,128)(2,1)}, u32[]{:S(2)}, u32[]{:S(2)}) %collective-permute-start.40) | collective-permute-done | bytes 983072 | tf_op jit(solution)/shard_map/ppermute | solution.py:39
  554.1 7.9 %collective-permute-done.50 = bf16[96,1664]{1,0:T(8,128)(2,1)S(1)} collective-permute-done((bf16[96,1664]{1,0:T(8,128)(2,1)S(1)}, bf16[96,1664]{1,0:T(8,128)(2,1)S(1)}, u32[]{:S(2)}, u32[]{:S(2)}) %collective-permute-start.50) | collective-permute-done | bytes 319520 | tf_op jit(solution)/shard_map/ppermute | solution.py:54
  562.1 5.1 collective-permute-done.44
  567.4 6.4 %collective-permute-done.51 = bf16[96,1664]{1,0:T(8,128)(2,1)S(1)} collective-permute-done((bf16[96,1664]{1,0:T(8,128)(2,1)S(1)}, bf16[96,1664]{1,0:T(8,128)(2,1)S(1)}, u32[]{:S(2)}, u32[]{:S(2)}) %collective-permute-start.51) | collective-permute-done | bytes 319520 | tf_op jit(solution)/shard_map/ppermute | solution.py:54
  (728 shorter events, 383.3 us)
Async XLA Ops:
  4.3 90.8 %collective-permute-start.11 = (bf16[96,1664]{1,0:T(8,128)(2,1)}, bf16[96,1664]{1,0:T(8,128)(2,1)}, u32[]{:S(2)}, u32[]{:S(2)}) collective-permute-start(bf16[96,1664]{1,0:T(8,128)(2,1)} %pad_maximum_fusion.12), channel_id=1, source_target_pairs={{0,8},{8,16},{16,24},{24,0},{1,9},{9,17},{17,25},{25,1},{2,10},{10... | collective-permute-start | bytes 958472 | tf_op jit(solution)/shard_map/ppermute | solution.py:54
  9.2 79.3 %collective-permute-start = (bf16[96,1280]{1,0:T(8,128)(2,1)}, bf16[96,1280]{1,0:T(8,128)(2,1)}, u32[]{:S(2)}, u32[]{:S(2)}) collective-permute-start(bf16[96,1280]{1,0:T(8,128)(2,1)} %concatenate.127), channel_id=1, source_target_pairs={{0,8},{8,16},{16,24},{24,0},{1,9},{9,17},{17,25},{25,1},{2,10},{10... | collective-permute-start | bytes 737288 | tf_op jit(solution)/shard_map/ppermute | solution.py:54
  11.4 73.3 %collective-permute-start.9 = (s32[147]{0:T(256)S(1)}, s32[147]{0:T(256)}, u32[]{:S(2)}, u32[]{:S(2)}) collective-permute-start(s32[147]{0:T(256)S(1)} %bitcast.853), channel_id=1, source_target_pairs={{0,16},{8,24},{16,0},{24,8},{1,17},{9,25},{17,1},{25,9},{2,18},{10... | collective-permute-start | bytes 1772 | tf_op jit(solution)/shard_map/ppermute | solution.py:54
  27.4 171.9 %collective-permute-start.7 = (bf16[147,768]{1,0:T(8,128)(2,1)}, bf16[147,768]{1,0:T(8,128)(2,1)}, u32[]{:S(2)}, u32[]{:S(2)}) collective-permute-start(bf16[147,768]{1,0:T(8,128)(2,1)} %reshape.561), channel_id=1, source_target_pairs={{0,16},{8,24},{16,0},{24,8},{1,17},{9,25},{17,1},{25,9},{2,18},{10... | collective-permute-start | bytes 677384 | tf_op jit(solution)/shard_map/ppermute | solution.py:54
  31.1 59.3 %collective-permute-start.21 = (bf16[64,1920]{1,0:T(8,128)(2,1)}, bf16[64,1920]{1,0:T(8,128)(2,1)}, u32[]{:S(2)}, u32[]{:S(2)}) collective-permute-start(bf16[64,1920]{1,0:T(8,128)(2,1)} %pad_maximum_fusion.13), channel_id=1, source_target_pairs={{0,8},{8,16},{16,24},{24,0},{1,9},{9,17},{17,25},{25,1},{2,10},{10... | collective-permute-start | bytes 737288 | tf_op jit(solution)/shard_map/ppermute | solution.py:54
  84.7 182.4 %collective-permute-start.31 = (f32[]{:T(128)}, f32[]{:T(128)}, u32[]{:S(2)}, u32[]{:S(2)}) collective-permute-start(f32[]{:T(128)} %mul.954), channel_id=1, source_target_pairs={{0,8},{8,0},{16,24},{24,16},{1,9},{9,1},{17,25},{25,17},{2,10},{10... | collective-permute-start | bytes 20 | tf_op jit(solution)/shard_map/ppermute | solution.py:65
  127.2 36.2 %collective-permute-start.24 = (bf16[4,64,1920]{2,1,0:T(8,128)(2,1)S(1)}, bf16[4,64,1920]{2,1,0:T(8,128)(2,1)S(1)}, u32[]{:S(2)}, u32[]{:S(2)}) collective-permute-start(bf16[4,64,1920]{2,1,0:T(8,128)(2,1)S(1)} %bitcast_dynamic-update-slice_fusion.13), channel_id=1, source_target_pairs={{0,2},{2,0},{1,3},{3,1},{4,6},{6,4},{5,7},{7,5},{8,10},{10,8},{9,1... | collective-permute-start | bytes 2949128 | tf_op jit(solution)/shard_map/ppermute | solution.py:39
  146.8 65.3 %collective-permute-start.14 = (bf16[4,96,1664]{2,1,0:T(8,128)(2,1)S(1)}, bf16[4,96,1664]{2,1,0:T(8,128)(2,1)}, u32[]{:S(2)}, u32[]{:S(2)}) collective-permute-start(bf16[4,96,1664]{2,1,0:T(8,128)(2,1)S(1)} %bitcast_dynamic-update-slice_fusion.9), channel_id=1, source_target_pairs={{0,2},{2,0},{1,3},{3,1},{4,6},{6,4},{5,7},{7,5},{8,10},{10,8},{9,1... | collective-permute-start | bytes 3833864 | tf_op jit(solution)/shard_map/ppermute | solution.py:39
  167.1 28.1 %collective-permute-start.6 = (bf16[2,96,1280]{2,1,0:T(8,128)(2,1)S(1)}, bf16[2,96,1280]{2,1,0:T(8,128)(2,1)S(1)}, u32[]{:S(2)}, u32[]{:S(2)}) collective-permute-start(bf16[2,96,1280]{2,1,0:T(8,128)(2,1)S(1)} %slice.665), channel_id=1, source_target_pairs={{0,2},{2,0},{1,3},{3,1},{4,6},{6,4},{5,7},{7,5},{8,10},{10,8},{9,1... | collective-permute-start | bytes 1474568 | tf_op jit(solution)/shard_map/ppermute | solution.py:39
  177.5 37.6 %collective-permute-start.15 = (bf16[4,96,1664]{2,1,0:T(8,128)(2,1)S(1)}, bf16[4,96,1664]{2,1,0:T(8,128)(2,1)S(1)}, u32[]{:S(2)}, u32[]{:S(2)}) collective-permute-start(bf16[4,96,1664]{2,1,0:T(8,128)(2,1)S(1)} %bitcast_dynamic-update-slice_fusion.9), channel_id=1, source_target_pairs={{0,4},{4,0},{1,5},{5,1},{2,6},{6,2},{3,7},{7,3},{8,12},{12,8},{9,1... | collective-permute-start | bytes 3833864 | tf_op jit(solution)/shard_map/ppermute | solution.py:39
  251.3 60.0 %collective-permute-start.20 = (bf16[588,1024]{1,0:T(8,128)(2,1)}, bf16[588,1024]{1,0:T(8,128)(2,1)}, u32[]{:S(2)}, u32[]{:S(2)}) collective-permute-start(bf16[588,1024]{1,0:T(8,128)(2,1)} %pad_maximum_fusion.3), channel_id=1, source_target_pairs={{0,16},{8,24},{16,0},{24,8},{1,17},{9,25},{17,1},{25,9},{2,18},{10... | collective-permute-start | bytes 3612680 | tf_op jit(solution)/shard_map/ppermute | solution.py:54
  258.3 56.0 %collective-permute-start.28 = (f32[588,512]{1,0:T(8,128)S(1)}, f32[588,512]{1,0:T(8,128)}, u32[]{:S(2)}, u32[]{:S(2)}) collective-permute-start(f32[588,512]{1,0:T(8,128)S(1)} %convolution_add_fusion.2), channel_id=1, source_target_pairs={{0,1},{1,0},{2,3},{3,2},{4,5},{5,4},{6,7},{7,6},{8,9},{9,8},{10,11... | collective-permute-start | bytes 3612680 | tf_op jit(solution)/shard_map/ppermute | solution.py:39
  267.6 38.7 %collective-permute-start.32 = (f32[]{:T(128)}, f32[]{:T(128)}, u32[]{:S(2)}, u32[]{:S(2)}) collective-permute-start(f32[]{:T(128)} %add.705), channel_id=1, source_target_pairs={{0,16},{8,24},{16,0},{24,8},{1,17},{9,25},{17,1},{25,9},{2,18},{10... | collective-permute-start | bytes 20 | tf_op jit(solution)/shard_map/ppermute | solution.py:65
  407.1 76.9 %collective-permute-start.54 = (bf16[4,64,1920]{2,1,0:T(8,128)(2,1)}, bf16[4,64,1920]{2,1,0:T(8,128)(2,1)}, u32[]{:S(2)}, u32[]{:S(2)}) collective-permute-start(bf16[4,64,1920]{2,1,0:T(8,128)(2,1)} %pad_maximum_fusion.7), channel_id=1, source_target_pairs={{0,4},{4,0},{1,5},{5,1},{2,6},{6,2},{3,7},{7,3},{8,12},{12,8},{9,1... | collective-permute-start | bytes 2949128 | tf_op jit(solution)/shard_map/ppermute | solution.py:39
  409.4 74.6 %collective-permute-start.56 = (bf16[4,64,1920]{2,1,0:T(8,128)(2,1)}, bf16[4,64,1920]{2,1,0:T(8,128)(2,1)}, u32[]{:S(2)}, u32[]{:S(2)}) collective-permute-start(bf16[4,64,1920]{2,1,0:T(8,128)(2,1)} %pad_maximum_fusion.8), channel_id=1, source_target_pairs={{0,2},{2,0},{1,3},{3,1},{4,6},{6,4},{5,7},{7,5},{8,10},{10,8},{9,1... | collective-permute-start | bytes 2949128 | tf_op jit(solution)/shard_map/ppermute | solution.py:39
  435.5 43.2 %collective-permute-start.46 = (bf16[2,96,1664]{2,1,0:T(8,128)(2,1)}, bf16[2,96,1664]{2,1,0:T(8,128)(2,1)}, u32[]{:S(2)}, u32[]{:S(2)}) collective-permute-start(bf16[2,96,1664]{2,1,0:T(8,128)(2,1)} %get-tuple-element.308), channel_id=1, source_target_pairs={{0,2},{2,0},{1,3},{3,1},{4,6},{6,4},{5,7},{7,5},{8,10},{10,8},{9,1... | collective-permute-start | bytes 1916936 | tf_op jit(solution)/shard_map/ppermute | solution.py:39
  437.3 42.5 %collective-permute-start.48 = (bf16[2,96,1664]{2,1,0:T(8,128)(2,1)}, bf16[2,96,1664]{2,1,0:T(8,128)(2,1)}, u32[]{:S(2)}, u32[]{:S(2)}) collective-permute-start(bf16[2,96,1664]{2,1,0:T(8,128)(2,1)} %get-tuple-element.310), channel_id=1, source_target_pairs={{0,4},{4,0},{1,5},{5,1},{2,6},{6,2},{3,7},{7,3},{8,12},{12,8},{9,1... | collective-permute-start | bytes 1916936 | tf_op jit(solution)/shard_map/ppermute | solution.py:39
  483.0 60.1 %collective-permute-start.47 = (bf16[4,96,1664]{2,1,0:T(8,128)(2,1)}, bf16[4,96,1664]{2,1,0:T(8,128)(2,1)S(1)}, u32[]{:S(2)}, u32[]{:S(2)}) collective-permute-start(bf16[4,96,1664]{2,1,0:T(8,128)(2,1)} %pad_maximum_fusion.1), channel_id=1, source_target_pairs={{0,4},{4,0},{1,5},{5,1},{2,6},{6,2},{3,7},{7,3},{8,12},{12,8},{9,1... | collective-permute-start | bytes 3833864 | tf_op jit(solution)/shard_map/ppermute | solution.py:39
  495.4 45.2 %collective-permute-start.40 = (bf16[4,96,1280]{2,1,0:T(8,128)(2,1)}, bf16[4,96,1280]{2,1,0:T(8,128)(2,1)}, u32[]{:S(2)}, u32[]{:S(2)}) collective-permute-start(bf16[4,96,1280]{2,1,0:T(8,128)(2,1)} %pad_maximum_fusion.5), channel_id=1, source_target_pairs={{0,4},{4,0},{1,5},{5,1},{2,6},{6,2},{3,7},{7,3},{8,12},{12,8},{9,1... | collective-permute-start | bytes 2949128 | tf_op jit(solution)/shard_map/ppermute | solution.py:39
  497.6 43.0 %collective-permute-start.42 = (bf16[4,96,1280]{2,1,0:T(8,128)(2,1)}, bf16[4,96,1280]{2,1,0:T(8,128)(2,1)}, u32[]{:S(2)}, u32[]{:S(2)}) collective-permute-start(bf16[4,96,1280]{2,1,0:T(8,128)(2,1)} %pad_maximum_fusion.6), channel_id=1, source_target_pairs={{0,2},{2,0},{1,3},{3,1},{4,6},{6,4},{5,7},{7,5},{8,10},{10,8},{9,1... | collective-permute-start | bytes 2949128 | tf_op jit(solution)/shard_map/ppermute | solution.py:39
  505.8 41.3 %collective-permute-start.49 = (bf16[4,96,1664]{2,1,0:T(8,128)(2,1)}, bf16[4,96,1664]{2,1,0:T(8,128)(2,1)}, u32[]{:S(2)}, u32[]{:S(2)}) collective-permute-start(bf16[4,96,1664]{2,1,0:T(8,128)(2,1)} %pad_maximum_fusion.2), channel_id=1, source_target_pairs={{0,2},{2,0},{1,3},{3,1},{4,6},{6,4},{5,7},{7,5},{8,10},{10,8},{9,1... | collective-permute-start | bytes 3833864 | tf_op jit(solution)/shard_map/ppermute | solution.py:39
  581.1 39.4 %collective-permute-start.69 = (bf16[512]{0:T(512)(128)(2,1)S(1)}, bf16[512]{0:T(512)(128)(2,1)S(1)}, u32[]{:S(2)}, u32[]{:S(2)}) collective-permute-start(bf16[512]{0:T(512)(128)(2,1)S(1)} %fusion.228), channel_id=1, source_target_pairs={{0,2},{2,0},{1,3},{3,1},{4,6},{6,4},{5,7},{7,5},{8,10},{10,8},{9,1... | collective-permute-start | bytes 3080 | tf_op jit(solution)/shard_map/ppermute | solution.py:39
  586.0 43.1 %collective-permute-start.66 = (bf16[192,384]{1,0:T(8,128)(2,1)}, bf16[192,384]{1,0:T(8,128)(2,1)}, u32[]{:S(2)}, u32[]{:S(2)}) collective-permute-start(bf16[192,384]{1,0:T(8,128)(2,1)} %maximum_select_fusion.2), channel_id=1, source_target_pairs={{0,2},{2,0},{1,3},{3,1},{4,6},{6,4},{5,7},{7,5},{8,10},{10,8},{9,1... | collective-permute-start | bytes 442376 | tf_op jit(solution)/shard_map/ppermute | solution.py:39
  592.6 33.9 %collective-permute-start.67 = (bf16[96,128]{1,0:T(8,128)(2,1)}, bf16[96,128]{1,0:T(8,128)(2,1)}, u32[]{:S(2)}, u32[]{:S(2)}) collective-permute-start(bf16[96,128]{1,0:T(8,128)(2,1)} %get-tuple-element.273), channel_id=1, source_target_pairs={{0,1},{1,0},{2,3},{3,2},{4,5},{5,4},{6,7},{7,6},{8,9},{9,8},{10,11... | collective-permute-start | bytes 73736 | tf_op jit(solution)/shard_map/ppermute | solution.py:39
  (177 other events, 1450.5 us)

commit v2 on v1

--- a/solution.py
+++ b/solution.py
@@ -1,8 +1,10 @@
-import math
+import numpy as np
 
 import jax
 import jax.numpy as jnp
 from jax import lax
+from jax.experimental import pallas as pl
+from jax.experimental.pallas import tpu as pltpu
 from jax.sharding import Mesh
 from jax.sharding import PartitionSpec as P
 
@@ -67,29 +69,60 @@
     return values
 
 
-def spread(blob):
+def after(value, *others):
+    return lax.optimization_barrier((value,) + others)[0]
+
+
+def assemble(parts, places, shape):
+    dims = len(places[0])
+    spots = jnp.stack([jnp.asarray(at, jnp.int32) for place in places for at in place])
+
+    def kernel(spots_ref, *refs):
+        whole = refs[len(parts)]
+        for number, part in enumerate(parts):
+            window = tuple(
+                pl.ds(spots_ref[number * dims + dim], part.shape[dim]) for dim in range(dims)
+            )
+            whole[window] = refs[number][...]
+
+    size = int(np.prod(shape)) * parts[0].dtype.itemsize
+    return pl.pallas_call(
+        kernel,
+        out_shape=jax.ShapeDtypeStruct(shape, parts[0].dtype),
+        in_specs=[pl.BlockSpec(memory_space=pltpu.SMEM)]
+        + [pl.BlockSpec(memory_space=pltpu.VMEM)] * len(parts),
+        out_specs=pl.BlockSpec(memory_space=pltpu.VMEM),
+        compiler_params=pltpu.CompilerParams(vmem_limit_bytes=32 * 2**20),
+        cost_estimate=pl.CostEstimate(flops=0, bytes_accessed=2 * size, transcendentals=0),
+    )(spots, *parts)
+
+
+def spread(blob, earlier_z=(), earlier=()):
     sizes = tuple(lax.axis_size(axis) for axis in ("x", "z", "y"))
     if sizes != (2, 4, 2):
-        return lax.all_gather(blob, ("x", "z", "y")).reshape(sizes + blob.shape)
-    x, z, y = (lax.axis_index(axis) for axis in ("x", "z", "y"))
-    column = jnp.zeros((4,) + blob.shape, blob.dtype)
-    moving = blob
-    for step in range(4):
-        column = lax.dynamic_update_index_in_dim(column, moving, (z - step) % 4, 0)
-        if step < 3:
-            moving = shift(moving, "z", 1)
-    from_x = swap(column, "x")
-    from_y = swap(column, "y")
-    corner = jnp.concatenate([swap(from_x[:2], "y"), swap(from_y[2:], "x")])
-    whole = jnp.zeros((2, 4, 2) + blob.shape, blob.dtype)
-    for part, at_x, at_y in (
-        (column, x, y),
-        (from_x, 1 - x, y),
-        (from_y, x, 1 - y),
-        (corner, 1 - x, 1 - y),
-    ):
-        whole = lax.dynamic_update_slice(whole, part[None, :, None], (at_x, 0, at_y, 0, 0))
-    return whole
+        return lax.all_gather(blob, ("x", "z", "y")).reshape(sizes + blob.shape), ((), (), (), ())
+    x, y, z = (lax.axis_index(axis) for axis in ("x", "y", "z"))
+    half = 2
+    blob = after(blob, *earlier_z)
+    moved = [blob] + [shift(blob, "z", step) for step in (1, 2, 3)]
+    column = assemble(
+        [part[None] for part in moved], [((z - step) % 4,) for step in range(4)], (4,) + blob.shape
+    )
+    column = after(column, *earlier)
+    from_x, from_y = swap(column, "x"), swap(column, "y")
+    corner = (swap(from_x[:half], "y"), swap(from_y[half:], "x"))
+    whole = assemble(
+        [part[None, :, None] for part in (column, from_x, from_y, *corner)],
+        [
+            (x, 0, y),
+            (1 - x, 0, y),
+            (x, 0, 1 - y),
+            (1 - x, 0, 1 - y),
+            (1 - x, half, 1 - y),
+        ],
+        (2, 4, 2) + blob.shape,
+    )
+    return whole, (moved[1:], (column,), (from_x, from_y), corner)
 
 
 def collect(grads):
@@ -98,37 +131,46 @@
     if sizes != (2, 4, 2):
         flat = grads.reshape((-1,) + shape)
         return lax.psum_scatter(flat, ("x", "z", "y"), scatter_dimension=0).astype(FLOAT_TYPE)
-    x, z, y = (lax.axis_index(axis) for axis in ("x", "z", "y"))
+    x, y, z = (lax.axis_index(axis) for axis in ("x", "y", "z"))
+    half = 2
 
     def part(at_x, at_y):
-        cut = lax.dynamic_slice(grads, (at_x, 0, at_y, 0, 0), (1, 4, 1) + shape)
-        return cut.reshape((4,) + shape)
+        cut = lax.dynamic_slice(grads, (at_x, 0, at_y, 0, 0), (1, sizes[1], 1) + shape)
+        return cut.reshape((sizes[1],) + shape)
 
     def add(*terms):
         return sum(term.astype(FLOAT_TYPE) for term in terms)
 
     corner = part(1 - x, 1 - y)
-    by_x = swap(corner[:2], "x")
-    by_y = swap(corner[2:], "y")
+    by_x = swap(corner[:half], "x")
+    by_y = swap(corner[half:], "y")
     to_y = part(x, 1 - y)
     to_x = part(1 - x, y)
-    to_y = jnp.concatenate([low(add(to_y[:2], by_x)), to_y[2:]])
-    to_x = jnp.concatenate([to_x[:2], low(add(to_x[2:], by_y))])
+    to_y = jnp.concatenate([low(add(to_y[:half], by_x)), to_y[half:]])
+    to_x = jnp.concatenate([to_x[:half], low(add(to_x[half:], by_y))])
     column = low(add(part(x, y), swap(to_y, "y"), swap(to_x, "x")))
 
     def at(index):
         return lax.dynamic_index_in_dim(column, index % 4, 0, keepdims=False)
 
-    moving = at(z - 1)
-    for step in range(1, 4):
-        moving = add(shift(moving, "z", 1), at(z - 1 - step))
-        if step < 3:
-            moving = low(moving)
-    return moving
+    return add(at(z), *(shift(at(z + step), "z", step) for step in (1, 2, 3)))
+
+
+def collect_pieces(pieces, data_size):
+    grads = jnp.concatenate(pieces, 2)
+    z_size = lax.axis_size("z")
+    return collect(grads.reshape(2, z_size, data_size // z_size, -1, grads.shape[2]))
 
 
 def exact_gelu(values):
     return jax.nn.gelu(values, approximate=False)
+
+
+def places_of(count, features):
+    half_width = features // 2
+    freqs = np.exp(-np.log(np.float32(10000.0)) * np.arange(half_width, dtype=np.float32) / np.float32(half_width))
+    angles = np.arange(count, dtype=np.float32)[:, None] * freqs[None, :]
+    return jnp.asarray(np.concatenate([np.sin(angles), np.cos(angles)], axis=1))
 
 
 def angles_of(places, features):
@@ -231,6 +273,20 @@
         fixed_one / (jnp.sqrt(fixed_two) + ADAM_EPS) + decay_rate * weight
     )
     return [weight, moment, second]
+
+
+def both(piece, axis, place, dimension):
+    other = swap(piece, axis)
+    return jnp.where(
+        place == 0,
+        jnp.concatenate([piece, other], dimension),
+        jnp.concatenate([other, piece], dimension),
+    )
+
+
+def halves_of(array, place):
+    half = array.shape[1] // 2
+    return jnp.where(place == 0, array[:, :half], array[:, half:])
 
 
 def one_hot(visible_row, tokens):
@@ -323,8 +379,8 @@
     patch_rows = patch_embed.shape[0] // 2
     half_enc, quarter_dec = width_enc // 2, width_dec // 4
     patch_piece = lax.dynamic_slice(
-        low(patch_embed), (c * patch_rows, x * half_enc), (patch_rows, half_enc)
-    ).reshape(rows_enc, -1)
+        low(patch_embed), (x * patch_rows, c * half_enc), (patch_rows, half_enc)
+    )
     embed_piece = lax.dynamic_slice(
         low(decoder_embed), (0, (2 * x + c) * quarter_dec), (rows_enc, quarter_dec)
     )
@@ -345,9 +401,9 @@
         [enc_in_low[:, 3 * part_enc :], enc_out_low[:, part_enc:], embed_piece], 1
     )
     third_blob = jnp.concatenate([dec_in_low, dec_out_low, head_low], 1)
-    first_all = spread(first_blob)
-    second_all = spread(second_blob)
-    third_all = spread(third_blob)
+    first_all, first_marks = spread(first_blob)
+    second_all, second_marks = spread(second_blob, first_marks[0], first_marks[3])
+    third_all, third_marks = spread(third_blob, second_marks[0], second_marks[3])
 
     def flat(array):
         return array.reshape(2, -1, array.shape[-1])
@@ -357,7 +413,8 @@
     dec_in_all, dec_out_all, head_all = columns_of(flat(third_all), third_widths)
     dec_qkv, dec_up = dec_in_all[..., : 3 * part_dec], dec_in_all[..., 3 * part_dec :]
     dec_proj, dec_down = dec_out_all[..., :part_dec], dec_out_all[..., part_dec:]
-    patch_all = patch_all.reshape(2, -1, half_enc)
+    patch_all = patch_all.reshape(2, data_size, patch_rows, half_enc).transpose(1, 0, 2, 3)
+    patch_all = patch_all.reshape(pix_width, half_enc)
     embed_other = swap(embed_all)
     embed_even = jnp.where(c == 0, embed_all, embed_other)
     embed_odd = jnp.where(c == 0, embed_other, embed_all)
@@ -376,30 +433,37 @@
     def shown_of(visible_row):
         return jnp.any(one_hot(visible_row, tokens), axis=0).astype(FLOAT_TYPE)
 
-    shown_slots = jnp.stack([shown_of(visible[slot]) for slot in range(slot_total)])
-    per_token = jnp.sum(valid, -1).astype(FLOAT_TYPE)
-    valid_count = jnp.sum((1.0 - shown_slots) * alive.astype(FLOAT_TYPE)[:, None] * per_token)
-    valid_count = total_over(valid_count * (pix_width // patch_positions), DATA)
-
-    def seen_of(slot):
+    start = after(x, first_blob)
+    away = slot_total - 1 - start
+    own_slot, away_slot = pick(pixels, start), pick(pixels, away)
+
+    def seen_of(slot, rows):
         chosen = low(one_hot(pick(visible, slot), tokens))
-        rows = low(product("vt,tp->vp", chosen, pick(pixels, slot)))
-        rows = rows.reshape(vis_count, data_size, 2, patch_rows)
-        return pick(rows, c, 2).reshape(vis_count, data_size * patch_rows)
-
-    def pixels_of(slot):
-        rows = pick(pixels, slot).reshape(tokens, 2, 2, pix_width // 4)
-        rows = pick(rows, c, 2).reshape(tokens, pix_width // 2)
-        return jnp.concatenate([rows, low(pick(valid, slot))], 1)
-
-    away = slot_total - 1 - x
-    visible_row = jnp.where(use_own, pick(visible, x), shift(pick(visible, away), "z", half_step))
-    seen_rows = jnp.where(use_own, seen_of(x), shift(seen_of(away), "z", half_step))
+        return low(product("vt,tp->vp", chosen, rows))
+
+    visible_row = jnp.where(use_own, pick(visible, start), shift(pick(visible, away), "z", half_step))
+    seen_away = halves_of(seen_of(away, away_slot), c)
+    seen_away = both(shift(seen_away, "z", half_step), "c", c, 1)
+    seen_rows = jnp.where(use_own, seen_of(after(start, *first_marks[0]), own_slot), seen_away)
     chosen = low(one_hot(visible_row, tokens))
     hidden_row = 1.0 - shown_of(visible_row)
 
-    stream = product("lp,xpd->xld", seen_rows, patch_all)
-    stream = join(jnp.concatenate([stream[0], stream[1]], 1)) + angles_of(visible_row, width_enc)
+    visible_late = after(visible, *first_marks[3])
+    counted = jnp.stack([1.0 - shown_of(visible_late[slot]) for slot in range(slot_total)])
+    counted = counted * alive.astype(FLOAT_TYPE)[:, None]
+    valid_count = jnp.sum(counted[:, :, None] * valid.astype(FLOAT_TYPE))
+    valid_count = total_over(valid_count * (pix_width // patch_positions), DATA)
+
+    def pixels_of(slot, rows):
+        place = after(c, *first_marks[3])
+        half = pix_width // 2
+        cols = [halves_of(rows[:, first : first + half], place) for first in (0, half)]
+        return jnp.concatenate(cols + [low(pick(valid, slot))], 1)
+
+    own_pack, away_pack = pixels_of(start, own_slot), pixels_of(away, away_slot)
+    pack_moved = shift(after(away_pack, *third_marks[0]), "z", half_step)
+
+    stream = both(product("lp,pd->ld", seen_rows, patch_all), "c", c, 1) + angles_of(visible_row, width_enc)
     stream, enc_attn_kept = attn_fwd(
         stream, enc_qkv, enc_proj, enc_gains[0], enc_gains[1], enc_heads
     )
@@ -408,23 +472,16 @@
     enc_normed_low = low(normed)
     embedded = product("ld,dc->lc", enc_normed_low, full_embed)
 
-    own_pixels = pixels_of(x)
-    sent_pixels, embedded = lax.optimization_barrier((pixels_of(away), embedded))
-    pixel_pack = jnp.where(use_own, own_pixels, shift(sent_pixels, "z", half_step))
 
     embedded_high = low(embedded)
     embedded_rest = low(embedded - embedded_high.astype(FLOAT_TYPE))
     placed = product("vt,vc->tc", chosen, jnp.concatenate([embedded_high, embedded_rest], 1))
     placed = placed[:, :width_dec] + placed[:, width_dec:]
-    stream = placed + hidden_row[:, None] * mask_token + angles_of(jnp.arange(tokens), width_dec)
+    stream = placed + hidden_row[:, None] * mask_token + places_of(tokens, width_dec)
     stream, dec_attn_kept = attn_fwd(
         stream, dec_qkv, dec_proj, dec_gains[0], dec_gains[1], dec_heads
     )
-    stream, dec_mlp_kept = mlp_fwd(stream, dec_up, dec_down, dec_gains[2], dec_gains[3])
-    normed, dec_norm_kept = norm_fwd(stream, dec_gains[4], dec_gains[5])
-    dec_normed_low = low(normed)
-    predicted = product("ld,xdp->xlp", dec_normed_low, head_all)
-
+    pixel_pack = jnp.where(use_own, own_pack, after(pack_moved, stream))
     pixel_cols = pixel_pack[:, : pix_width // 2].astype(FLOAT_TYPE)
     valid_cols = pixel_pack[:, pix_width // 2 :].astype(FLOAT_TYPE)
     half_mean = jnp.mean(pixel_cols, -1, keepdims=True)
@@ -435,6 +492,11 @@
     gap = half_both[:, :1] - other_both[:, :1]
     variance = (half_both[:, 1:] + other_both[:, 1:]) / pix_width + 0.25 * gap * gap
     target = (pixel_cols - mean) * lax.rsqrt(variance + EPS_PIX)
+    stream, dec_mlp_kept = mlp_fwd(stream, dec_up, dec_down, dec_gains[2], dec_gains[3])
+    normed, dec_norm_kept = norm_fwd(stream, dec_gains[4], dec_gains[5])
+    dec_normed_low = low(normed)
+    predicted = product("ld,xdp->xlp", dec_normed_low, head_all)
+
     half_positions = patch_positions // 2
     front = jnp.where(c == 0, valid_cols[:, :half_positions], valid_cols[:, half_positions:])
     back = jnp.where(c == 0, valid_cols[:, half_positions:], valid_cols[:, :half_positions])
@@ -454,13 +516,11 @@
     stream_grad, dec_up_grad, dec_down_grad, dec_gain_three, dec_shift_three = mlp_back(
         stream_grad, dec_mlp_kept, dec_up, dec_down, dec_gains[2]
     )
+    dec_tail_sum = collect_pieces([dec_up_grad, dec_down_grad, head_grad], data_size)
     stream_grad, dec_qkv_grad, dec_proj_grad, dec_gain_one, dec_shift_one = attn_back(
         stream_grad, dec_attn_kept, dec_qkv, dec_proj, dec_gains[0], dec_heads
     )
-    third_grads = jnp.concatenate(
-        [dec_qkv_grad, dec_up_grad, dec_proj_grad, dec_down_grad, head_grad], 2
-    )
-    third_sum = collect(third_grads.reshape(third_all.shape))
+    dec_attn_sum = collect_pieces([dec_qkv_grad, dec_proj_grad], data_size)
     mask_grad = jnp.sum(hidden_row[:, None] * stream_grad, axis=0)
     embedded_grad = low(product("vt,tc->vc", chosen, low(stream_grad)))
     embed_mine = jnp.stack(
@@ -474,15 +534,13 @@
     stream_grad, enc_up_grad, enc_down_grad, enc_gain_three, enc_shift_three = mlp_back(
         stream_grad, enc_mlp_kept, enc_up, enc_down, enc_gains[2]
     )
-    second_grads = jnp.concatenate([enc_up_grad, enc_down_grad, embed_grad], 2)
-    second_sum = collect(second_grads.reshape(second_all.shape))
+    enc_tail_sum = collect_pieces([enc_up_grad, enc_down_grad, embed_grad], data_size)
     stream_grad, enc_qkv_grad, enc_proj_grad, enc_gain_one, enc_shift_one = attn_back(
         stream_grad, enc_attn_kept, enc_qkv, enc_proj, enc_gains[0], enc_heads
     )
     stream_low = low(stream_grad)
-    patch_grad = low(
-        product("lp,xld->xpd", seen_rows, jnp.stack([stream_low[:, :half_enc], stream_low[:, half_enc:]]))
-    )
+    patch_grad = low(product("lp,ld->pd", seen_rows, halves_of(stream_low, c)))
+    patch_grad = patch_grad.reshape(data_size, 2, patch_rows, half_enc).transpose(1, 0, 2, 3)
     norm_pieces = jnp.concatenate(
         [
             enc_gain_one,
@@ -507,20 +565,22 @@
     norm_half = norm_share // 2
     norm_grads = low(norm_grad).reshape(data_size, 2, norm_half).transpose(1, 0, 2)
     norm_grads = jnp.pad(norm_grads, ((0, 0), (0, 0), (0, norm_room - norm_half)))
-    first_grads = jnp.concatenate(
+    enc_attn_sum = collect_pieces(
         [
             enc_qkv_grad,
             enc_proj_grad,
             patch_grad.reshape(2, width_enc, -1),
             norm_grads.reshape(2, width_enc, LANES),
         ],
-        2,
-    )
-    first_sum = collect(first_grads.reshape(first_all.shape))
-
-    qkv_sum, proj_sum, patch_sum, norm_sum = columns_of(first_sum, first_widths)
-    up_sum, down_sum, embed_sum = columns_of(second_sum, second_widths)
-    dec_in_sum, dec_out_sum, head_sum = columns_of(third_sum, third_widths)
+        data_size,
+    )
+
+    qkv_sum, proj_sum, patch_sum, norm_sum = columns_of(enc_attn_sum, first_widths)
+    up_sum, down_sum, embed_sum = columns_of(enc_tail_sum, second_widths)
+    dec_qkv_sum, dec_proj_sum = columns_of(dec_attn_sum, (3 * part_dec, part_dec))
+    dec_up_sum, dec_down_sum, head_sum = columns_of(
+        dec_tail_sum, (4 * part_dec, 4 * part_dec, head_low.shape[1])
+    )
     norm_sum = low(norm_sum.reshape(-1)[:norm_half])
     patch_sum, embed_sum = low(patch_sum), low(embed_sum)
     shared_square = sum(
@@ -528,30 +588,23 @@
     ) + 0.5 * jnp.sum(jnp.square(norm_sum.astype(FLOAT_TYPE)))
     own_square = sum(
         jnp.sum(jnp.square(piece))
-        for piece in (qkv_sum, proj_sum, up_sum, down_sum, third_sum)
+        for piece in (qkv_sum, proj_sum, up_sum, down_sum, dec_attn_sum, dec_tail_sum)
     )
     totals = total_over(
         jnp.stack([loss_part, own_square + shared_square]), ("c", "x", "y", "z")
     )
     loss_sum, grad_norm = totals[0], jnp.sqrt(totals[1])
 
-    def both(piece, axis, place, dimension):
-        other = swap(piece, axis)
-        return jnp.where(
-            place == 0,
-            jnp.concatenate([piece, other], dimension),
-            jnp.concatenate([other, piece], dimension),
-        )
-
-    patch_sum = patch_sum.reshape(patch_rows, half_enc)
-    patch_sum = both(both(patch_sum, "c", c, 0), "x", x, 1)
+    patch_sum = both(both(patch_sum, "c", c, 1), "x", x, 0)
     embed_sum = both(both(embed_sum, "c", c, 1), "x", x, 1)
     norm_sum = both(norm_sum, "x", x, 0)
     reduced = (
         jnp.concatenate([qkv_sum, up_sum], 1).reshape(encoder_in.shape),
         jnp.concatenate([proj_sum, down_sum], 1).reshape(rows_enc, -1, part_enc).transpose(1, 2, 0),
-        dec_in_sum.reshape(decoder_in.shape),
-        dec_out_sum.reshape(rows_dec, -1, part_dec).transpose(1, 2, 0),
+        jnp.concatenate([dec_qkv_sum, dec_up_sum], 1).reshape(decoder_in.shape),
+        jnp.concatenate([dec_proj_sum, dec_down_sum], 1)
+        .reshape(rows_dec, -1, part_dec)
+        .transpose(1, 2, 0),
         patch_sum.astype(FLOAT_TYPE),
         embed_sum.astype(FLOAT_TYPE),
         head_sum,

time: 643 us -> 593 us (0.922)
  local copies, waits for them, and re-layouts: 139 us -> 106 us
  waiting for transfers between devices: 218 us -> 188 us
  starting transfers between devices: 76.9 us -> 94.2 us
    ppermute x21 -> x24, starting transfers between devices: 18.2 us -> 44.7 us  [shift(): lax.ppermute(values, axis, [(i, (i + step) % size) for i in range(size)])]
    ppermute x8, waiting for transfers between devices: 40.5 us -> 16.3 us  [total_over(): lax.ppermute(values, axis, [(i, i ^ step) for i in range(size)])]
    dynamic_slice x8 -> x5, local copies, waits for them, and re-layouts: 34.5 us -> 12.4 us  [pick(): return lax.dynamic_index_in_dim(array, index, axis, keepdims=False)]
    ppermute x41 -> x46, waiting for transfers between devices: 120 us -> 99.8 us  [swap(): return lax.ppermute(values, axis, SWAP)]
    ppermute x21 -> x24, waiting for transfers between devices: 57.2 us -> 71.7 us  [shift(): lax.ppermute(values, axis, [(i, (i + step) % size) for i in range(size)])]
    dynamic_update_slice x19 -> x0, local copies, waits for them, and re-layouts: 12.4 us -> none  [the longest x9 6.26 us: spread(): lax.dynamic_update_slice(whole, part[None, :, None], (at_x, 0, at_y, 0, 0))]
    ppermute x8, starting transfers between devices: 19.1 us -> 10.1 us  [total_over(): lax.ppermute(values, axis, [(i, i ^ step) for i in range(size)])]
    reshape x6 -> x1, local copies, waits for them, and re-layouts: 8.78 us -> 1.15 us  [on_device(): patch_grad.reshape(data_size, 2, patch_rows, half_enc).transpose(1, 0, 2, 3)]
  transfers between devices with their start and end apart: 70 -> 78, of which waited for: 38 -> 39; matrix products, arithmetic and copies ran while one was open for 38% -> 39% of each run, Pallas kernels for 0% -> 1%
where the time goes in v2:
time: 593 us; the launch traced here: 585 us
  waiting for transfers between devices  188 us (32%)
  local copies, waits for them, and re-layouts  106 us (18%)
  starting transfers between devices  94.2 us (16%)
  other arithmetic  88.5 us (15%)
  matrix products  86.9 us (15%)
  between operations  15.3 us (3%)
    ppermute x46, waiting for transfers between devices, swap(): return lax.ppermute(values, axis, SWAP)  99.8 us
    dot_general x57, matrix products, product(): return jnp.einsum(spec, left, right, preferred_element_type=FLOAT_TYPE)  86.9 us
    ppermute x24, waiting for transfers between devices, shift(): lax.ppermute(values, axis, [(i, (i + step) % size) for i in range(size)])  71.7 us
    ppermute x24, starting transfers between devices, shift(): lax.ppermute(values, axis, [(i, (i + step) % size) for i in range(size)])  44.7 us
    ppermute x46, starting transfers between devices, swap(): return lax.ppermute(values, axis, SWAP)  39.4 us
    unnamed x335, local copies, waits for them, and re-layouts  29.9 us
    concatenate x7, local copies, waits for them, and re-layouts, collect_pieces(): grads = jnp.concatenate(pieces, 2)  24.6 us
    convert_element_type x17, other arithmetic, low(): return values.astype(NARROW_TYPE)  17.9 us
  transfers between devices with their start and end apart: 78, of which 39 were waited for; matrix products, arithmetic and copies ran while one was open for 39% of the time, Pallas kernels for 1%

profile of v2, /device:TPU:0, one launch (start us, length us, event | category | flops | bytes accessed | tf_op | source)
XLA Modules:
  0.0 584.8 jit_solution(1626370662834140811)
XLA Ops:
  6.2 5.1 collective-permute-start.2
  24.7 9.8 %constant_dynamic-slice_fusion.8 = (bf16[1,588,1536]{2,0,1:T(2,128)(2,1)S(1)}, bf16[1,588,1536]{2,0,1:T(2,128)(2,1)S(1)}) fusion(bf16[4,588,1536]{2,0,1:T(4,128)(2,1)} %param.29, s32[]{:T(128)S(6)} %select_n.346, s32[]{:T(128)S(6)} %select_n.349), kind=kLoop, calls=%fused_computation.535 | loop fusion | bytes 7225352 | tf_op jit(solution)/shard_map/jit(dynamic_index_in_dim)/dynamic_slice | solution.py:297
  52.7 12.8 %collective-permute-done.14 = s32[147]{0:T(256)S(1)} collective-permute-done((s32[147]{0:T(256)S(1)}, s32[147]{0:T(256)S(1)}, u32[]{:S(2)}, u32[]{:S(2)}) %collective-permute-start.14) | collective-permute-done | bytes 620 | tf_op jit(solution)/shard_map/ppermute | solution.py:56
  67.8 9.2 %collective-permute-done.15 = bf16[147,768]{1,0:T(8,128)(2,1)S(1)} collective-permute-done((bf16[147,768]{1,0:T(8,128)(2,1)S(1)}, bf16[147,768]{1,0:T(8,128)(2,1)S(1)}, u32[]{:S(2)}, u32[]{:S(2)}) %collective-permute-start.15) | collective-permute-done | bytes 225824 | tf_op jit(solution)/shard_map/ppermute | solution.py:56
  81.1 6.4 %collective-permute-done.7 = bf16[96,1664]{1,0:T(8,128)(2,1)S(1)} collective-permute-done((bf16[96,1664]{1,0:T(8,128)(2,1)}, bf16[96,1664]{1,0:T(8,128)(2,1)S(1)}, u32[]{:S(2)}, u32[]{:S(2)}) %collective-permute-start.7) | collective-permute-done | bytes 319520 | tf_op jit(solution)/shard_map/ppermute | solution.py:56
  94.7 13.8 %collective-permute-done.11 = bf16[64,1920]{1,0:T(8,128)(2,1)S(1)} collective-permute-done((bf16[64,1920]{1,0:T(8,128)(2,1)S(1)}, bf16[64,1920]{1,0:T(8,128)(2,1)S(1)}, u32[]{:S(2)}, u32[]{:S(2)}) %collective-permute-start.11) | collective-permute-done | bytes 245792 | tf_op jit(solution)/shard_map/ppermute | solution.py:56
  146.4 10.9 %collective-permute-done.22 = bf16[2,96,1664]{2,1,0:T(8,128)(2,1)S(1)} collective-permute-done((bf16[2,96,1664]{2,1,0:T(8,128)(2,1)S(1)}, bf16[2,96,1664]{2,1,0:T(8,128)(2,1)S(1)}, u32[]{:S(2)}, u32[]{:S(2)}) %collective-permute-start.22) | collective-permute-done | bytes 639008 | tf_op jit(solution)/shard_map/ppermute | solution.py:41
  172.4 7.4 %collective-permute-done.26 = bf16[4,64,1920]{2,1,0:T(8,128)(2,1)S(1)} collective-permute-done((bf16[4,64,1920]{2,1,0:T(8,128)(2,1)S(1)}, bf16[4,64,1920]{2,1,0:T(8,128)(2,1)S(1)}, u32[]{:S(2)}, u32[]{:S(2)}) %collective-permute-start.26) | collective-permute-done | bytes 983072 | tf_op jit(solution)/shard_map/ppermute | solution.py:41
  183.8 6.5 %collective-permute-done.28 = bf16[2,64,1920]{2,1,0:T(8,128)(2,1)S(1)} collective-permute-done((bf16[2,64,1920]{2,1,0:T(8,128)(2,1)S(1)}, bf16[2,64,1920]{2,1,0:T(8,128)(2,1)S(1)}, u32[]{:S(2)}, u32[]{:S(2)}) %collective-permute-start.28) | collective-permute-done | bytes 491552 | tf_op jit(solution)/shard_map/ppermute | solution.py:41
  206.8 4.3 multiply_reduce_fusion.2
  216.7 3.9 collective-permute-start.33
  232.5 7.5 %fusion.12 = (bf16[2,588,512]{2,1,0:T(8,128)(2,1)S(1)}, f32[2,588,512]{2,1,0:T(8,128)}, f32[2,512,588]{1,2,0:T(8,128)}) fusion(f32[588,512]{1,0:T(8,128)S(1)} %get-tuple-element.224, f32[512]{0:T(512)S(1)} %copy-done.143, f32[512]{0:T(512)S(1)} %copy-done.109, f32[588]{0:T(1024)S(1)} %add_rsqrt_fusion.1, f32[588]{0:T(1024)S(1)} %broadcast_multiply_fusion.9, ...), kind=kOutput, calls=%fused_computation.35 | convolution fusion | flops 657205248 | bytes 8294400 | tf_op jit(solution)/shard_map/ld,xdc->xlc/dot_general | solution.py:33
  263.0 4.7 copy.421
  273.1 8.0 %collective-permute-done.61 = bf16[2,64,1408]{2,1,0:T(8,128)(2,1)S(1)} collective-permute-done((bf16[2,64,1408]{2,1,0:T(8,128)(2,1)S(1)}, bf16[2,64,1408]{2,1,0:T(8,128)(2,1)S(1)}, u32[]{:S(2)}, u32[]{:S(2)}) %collective-permute-start.61) | collective-permute-done | bytes 360480 | tf_op jit(solution)/shard_map/ppermute | solution.py:41
  291.3 7.3 %fusion.68 = bf16[2,588,1,4,32]{1,4,3,0,2:T(8,128)(2,1)} fusion(bf16[2,4,588,32]{2,3,1,0:T(8,128)(2,1)S(1)} %bitcast.865, f32[2,4,588,588]{2,3,1,0:T(8,128)} %copy-done.9, f32[2,4,588]{2,1,0:T(4,128)S(1)} %log_add_fusion), kind=kOutput, calls=%fused_computation.151 | convolution fusion | flops 185469312 | bytes 11684736 | tf_op jit(solution)/shard_map/xhqk,xhqe->xkhe/dot_general | solution.py:33
  298.5 8.0 %multiply_reduce_fusion = (f32[2,4,588]{2,1,0:T(4,128)S(1)}, f32[2,4,588,588]{2,3,1,0:T(8,128)S(1)}) fusion(f32[2,4,588,588]{2,3,1,0:T(8,128)} %copy-done.9, f32[2,4,588]{2,1,0:T(4,128)S(1)} %log_add_fusion, bf16[2,4,588,32]{2,3,1,0:T(8,128)(2,1)} %bitcast.866, bf16[3,2,4,588,32]{3,4,2,1,0:T(8,128)(2,1)} %bitcast.843), kind=kOutput, calls=%fused_computation.1 | convolution fusion | flops 188080032 | bytes 23880960 | tf_op jit(solution)/shard_map/xhqe,xhke->xhqk/dot_general | solution.py:33
  366.0 7.7 %copy.408 = bf16[2,768,1664]{2,1,0:T(8,128)(2,1)} copy(bf16[2,768,1664]{1,2,0:T(8,128)(2,1)} %pad_maximum_fusion) | data formatting | bytes 10223616 | tf_op jit(solution)/shard_map/concatenate | solution.py:160
  406.6 6.4 %concatenate.160 = bf16[2,4,2,96,1280]{4,3,2,1,0:T(8,128)(2,1)} concatenate(bf16[2,4,2,96,576]{4,3,2,1,0:T(8,128)(2,1)S(1)} %bitcast.846, bf16[2,4,2,96,192]{4,3,2,1,0:T(8,128)(2,1)S(1)} %bitcast.862, bf16[2,4,2,96,384]{4,3,2,1,0:T(8,128)(2,1)} %bitcast.860, bf16[2,4,2,96,128]{4,3,2,1,0:T(8,128)(2,1)S(1)} %copy-done.48), dimensions={4} | concatenate | bytes 7864320 | tf_op jit(solution)/shard_map/concatenate | solution.py:160
  421.0 8.0 %collective-permute-done.40 = bf16[2,96,1280]{2,1,0:T(8,128)(2,1)S(1)} collective-permute-done((bf16[2,96,1280]{2,1,0:T(8,128)(2,1)S(1)}, bf16[2,96,1280]{2,1,0:T(8,128)(2,1)S(1)}, u32[]{:S(2)}, u32[]{:S(2)}) %collective-permute-start.40) | collective-permute-done | bytes 491552 | tf_op jit(solution)/shard_map/ppermute | solution.py:41
  435.5 24.5 %collective-permute-done.50 = bf16[4,96,1664]{2,1,0:T(8,128)(2,1)S(1)} collective-permute-done((bf16[4,96,1664]{2,1,0:T(8,128)(2,1)S(1)}, bf16[4,96,1664]{2,1,0:T(8,128)(2,1)S(1)}, u32[]{:S(2)}, u32[]{:S(2)}) %collective-permute-start.50) | collective-permute-done | bytes 1277984 | tf_op jit(solution)/shard_map/ppermute | solution.py:41
  463.4 15.8 %collective-permute-done.43 = bf16[4,96,1280]{2,1,0:T(8,128)(2,1)S(1)} collective-permute-done((bf16[4,96,1280]{2,1,0:T(8,128)(2,1)S(1)}, bf16[4,96,1280]{2,1,0:T(8,128)(2,1)S(1)}, u32[]{:S(2)}, u32[]{:S(2)}) %collective-permute-start.43) | collective-permute-done | bytes 983072 | tf_op jit(solution)/shard_map/ppermute | solution.py:41
  491.8 10.7 %collective-permute-start.52 = (bf16[96,1664]{1,0:T(8,128)(2,1)}, bf16[96,1664]{1,0:T(8,128)(2,1)}, u32[]{:S(2)}, u32[]{:S(2)}) collective-permute-start(bf16[96,1664]{1,0:T(8,128)(2,1)} %get-tuple-element.270), channel_id=1, source_target_pairs={{0,16},{8,24},{16,0},{24,8},{1,17},{9,25},{17,1},{25,9},{2,18},{10... | collective-permute-start | bytes 958472 | tf_op jit(solution)/shard_map/ppermute | solution.py:56
  502.5 12.3 %collective-permute-done.45 = bf16[96,1280]{1,0:T(8,128)(2,1)S(1)} collective-permute-done((bf16[96,1280]{1,0:T(8,128)(2,1)S(1)}, bf16[96,1280]{1,0:T(8,128)(2,1)S(1)}, u32[]{:S(2)}, u32[]{:S(2)}) %collective-permute-start.45) | collective-permute-done | bytes 245792 | tf_op jit(solution)/shard_map/ppermute | solution.py:56
  520.1 11.9 %collective-permute-done.52 = bf16[96,1664]{1,0:T(8,128)(2,1)} collective-permute-done((bf16[96,1664]{1,0:T(8,128)(2,1)}, bf16[96,1664]{1,0:T(8,128)(2,1)}, u32[]{:S(2)}, u32[]{:S(2)}) %collective-permute-start.52) | collective-permute-done | bytes 319520 | tf_op jit(solution)/shard_map/ppermute | solution.py:56
  (768 shorter events, 346.6 us)
Async XLA Ops:
  6.2 34.8 %collective-permute-start.2 = (bf16[96,1280]{1,0:T(8,128)(2,1)S(1)}, bf16[96,1280]{1,0:T(8,128)(2,1)S(1)}, u32[]{:S(2)}, u32[]{:S(2)}) collective-permute-start(bf16[96,1280]{1,0:T(8,128)(2,1)S(1)} %concatenate.141), channel_id=1, source_target_pairs={{0,24},{8,0},{16,8},{24,16},{1,25},{9,1},{17,9},{25,17},{2,26},{10... | collective-permute-start | bytes 737288 | tf_op jit(solution)/shard_map/ppermute | solution.py:56
  41.0 37.9 %collective-permute-start.9 = (bf16[96,1664]{1,0:T(8,128)(2,1)}, bf16[96,1664]{1,0:T(8,128)(2,1)}, u32[]{:S(2)}, u32[]{:S(2)}) collective-permute-start(bf16[96,1664]{1,0:T(8,128)(2,1)} %pad_maximum_fusion.13), channel_id=1, source_target_pairs={{0,24},{8,0},{16,8},{24,16},{1,25},{9,1},{17,9},{25,17},{2,26},{10... | collective-permute-start | bytes 958472 | tf_op jit(solution)/shard_map/ppermute | solution.py:56
  43.9 37.2 %collective-permute-start.8 = (bf16[96,1664]{1,0:T(8,128)(2,1)}, bf16[96,1664]{1,0:T(8,128)(2,1)}, u32[]{:S(2)}, u32[]{:S(2)}) collective-permute-start(bf16[96,1664]{1,0:T(8,128)(2,1)} %pad_maximum_fusion.13), channel_id=1, source_target_pairs={{0,16},{8,24},{16,0},{24,8},{1,17},{9,25},{17,1},{25,9},{2,18},{10... | collective-permute-start | bytes 958472 | tf_op jit(solution)/shard_map/ppermute | solution.py:56
  45.6 31.4 %collective-permute-start.5 = (bf16[4,96,1280]{2,1,0:T(8,128)(2,1)S(1)}, bf16[4,96,1280]{2,1,0:T(8,128)(2,1)S(1)}, u32[]{:S(2)}, u32[]{:S(2)}) collective-permute-start(bf16[4,96,1280]{2,1,0:T(8,128)(2,1)S(1)} %shard_map.484), channel_id=1, source_target_pairs={{0,4},{4,0},{1,5},{5,1},{2,6},{6,2},{3,7},{7,3},{8,12},{12,8},{9,1... | collective-permute-start | bytes 2949128 | tf_op jit(solution)/shard_map/ppermute | solution.py:41
  47.2 30.1 %collective-permute-start.3 = (bf16[4,96,1280]{2,1,0:T(8,128)(2,1)S(1)}, bf16[4,96,1280]{2,1,0:T(8,128)(2,1)S(1)}, u32[]{:S(2)}, u32[]{:S(2)}) collective-permute-start(bf16[4,96,1280]{2,1,0:T(8,128)(2,1)S(1)} %shard_map.484), channel_id=1, source_target_pairs={{0,2},{2,0},{1,3},{3,1},{4,6},{6,4},{5,7},{7,5},{8,10},{10,8},{9,1... | collective-permute-start | bytes 2949128 | tf_op jit(solution)/shard_map/ppermute | solution.py:41
  77.3 31.8 %collective-permute-start.6 = (bf16[2,96,1280]{2,1,0:T(8,128)(2,1)S(1)}, bf16[2,96,1280]{2,1,0:T(8,128)(2,1)S(1)}, u32[]{:S(2)}, u32[]{:S(2)}) collective-permute-start(bf16[2,96,1280]{2,1,0:T(8,128)(2,1)S(1)} %slice.759), channel_id=1, source_target_pairs={{0,2},{2,0},{1,3},{3,1},{4,6},{6,4},{5,7},{7,5},{8,10},{10,8},{9,1... | collective-permute-start | bytes 1474568 | tf_op jit(solution)/shard_map/ppermute | solution.py:41
  78.9 30.2 %collective-permute-start.4 = (bf16[2,96,1280]{2,1,0:T(8,128)(2,1)S(1)}, bf16[2,96,1280]{2,1,0:T(8,128)(2,1)S(1)}, u32[]{:S(2)}, u32[]{:S(2)}) collective-permute-start(bf16[2,96,1280]{2,1,0:T(8,128)(2,1)S(1)} %slice.758), channel_id=1, source_target_pairs={{0,4},{4,0},{1,5},{5,1},{2,6},{6,2},{3,7},{7,3},{8,12},{12,8},{9,1... | collective-permute-start | bytes 1474568 | tf_op jit(solution)/shard_map/ppermute | solution.py:41
  137.0 91.0 %collective-permute-start.13 = (bf16[588,1024]{1,0:T(8,128)(2,1)}, bf16[588,1024]{1,0:T(8,128)(2,1)}, u32[]{:S(2)}, u32[]{:S(2)}) collective-permute-start(bf16[588,1024]{1,0:T(8,128)(2,1)} %pad_maximum_fusion.4), channel_id=1, source_target_pairs={{0,16},{8,24},{16,0},{24,8},{1,17},{9,25},{17,1},{25,9},{2,18},{10... | collective-permute-start | bytes 3612680 | tf_op jit(solution)/shard_map/ppermute | solution.py:56
  283.4 60.2 %collective-permute-start.64 = (bf16[4,64,1408]{2,1,0:T(8,128)(2,1)}, bf16[4,64,1408]{2,1,0:T(8,128)(2,1)}, u32[]{:S(2)}, u32[]{:S(2)}) collective-permute-start(bf16[4,64,1408]{2,1,0:T(8,128)(2,1)} %pad_maximum_fusion.11), channel_id=1, source_target_pairs={{0,2},{2,0},{1,3},{3,1},{4,6},{6,4},{5,7},{7,5},{8,10},{10,8},{9,1... | collective-permute-start | bytes 2162696 | tf_op jit(solution)/shard_map/ppermute | solution.py:41
  286.0 57.6 %collective-permute-start.62 = (bf16[4,64,1408]{2,1,0:T(8,128)(2,1)}, bf16[4,64,1408]{2,1,0:T(8,128)(2,1)}, u32[]{:S(2)}, u32[]{:S(2)}) collective-permute-start(bf16[4,64,1408]{2,1,0:T(8,128)(2,1)} %pad_maximum_fusion.10), channel_id=1, source_target_pairs={{0,4},{4,0},{1,5},{5,1},{2,6},{6,2},{3,7},{7,3},{8,12},{12,8},{9,1... | collective-permute-start | bytes 2162696 | tf_op jit(solution)/shard_map/ppermute | solution.py:41
  346.3 85.1 %collective-permute-start.65 = (bf16[64,1408]{1,0:T(8,128)(2,1)}, bf16[64,1408]{1,0:T(8,128)(2,1)}, u32[]{:S(2)}, u32[]{:S(2)}) collective-permute-start(bf16[64,1408]{1,0:T(8,128)(2,1)} %get-tuple-element.281), channel_id=1, source_target_pairs={{0,8},{8,16},{16,24},{24,0},{1,9},{9,17},{17,25},{25,1},{2,10},{10... | collective-permute-start | bytes 540680 | tf_op jit(solution)/shard_map/ppermute | solution.py:56
  346.3 86.5 %collective-permute-start.67 = (bf16[64,1408]{1,0:T(8,128)(2,1)}, bf16[64,1408]{1,0:T(8,128)(2,1)}, u32[]{:S(2)}, u32[]{:S(2)}) collective-permute-start(bf16[64,1408]{1,0:T(8,128)(2,1)} %get-tuple-element.282), channel_id=1, source_target_pairs={{0,24},{8,0},{16,8},{24,16},{1,25},{9,1},{17,9},{25,17},{2,26},{10... | collective-permute-start | bytes 540680 | tf_op jit(solution)/shard_map/ppermute | solution.py:56
  350.1 83.4 %collective-permute-start.66 = (bf16[64,1408]{1,0:T(8,128)(2,1)}, bf16[64,1408]{1,0:T(8,128)(2,1)}, u32[]{:S(2)}, u32[]{:S(2)}) collective-permute-start(bf16[64,1408]{1,0:T(8,128)(2,1)} %get-tuple-element.283), channel_id=1, source_target_pairs={{0,16},{8,24},{16,0},{24,8},{1,17},{9,25},{17,1},{25,9},{2,18},{10... | collective-permute-start | bytes 540680 | tf_op jit(solution)/shard_map/ppermute | solution.py:56
  378.9 36.9 %collective-permute-start.47 = (bf16[2,96,1664]{2,1,0:T(8,128)(2,1)}, bf16[2,96,1664]{2,1,0:T(8,128)(2,1)}, u32[]{:S(2)}, u32[]{:S(2)}) collective-permute-start(bf16[2,96,1664]{2,1,0:T(8,128)(2,1)} %get-tuple-element.245), channel_id=1, source_target_pairs={{0,2},{2,0},{1,3},{3,1},{4,6},{6,4},{5,7},{7,5},{8,10},{10,8},{9,1... | collective-permute-start | bytes 1916936 | tf_op jit(solution)/shard_map/ppermute | solution.py:41
  429.0 31.0 %collective-permute-start.50 = (bf16[4,96,1664]{2,1,0:T(8,128)(2,1)S(1)}, bf16[4,96,1664]{2,1,0:T(8,128)(2,1)S(1)}, u32[]{:S(2)}, u32[]{:S(2)}) collective-permute-start(bf16[4,96,1664]{2,1,0:T(8,128)(2,1)S(1)} %pad_maximum_fusion.3), channel_id=1, source_target_pairs={{0,2},{2,0},{1,3},{3,1},{4,6},{6,4},{5,7},{7,5},{8,10},{10,8},{9,1... | collective-permute-start | bytes 3833864 | tf_op jit(solution)/shard_map/ppermute | solution.py:41
  430.6 31.0 %collective-permute-start.48 = (bf16[4,96,1664]{2,1,0:T(8,128)(2,1)S(1)}, bf16[4,96,1664]{2,1,0:T(8,128)(2,1)S(1)}, u32[]{:S(2)}, u32[]{:S(2)}) collective-permute-start(bf16[4,96,1664]{2,1,0:T(8,128)(2,1)S(1)} %pad_maximum_fusion.2), channel_id=1, source_target_pairs={{0,4},{4,0},{1,5},{5,1},{2,6},{6,2},{3,7},{7,3},{8,12},{12,8},{9,1... | collective-permute-start | bytes 3833864 | tf_op jit(solution)/shard_map/ppermute | solution.py:41
  431.4 47.8 %collective-permute-start.43 = (bf16[4,96,1280]{2,1,0:T(8,128)(2,1)S(1)}, bf16[4,96,1280]{2,1,0:T(8,128)(2,1)S(1)}, u32[]{:S(2)}, u32[]{:S(2)}) collective-permute-start(bf16[4,96,1280]{2,1,0:T(8,128)(2,1)S(1)} %pad_maximum_fusion.8), channel_id=1, source_target_pairs={{0,2},{2,0},{1,3},{3,1},{4,6},{6,4},{5,7},{7,5},{8,10},{10,8},{9,1... | collective-permute-start | bytes 2949128 | tf_op jit(solution)/shard_map/ppermute | solution.py:41
  432.8 47.7 %collective-permute-start.41 = (bf16[4,96,1280]{2,1,0:T(8,128)(2,1)S(1)}, bf16[4,96,1280]{2,1,0:T(8,128)(2,1)S(1)}, u32[]{:S(2)}, u32[]{:S(2)}) collective-permute-start(bf16[4,96,1280]{2,1,0:T(8,128)(2,1)S(1)} %pad_maximum_fusion.7), channel_id=1, source_target_pairs={{0,4},{4,0},{1,5},{5,1},{2,6},{6,2},{3,7},{7,3},{8,12},{12,8},{9,1... | collective-permute-start | bytes 2949128 | tf_op jit(solution)/shard_map/ppermute | solution.py:41
  487.0 33.1 %collective-permute-start.51 = (bf16[96,1664]{1,0:T(8,128)(2,1)}, bf16[96,1664]{1,0:T(8,128)(2,1)S(1)}, u32[]{:S(2)}, u32[]{:S(2)}) collective-permute-start(bf16[96,1664]{1,0:T(8,128)(2,1)} %get-tuple-element.268), channel_id=1, source_target_pairs={{0,8},{8,16},{16,24},{24,0},{1,9},{9,17},{17,25},{25,1},{2,10},{10... | collective-permute-start | bytes 958472 | tf_op jit(solution)/shard_map/ppermute | solution.py:56
  487.0 33.0 %collective-permute-start.53 = (bf16[96,1664]{1,0:T(8,128)(2,1)}, bf16[96,1664]{1,0:T(8,128)(2,1)}, u32[]{:S(2)}, u32[]{:S(2)}) collective-permute-start(bf16[96,1664]{1,0:T(8,128)(2,1)} %get-tuple-element.269), channel_id=1, source_target_pairs={{0,24},{8,0},{16,8},{24,16},{1,25},{9,1},{17,9},{25,17},{2,26},{10... | collective-permute-start | bytes 958472 | tf_op jit(solution)/shard_map/ppermute | solution.py:56
  491.8 40.2 %collective-permute-start.52 = (bf16[96,1664]{1,0:T(8,128)(2,1)}, bf16[96,1664]{1,0:T(8,128)(2,1)}, u32[]{:S(2)}, u32[]{:S(2)}) collective-permute-start(bf16[96,1664]{1,0:T(8,128)(2,1)} %get-tuple-element.270), channel_id=1, source_target_pairs={{0,16},{8,24},{16,0},{24,8},{1,17},{9,25},{17,1},{25,9},{2,18},{10... | collective-permute-start | bytes 958472 | tf_op jit(solution)/shard_map/ppermute | solution.py:56
  516.8 50.2 %collective-permute-start.77 = (bf16[512]{0:T(512)(128)(2,1)S(1)}, bf16[512]{0:T(512)(128)(2,1)S(1)}, u32[]{:S(2)}, u32[]{:S(2)}) collective-permute-start(bf16[512]{0:T(512)(128)(2,1)S(1)} %fusion.221), channel_id=1, source_target_pairs={{0,2},{2,0},{1,3},{3,1},{4,6},{6,4},{5,7},{7,5},{8,10},{10,8},{9,1... | collective-permute-start | bytes 3080 | tf_op jit(solution)/shard_map/ppermute | solution.py:41
  516.8 57.8 %collective-permute-start.73 = (bf16[96,384]{1,0:T(8,128)(2,1)}, bf16[96,384]{1,0:T(8,128)(2,1)}, u32[]{:S(2)}, u32[]{:S(2)}) collective-permute-start(bf16[96,384]{1,0:T(8,128)(2,1)} %get-tuple-element.210), channel_id=1, source_target_pairs={{0,1},{1,0},{2,3},{3,2},{4,5},{5,4},{6,7},{7,6},{8,9},{9,8},{10,11... | collective-permute-start | bytes 221192 | tf_op jit(solution)/shard_map/ppermute | solution.py:41
  539.8 33.3 %collective-permute-start.75 = (bf16[96,128]{1,0:T(8,128)(2,1)}, bf16[96,128]{1,0:T(8,128)(2,1)}, u32[]{:S(2)}, u32[]{:S(2)}) collective-permute-start(bf16[96,128]{1,0:T(8,128)(2,1)} %get-tuple-element.208), channel_id=1, source_target_pairs={{0,1},{1,0},{2,3},{3,2},{4,5},{5,4},{6,7},{7,6},{8,9},{9,8},{10,11... | collective-permute-start | bytes 73736 | tf_op jit(solution)/shard_map/ppermute | solution.py:41
  (209 other events, 1422.3 us)

commit v3 on v2

v3 whole, which is shorter than its diff:
```python
import numpy as np

import jax
import jax.numpy as jnp
from jax import lax
from jax.experimental import pallas as pl
from jax.experimental.pallas import tpu as pltpu
from jax.sharding import Mesh
from jax.sharding import PartitionSpec as P

HEADS_ENC = 12
HEADS_DEC = 16
STEP = 10


EPS_NORM = 1e-05
EPS_PIX = 1e-06
CLIP = 0.0002
LR_MATRIX = 0.03
LR_NORM = 0.5
BETA_ONE = 0.9
BETA_TWO = 0.95
ADAM_EPS = 1e-10
DECAY = 0.05
FLOAT_TYPE = jnp.float32
NARROW_TYPE = jnp.bfloat16
SWAP = [(0, 1), (1, 0)]
ACROSS = [(0, 3), (1, 2), (2, 1), (3, 0)]
LANES = 128
VMEM_ROOM = 56 * 2**20
SQRT_HALF = 0.5**0.5
DENSITY = (2.0 * np.pi) ** -0.5
DATA = ("z", "y")


def product(spec, left, right):
    return jnp.einsum(spec, left, right, preferred_element_type=FLOAT_TYPE)


def low(values):
    return values.astype(NARROW_TYPE)


def swap(values, axis="c"):
    return lax.ppermute(values, axis, SWAP)


def join(partial):
    return partial + swap(partial)


def join_low(partial):
    mine = low(partial)
    other = swap(mine)
    return mine.astype(FLOAT_TYPE) + other.astype(FLOAT_TYPE)


def shift(values, axis, step):
    size = lax.axis_size(axis)
    return lax.ppermute(values, axis, [(i, (i + step) % size) for i in range(size)])


def total_over(values, axes):
    for axis in axes:
        size = lax.axis_size(axis)
        if size & (size - 1):
            values = lax.psum(values, axis)
            continue
        step = 1
        while step < size:
            values = values + lax.ppermute(values, axis, [(i, i ^ step) for i in range(size)])
            step *= 2
    return values


def after(value, *others):
    return lax.optimization_barrier((value,) + others)[0]


def vmem_call(body, outs, *ins, scalars=(), scratch=(), flops=0):
    shapes = [jax.ShapeDtypeStruct(shape, kind) for shape, kind in outs]
    moved = sum(int(np.prod(a.shape)) * a.dtype.itemsize for a in [*ins, *shapes])
    return pl.pallas_call(
        body,
        out_shape=shapes,
        in_specs=[pl.BlockSpec(memory_space=pltpu.SMEM)] * len(scalars)
        + [pl.BlockSpec(memory_space=pltpu.VMEM)] * len(ins),
        out_specs=[pl.BlockSpec(memory_space=pltpu.VMEM)] * len(shapes),
        scratch_shapes=list(scratch),
        compiler_params=pltpu.CompilerParams(vmem_limit_bytes=VMEM_ROOM),
        cost_estimate=pl.CostEstimate(flops=flops, bytes_accessed=moved, transcendentals=0),
    )(*scalars, *ins)


class Spread:
    def __init__(self, blob, *earlier):
        self.half = blob.shape[0] // 2
        self.blob = after(blob, *earlier)
        self.near = self.plane(self.blob[None])

    def plane(self, part):
        from_x, from_y = swap(part, "x"), swap(part, "y")
        corner = (swap(from_x[:, : self.half], "y"), swap(from_y[:, self.half :], "x"))
        return from_x, from_y, *corner

    def along_z(self, *earlier):
        blob = after(self.blob, *earlier)
        self.moved = [shift(blob, "z", step) for step in (1, 2, 3)]

    def round_plane(self, *earlier):
        self.stack = after(jnp.stack(self.moved), *earlier)
        self.far = self.plane(self.stack)

    def whole(self, widths):
        rows = self.blob.shape[0]
        x, y, z = (lax.axis_index(axis) for axis in ("x", "y", "z"))
        starts = np.cumsum([0, *widths])

        def body(spot, *refs):
            here_x, here_y, here_z = spot[0], spot[1], spot[2]
            outs = refs[10:]
            for group in (0, 5):
                own, from_x, from_y, low_corner, high_corner = refs[group : group + 5]
                for number in range(own.shape[0]):
                    level = lax.rem(here_z - number + 3 if group else here_z + 4, 4)
                    for ref, at_x, at_y, first in (
                        (own, here_x, here_y, 0),
                        (from_x, 1 - here_x, here_y, 0),
                        (from_y, here_x, 1 - here_y, 0),
                        (low_corner, 1 - here_x, 1 - here_y, 0),
                        (high_corner, 1 - here_x, 1 - here_y, self.half),
                    ):
                        count = ref.shape[1]
                        for out, start, width in zip(outs, starts, widths):
                            out[at_x, level, at_y, first : first + count, :] = ref[
                                number, :, start : start + width
                            ]

        parts = (self.blob[None], *self.near, self.stack, *self.far)
        outs = [((2, 4, 2, rows, width), self.blob.dtype) for width in widths]
        wholes = vmem_call(body, outs, *parts, scalars=(jnp.stack([x, y, z]),))
        return [whole.reshape(2, 8 * rows, -1) for whole in wholes]


def spread_all(blobs, widths, arrived):
    sizes = tuple(lax.axis_size(axis) for axis in ("x", "z", "y"))
    if sizes != (2, 4, 2):
        wholes = [lax.all_gather(blob, ("x", "z", "y")) for blob in blobs]
        wholes = [whole.reshape(2, -1, whole.shape[-1]) for whole in wholes]
        pieces = [columns_of(whole, width) for whole, width in zip(wholes, widths)]
        return pieces, [wholes[0]] * 4
    first, second, third = (Spread(blob) for blob in blobs)
    first.along_z()
    second.along_z(*first.moved, arrived)
    first.round_plane()
    third.along_z(*first.far[:2])
    second.moved = [after(moved, *first.far[:2]) for moved in second.moved]
    second.round_plane(*first.far)
    third.moved = [after(moved, *second.far[:2]) for moved in third.moved]
    third.round_plane(*second.far)
    pieces = [group.whole(width) for group, width in zip((first, second, third), widths)]
    return pieces, [first.stack, first.far[0], first.far[2], third.stack]


def share(pieces, rows, patch=None, norms=None):
    x, y = lax.axis_index("x"), lax.axis_index("y")
    levels = lax.axis_size("z")
    half = levels // 2
    if (lax.axis_size("x"), levels, lax.axis_size("y")) != (2, 4, 2):
        cuts = []
        if patch is not None:
            cut = low(product("ld,lc->dc", *patch)).reshape(2 * levels, 2, rows, -1)
            cuts.append(cut.transpose(1, 0, 2, 3).reshape(2, 2 * levels * rows, -1))
        if norms is not None:
            cuts.append(norms.reshape(2, 2 * levels * rows, -1))
        cuts += [low(product("ld,xlc->xdc", left, right)) for left, right in pieces]
        return (jnp.concatenate(cuts, 2).reshape(4 * levels, rows, -1),)
    extra = []
    columns = 0
    if patch is not None:
        extra += [*patch]
        columns += patch[1].shape[1]
    if norms is not None:
        extra += [norms]
        columns += LANES
    first_column = columns
    for left, right in pieces:
        columns += right.shape[2]
    tallest = max([left.shape[1] for left, _ in pieces] + ([patch[0].shape[1]] if patch else []))
    widest = max([right.shape[2] for _, right in pieces] + ([patch[1].shape[1]] if patch else []))
    flops = sum(4 * left.shape[0] * left.shape[1] * right.shape[2] for left, right in pieces)

    def body(spot, *refs):
        ins, outs = refs[: len(extra) + 2 * len(pieces)], refs[len(extra) + 2 * len(pieces) : -1]
        total = refs[-1]
        cuts = ((outs[0], outs[1]), (outs[2], outs[3]), (outs[4], outs[5]), (outs[6], outs[7]))

        def put(far_x, far_y, level, window, value):
            target = cuts[2 * far_x + far_y][level // half]
            target[(level % half, *window)] = value

        used, column = 0, 0
        if patch is not None:
            left, right = ins[0], ins[1]
            width = right.shape[1]
            tall = left.shape[1]
            total[:tall, :width] = dot_tn(left[...], right[...])
            for far_x in (0, 1):
                for far_y in (0, 1):
                    at_x, at_y = spot[0] ^ far_x, spot[1] ^ far_y
                    for level in range(levels):
                        start = pl.multiple_of(((2 * level + at_y) * 2 + at_x) * rows, 8)
                        value = total[pl.ds(start, rows), :width].astype(NARROW_TYPE)
                        put(far_x, far_y, level, (slice(None), slice(0, width)), value)
            used, column = 2, width
        if norms is not None:
            source = ins[used]
            count = source.shape[2]
            for far_x in (0, 1):
                for far_y in (0, 1):
                    at_x, at_y = spot[0] ^ far_x, spot[1] ^ far_y
                    for level in range(levels):
                        window = (slice(None), slice(column, column + LANES))
                        put(far_x, far_y, level, window, source[at_x, 2 * level + at_y])
            used, column = used + 1, column + LANES
        for number, (_, right) in enumerate(pieces):
            left_ref, right_ref = ins[used + 2 * number], ins[used + 2 * number + 1]
            width = right.shape[2]
            tall = left_ref.shape[1]
            for far_x in (0, 1):
                at_x = spot[0] ^ far_x
                total[:tall, :width] = dot_tn(left_ref[...], right_ref[at_x])
                for far_y in (0, 1):
                    at_y = spot[1] ^ far_y
                    for level in range(levels):
                        start = pl.multiple_of((2 * level + at_y) * rows, 8)
                        value = total[pl.ds(start, rows), :width].astype(NARROW_TYPE)
                        put(far_x, far_y, level, (slice(None), slice(column, column + width)), value)
            column += width

    outs = [((half, rows, columns), NARROW_TYPE)] * 8
    flat = [array for piece in pieces for array in piece]
    return vmem_call(
        body,
        outs,
        *extra,
        *flat,
        scalars=(jnp.stack([x, y]),),
        scratch=[pltpu.VMEM((tallest, widest), FLOAT_TYPE)],
        flops=flops,
    )


def add(*terms):
    return sum(term.astype(FLOAT_TYPE) for term in terms)


class Collect:
    def __init__(self, *cuts):
        self.direct = None
        self.mark = ()
        if len(cuts) == 1:
            self.direct = lax.psum_scatter(cuts[0], ("x", "z", "y"), scatter_dimension=0)
            return
        self.own, self.by_y, self.by_x, corner = cuts[:2], cuts[2:4], cuts[4:6], cuts[6:]
        self.corner = (swap(corner[0], "x"), swap(corner[1], "y"))
        self.early = (swap(self.by_x[0], "x"), swap(self.by_y[1], "y"))

    def second(self, *earlier):
        if self.direct is not None:
            return ()
        from_x, from_y = lax.optimization_barrier((*self.corner, *earlier))[:2]
        to_y, to_x = low(add(self.by_y[0], from_x)), low(add(self.by_x[1], from_y))
        self.late = (swap(to_y, "y"), swap(to_x, "x"))
        return to_y, to_x

    def third(self, *earlier):
        if self.direct is not None:
            return ()
        x_low, y_high, y_low, x_high = lax.optimization_barrier((*self.early, *self.late, *earlier))[:4]
        column = jnp.concatenate(
            [low(add(self.own[0], x_low, y_low)), low(add(self.own[1], x_high, y_high))]
        )
        z = lax.axis_index("z")
        parts = [lax.dynamic_index_in_dim(column, (z + n) % 4, 0, keepdims=False) for n in range(4)]
        self.mine = parts[0]
        self.moved = [shift(part, "z", step) for step, part in enumerate(parts[1:], 1)]
        return tuple(parts)

    def total(self, *earlier):
        if self.direct is not None:
            return self.direct.astype(FLOAT_TYPE)
        return add(self.mine, *lax.optimization_barrier((*self.moved, *earlier))[:3])


def dot_nn(left, right):
    return jnp.dot(left, right, preferred_element_type=FLOAT_TYPE)


def dot_nt(left, right):
    return lax.dot_general(left, right, (((1,), (1,)), ((), ())), preferred_element_type=FLOAT_TYPE)


def dot_tn(left, right):
    return lax.dot_general(left, right, (((0,), (0,)), ((), ())), preferred_element_type=FLOAT_TYPE)


def angles_of(places, features):
    half_width = features // 2
    freqs = jnp.exp(-jnp.log(10000.0) * jnp.arange(half_width, dtype=FLOAT_TYPE) / half_width)
    angles = places.astype(FLOAT_TYPE)[:, None] * freqs[None, :]
    return jnp.concatenate([jnp.sin(angles), jnp.cos(angles)], axis=1)


def places_of(count, features):
    half_width = features // 2
    powers = np.arange(half_width, dtype=np.float32) / np.float32(half_width)
    freqs = np.exp(-np.log(np.float32(10000.0)) * powers)
    angles = np.arange(count, dtype=np.float32)[:, None] * freqs[None, :]
    return jnp.asarray(np.concatenate([np.sin(angles), np.cos(angles)], axis=1))


def norm_state(stream):
    centred = stream - jnp.mean(stream, -1, keepdims=True)
    inverse = lax.rsqrt(jnp.mean(centred * centred, -1, keepdims=True) + EPS_NORM)
    return centred * inverse, inverse


def norm_low(stream, gains, row):
    return low(norm_state(stream)[0] * gains[row : row + 1, :] + gains[row + 1 : row + 2, :])


def norm_back(upstream, stream, gains, row):
    scaled, inverse = norm_state(stream)
    weighted = upstream * gains[row : row + 1, :]
    input_grad = inverse * (
        weighted
        - jnp.mean(weighted, -1, keepdims=True)
        - scaled * jnp.mean(weighted * scaled, -1, keepdims=True)
    )
    sums = (jnp.sum(upstream * scaled, 0, keepdims=True), jnp.sum(upstream, 0, keepdims=True))
    return input_grad, sums


def head_masks(width, count):
    size = width // count
    lane = lax.broadcasted_iota(jnp.int32, (1, width), 1)
    return [
        jnp.where((lane >= head * size) & (lane < (head + 1) * size), 1.0, 0.0).astype(NARROW_TYPE)
        for head in range(count)
    ]


def attn_fwd(stream, gains, w_qkv, w_proj, head_count):
    length, features = stream.shape
    width = w_proj.shape[2]
    factor = (width // head_count) ** (-0.5)

    def body(stream, gains, w_qkv, w_proj, partial, triple, mixture, log_total):
        normed = norm_low(stream[...], gains, 0)
        masks = head_masks(width, head_count)
        output = None
        for part in (0, 1):
            projected = low(dot_nn(normed, w_qkv[part]))
            triple[part] = projected
            query, key, value = (projected[:, n * width : (n + 1) * width] for n in range(3))
            mixed = None
            for head, mask in enumerate(masks):
                scores = dot_nt(query * mask, key) * factor
                largest = jnp.max(scores, -1, keepdims=True)
                powers = jnp.exp(scores - largest)
                total = jnp.sum(powers, -1, keepdims=True)
                number = part * head_count + head
                log_total[:, number : number + 1] = largest + jnp.log(total)
                term = dot_nn(low(powers * (1.0 / total)), value * mask)
                mixed = term if mixed is None else mixed + term
            mixed = low(mixed)
            mixture[part] = mixed
            term = dot_nt(mixed, w_proj[part])
            output = term if output is None else output + term
        partial[...] = output

    outs = [
        ((length, features), FLOAT_TYPE),
        ((2, length, 3 * width), NARROW_TYPE),
        ((2, length, width), NARROW_TYPE),
        ((length, 2 * head_count), FLOAT_TYPE),
    ]
    flops = 16 * length * features * width + 8 * head_count * length * length * width
    return vmem_call(body, outs, stream, gains, w_qkv, w_proj, flops=flops)


def attn_back(stream_grad, own, other, middle, stream, kept, gains, w_qkv, w_proj, head_count):
    length, features = stream.shape
    width = w_proj.shape[2]
    factor = (width // head_count) ** (-0.5)
    triple, log_total = kept

    def body(
        stream_grad, own, other, middle, stream, triple, log_total, gains, w_qkv, w_proj,
        new_grad, grad_low, normed, triple_grad, partial, norm_grads,
    ):
        upstream = own[...].astype(FLOAT_TYPE) + other[...].astype(FLOAT_TYPE)
        input_grad, sums = norm_back(upstream, middle[...], gains, 2)
        norm_grads[0:1, :], norm_grads[1:2, :] = sums
        upstream = stream_grad[...] + input_grad
        new_grad[...] = upstream
        upstream = low(upstream)
        grad_low[...] = upstream
        normed[...] = norm_low(stream[...], gains, 0)
        masks = head_masks(width, head_count)
        output = None
        for part in (0, 1):
            projected = triple[part]
            query, key, value = (projected[:, n * width : (n + 1) * width] for n in range(3))
            mix_grad = low(dot_nn(upstream, w_proj[part]))
            query_grad = key_grad = value_grad = None
            for head, mask in enumerate(masks):
                query_part, mix_part = query * mask, mix_grad * mask
                number = part * head_count + head
                scores = dot_nt(query_part, key) * factor
                attend = jnp.exp(scores - log_total[:, number : number + 1])
                attend_grad = dot_nt(mix_part, value)
                inner = jnp.sum(attend * attend_grad, -1, keepdims=True)
                score_grad = low(attend * (attend_grad - inner))
                terms = (
                    dot_nn(score_grad, key * mask),
                    dot_tn(score_grad, query_part),
                    dot_tn(low(attend), mix_part),
                )
                if head == 0:
                    query_grad, key_grad, value_grad = terms
                else:
                    query_grad, key_grad, value_grad = (
                        query_grad + terms[0],
                        key_grad + terms[1],
                        value_grad + terms[2],
                    )
            grads = (low(query_grad * factor), low(key_grad * factor), low(value_grad))
            for number, grad in enumerate(grads):
                triple_grad[part, :, number * width : (number + 1) * width] = grad
            term = dot_nt(triple_grad[part], w_qkv[part])
            output = term if output is None else output + term
        partial[...] = low(output)

    outs = [
        ((length, features), FLOAT_TYPE),
        ((length, features), NARROW_TYPE),
        ((length, features), NARROW_TYPE),
        ((2, length, 3 * width), NARROW_TYPE),
        ((length, features), NARROW_TYPE),
        ((2, features), FLOAT_TYPE),
    ]
    flops = 16 * length * features * width + 20 * head_count * length * length * width
    return vmem_call(
        body, outs, stream_grad, own, other, middle, stream, triple, log_total, gains, w_qkv, w_proj,
        flops=flops,
    )


def mlp_fwd(stream, own, other, gains, w_up, w_down):
    length, features = stream.shape
    width = w_up.shape[2]

    def body(stream, own, other, gains, w_up, w_down, middle, partial):
        values = stream[...] + (own[...] + other[...])
        middle[...] = values
        normed = norm_low(values, gains, 2)
        output = None
        for part in (0, 1):
            upward = dot_nn(normed, w_up[part])
            hidden = low(0.5 * upward * (1.0 + lax.erf(upward * SQRT_HALF)))
            term = dot_nt(hidden, w_down[part])
            output = term if output is None else output + term
        partial[...] = output

    outs = [((length, features), FLOAT_TYPE)] * 2
    flops = 8 * length * features * width
    return vmem_call(body, outs, stream, own, other, gains, w_up, w_down, flops=flops)


def mlp_back(upstream, last, middle, gains, w_up, w_down):
    length, features = last.shape
    width = w_up.shape[2]
    count = len(upstream)

    def body(*refs):
        last, middle, gains, w_up, w_down = refs[count : count + 5]
        new_grad, grad_low, normed_low, hidden_low, upward_low, partial, norm_grads = refs[count + 5 :]
        arrived = add(*(ref[...] for ref in refs[:count]))
        input_grad, sums = norm_back(arrived, last[...], gains, 4)
        norm_grads[0:1, :], norm_grads[1:2, :] = sums
        new_grad[...] = input_grad
        grad = low(input_grad)
        grad_low[...] = grad
        normed = norm_low(middle[...], gains, 2)
        normed_low[...] = normed
        output = None
        for part in (0, 1):
            upward = dot_nn(normed, w_up[part])
            below = 0.5 * (1.0 + lax.erf(upward * SQRT_HALF))
            hidden_low[part] = low(upward * below)
            slope = below + upward * (jnp.exp(-0.5 * upward * upward) * DENSITY)
            upward_grad = low(dot_nn(grad, w_down[part]) * slope)
            upward_low[part] = upward_grad
            term = dot_nt(upward_grad, w_up[part])
            output = term if output is None else output + term
        partial[...] = low(output)

    outs = [
        ((length, features), FLOAT_TYPE),
        ((length, features), NARROW_TYPE),
        ((length, features), NARROW_TYPE),
        ((2, length, width), NARROW_TYPE),
        ((2, length, width), NARROW_TYPE),
        ((length, features), NARROW_TYPE),
        ((2, features), FLOAT_TYPE),
    ]
    flops = 12 * length * features * width
    return vmem_call(body, outs, *upstream, last, middle, gains, w_up, w_down, flops=flops)


def between(middle, own, other, gains, embed, chosen, hidden_row, mask_token, places):
    length, features = middle.shape
    tokens, width = places.shape

    def body(middle, own, other, gains, embed, chosen, hidden_row, mask_token, places, last, normed_low, stream):
        values = middle[...] + (own[...] + other[...])
        last[...] = values
        normed = norm_low(values, gains, 4)
        normed_low[...] = normed
        embedded = dot_nn(normed, embed[...])
        high = low(embedded)
        rest = low(embedded - high.astype(FLOAT_TYPE))
        placed = dot_tn(chosen[...], high) + dot_tn(chosen[...], rest)
        stream[...] = placed + hidden_row[...] * mask_token[...] + places[...]

    outs = [
        ((length, features), FLOAT_TYPE),
        ((length, features), NARROW_TYPE),
        ((tokens, width), FLOAT_TYPE),
    ]
    return vmem_call(body, outs, middle, own, other, gains, embed, chosen, hidden_row, mask_token, places)


def head_loss(middle, own, other, gains, w_head, goal, mask):
    length, features = middle.shape
    width = w_head.shape[2]

    def body(middle, own, other, gains, w_head, goal, mask, last, normed_low, pred_low, partial, loss):
        values = middle[...] + (own[...] + other[...])
        last[...] = values
        normed = norm_low(values, gains, 4)
        normed_low[...] = normed
        weights = mask[...]
        output, lost = None, None
        for part in (0, 1):
            errors = dot_nn(normed, w_head[part]) - goal[part]
            weighted = weights * errors
            square = jnp.sum(weighted * errors, 0, keepdims=True)
            pred_grad = low(weighted * 2.0)
            pred_low[part] = pred_grad
            term = dot_nt(pred_grad, w_head[part])
            output = term if output is None else output + term
            lost = square if lost is None else lost + square
        partial[...] = low(output)
        loss[...] = lost

    outs = [
        ((length, features), FLOAT_TYPE),
        ((length, features), NARROW_TYPE),
        ((2, length, width), NARROW_TYPE),
        ((length, features), NARROW_TYPE),
        ((1, width), FLOAT_TYPE),
    ]
    flops = 8 * length * features * width
    return vmem_call(body, outs, middle, own, other, gains, w_head, goal, mask, flops=flops)


def decoder_end(stream_grad, own, other, stream, gains, chosen, hidden_row, embed, place):
    length, features = stream.shape
    vis_count = chosen.shape[0]
    quarter = features // 4

    def body(
        place, stream_grad, own, other, stream, gains, chosen, hidden_row, embed,
        embed_mine, normed_grad, mask_grad, norm_grads,
    ):
        upstream = own[...].astype(FLOAT_TYPE) + other[...].astype(FLOAT_TYPE)
        input_grad, sums = norm_back(upstream, stream[...], gains, 0)
        norm_grads[0:1, :], norm_grads[1:2, :] = sums
        grad = stream_grad[...] + input_grad
        mask_grad[...] = jnp.sum(grad * hidden_row[...], 0, keepdims=True)
        embedded = low(dot_nn(chosen[...], low(grad)))
        for part in (0, 1):
            start = 2 * part * quarter
            cuts = [embedded[:, start + n * quarter : start + (n + 1) * quarter] for n in (0, 1)]
            embed_mine[part] = jnp.where(place[0] == 0, *cuts)
        normed_grad[...] = dot_nt(embedded, embed[...])

    outs = [
        ((2, vis_count, quarter), NARROW_TYPE),
        ((vis_count, embed.shape[0]), FLOAT_TYPE),
        ((1, features), FLOAT_TYPE),
        ((2, features), FLOAT_TYPE),
    ]
    return vmem_call(
        body, outs, stream_grad, own, other, stream, gains, chosen, hidden_row, embed, scalars=(place,)
    )


def encoder_end(stream_grad, own, other, stream, gains, place):
    length, features = stream.shape
    half = features // 2

    def body(place, stream_grad, own, other, stream, gains, grad_mine, norm_grads):
        upstream = own[...].astype(FLOAT_TYPE) + other[...].astype(FLOAT_TYPE)
        input_grad, sums = norm_back(upstream, stream[...], gains, 0)
        norm_grads[0:1, :], norm_grads[1:2, :] = sums
        grad = low(stream_grad[...] + input_grad)
        grad_mine[...] = jnp.where(place[0] == 0, grad[:, :half], grad[:, half:])

    outs = [((length, half), NARROW_TYPE), ((2, features), FLOAT_TYPE)]
    return vmem_call(body, outs, stream_grad, own, other, stream, gains, scalars=(place,))


def adam_update(weight, moment, second, gradient, step_rate, decay_rate):
    moment = BETA_ONE * moment + (1.0 - BETA_ONE) * gradient
    second = BETA_TWO * second + (1.0 - BETA_TWO) * gradient * gradient
    fixed_one = moment / (1.0 - BETA_ONE**STEP)
    fixed_two = second / (1.0 - BETA_TWO**STEP)
    weight = weight - step_rate * (
        fixed_one / (jnp.sqrt(fixed_two) + ADAM_EPS) + decay_rate * weight
    )
    return [weight, moment, second]


def adam_all(scale, masters, moments, seconds, grads):
    orders = ((1, 0, 2), None, (1, 0, 2), (0, 2, 1))
    shapes = [array.shape for array in masters]

    def view(array, number):
        if number < 4:
            return array if orders[number] is None else array.transpose(orders[number])
        return array.reshape(-1, LANES) if array.ndim == 1 else array

    def unview(array, number):
        if number < 4 and orders[number] is not None:
            return array.transpose(np.argsort(orders[number]))
        return array.reshape(shapes[number])

    triples = [
        [view(array, number) for array in (masters[number], moments[number], seconds[number])]
        for number in range(8)
    ]
    grads = [view(grad, 7) if number == 7 else grad for number, grad in enumerate(grads)]

    def body(scale, *refs):
        arrays, gradients, outs = refs[:24], refs[24:32], refs[32:]
        factor = scale[0]
        for number in range(8):
            ins, news = arrays[3 * number : 3 * number + 3], outs[3 * number : 3 * number + 3]
            step_rate = LR_NORM if number == 7 else LR_MATRIX
            decay_rate = 0.0 if number == 7 else DECAY
            blocks = ins[0].shape[0] if number < 4 else 1
            for block in range(blocks):
                if number < 4:
                    width = ins[0].shape[1] if number == 1 else ins[0].shape[2]
                    grad = gradients[number][:, block * width : (block + 1) * width]
                    grad = grad.T if number == 1 else grad
                    values = [ref[block] for ref in ins]
                else:
                    grad = gradients[number][...].astype(FLOAT_TYPE)
                    values = [ref[...] for ref in ins]
                results = adam_update(*values, grad * factor, step_rate, decay_rate)
                for ref, result in zip(news, results):
                    if number < 4:
                        ref[block] = result
                    else:
                        ref[...] = result

    flat = [array for triple in triples for array in triple]
    outs = [(array.shape, FLOAT_TYPE) for array in flat]
    results = vmem_call(body, outs, *flat, *grads, scalars=(scale[None],))
    return [unview(result, index // 3) for index, result in enumerate(results)]


def from_all(piece, x, c):
    there = [piece, swap(piece, "c"), swap(piece, "x"), lax.ppermute(piece, ("x", "c"), ACROSS)]
    ordered = []
    for number in range(4):
        at_x, at_c = x ^ (number // 2), c ^ (number % 2)
        ordered.append(
            jnp.where(
                at_x == 0,
                jnp.where(at_c == 0, there[0], there[1]),
                jnp.where(at_c == 0, there[2], there[3]),
            )
        )
    return ordered


def both(piece, axis, place, dimension):
    other = swap(piece, axis)
    return jnp.where(
        place == 0,
        jnp.concatenate([piece, other], dimension),
        jnp.concatenate([other, piece], dimension),
    )


def halves_of(array, place):
    half = array.shape[1] // 2
    return jnp.where(place == 0, array[:, :half], array[:, half:])


def one_hot(visible_row, tokens):
    return visible_row[:, None] == jnp.arange(tokens)[None, :]


def pick(array, index, axis=0):
    return lax.dynamic_index_in_dim(array, index, axis, keepdims=False)


def columns_of(blob, widths):
    pieces, start = [], 0
    for width in widths:
        pieces.append(blob[..., start : start + width])
        start += width
    return pieces


def on_device(
    pixels,
    visible,
    valid,
    row_dest,
    encoder_in,
    encoder_in_moment,
    encoder_in_second,
    encoder_out,
    encoder_out_moment,
    encoder_out_second,
    decoder_in,
    decoder_in_moment,
    decoder_in_second,
    decoder_out,
    decoder_out_moment,
    decoder_out_second,
    patch_embed,
    patch_embed_moment,
    patch_embed_second,
    decoder_embed,
    decoder_embed_moment,
    decoder_embed_second,
    pixel_head,
    pixel_head_moment,
    pixel_head_second,
    norm_params,
    norm_params_moment,
    norm_params_second,
):
    masters = [
        encoder_in,
        encoder_out,
        decoder_in,
        decoder_out,
        patch_embed,
        decoder_embed,
        pixel_head,
        norm_params,
    ]
    moments = [
        encoder_in_moment,
        encoder_out_moment,
        decoder_in_moment,
        decoder_out_moment,
        patch_embed_moment,
        decoder_embed_moment,
        pixel_head_moment,
        norm_params_moment,
    ]
    seconds = [
        encoder_in_second,
        encoder_out_second,
        decoder_in_second,
        decoder_out_second,
        patch_embed_second,
        decoder_embed_second,
        pixel_head_second,
        norm_params_second,
    ]
    x, c = lax.axis_index("x"), lax.axis_index("c")
    data_size = lax.axis_size("z") * lax.axis_size("y")
    slot_total, tokens, pix_width = pixels.shape
    vis_count = visible.shape[1]
    patch_positions = valid.shape[2]
    rows_enc, _, part_enc = encoder_in.shape
    rows_dec, _, part_dec = decoder_in.shape
    width_enc, width_dec = patch_embed.shape[1], decoder_embed.shape[1]
    enc_heads = HEADS_ENC // 4
    dec_heads = HEADS_DEC // 4

    patch_rows = patch_embed.shape[0] // 2
    half_enc, quarter_dec = width_enc // 2, width_dec // 4
    patch_piece = lax.dynamic_slice(
        low(patch_embed), (x * patch_rows, c * half_enc), (patch_rows, half_enc)
    )
    embed_piece = lax.dynamic_slice(
        low(decoder_embed), (0, (2 * x + c) * quarter_dec), (rows_enc, quarter_dec)
    )
    norm_share, norm_room = norm_params.shape[0], rows_enc * LANES
    norm_piece = jnp.pad(low(norm_params), (0, norm_room - norm_share)).reshape(rows_enc, LANES)
    enc_in_low = low(encoder_in).reshape(rows_enc, -1)
    enc_out_low = low(encoder_out).transpose(2, 0, 1).reshape(rows_enc, -1)
    dec_in_low = low(decoder_in).reshape(rows_dec, -1)
    dec_out_low = low(decoder_out).transpose(2, 0, 1).reshape(rows_dec, -1)
    head_low = low(pixel_head)
    first_blob = jnp.concatenate(
        [patch_piece, norm_piece, enc_in_low[:, : 3 * part_enc], enc_out_low[:, :part_enc]], 1
    )
    second_blob = jnp.concatenate(
        [enc_in_low[:, 3 * part_enc :], enc_out_low[:, part_enc:], embed_piece], 1
    )
    third_blob = jnp.concatenate([dec_in_low, dec_out_low, head_low], 1)
    widths = (
        (half_enc, LANES, 3 * part_enc, part_enc),
        (4 * part_enc, 4 * part_enc, quarter_dec),
        (3 * part_dec, 4 * part_dec, part_dec, 4 * part_dec, head_low.shape[1]),
    )

    buf_rows = data_size * -(-(slot_total * vis_count) // data_size)
    alive = row_dest[:, 0] < buf_rows
    use_own = pick(alive, x)
    half_step = lax.axis_size("z") // 2

    def shown_of(visible_row):
        return jnp.any(one_hot(visible_row, tokens), axis=0).astype(FLOAT_TYPE)

    start = after(x, first_blob)
    away = slot_total - 1 - start
    own_slot, away_slot = pick(pixels, start), pick(pixels, away)

    def seen_of(slot, rows):
        return low(product("vt,tp->vp", low(one_hot(pick(visible, slot), tokens)), rows))

    visible_row = jnp.where(use_own, pick(visible, start), shift(pick(visible, away), "z", half_step))
    seen_away = shift(halves_of(seen_of(away, away_slot), c), "z", half_step)

    (first_all, second_all, third_all), marks = spread_all(
        (first_blob, second_blob, third_blob), widths, seen_away
    )

    patch_all, norm_all, enc_qkv, enc_proj = first_all
    enc_up, enc_down, embed_all = second_all
    dec_qkv, dec_up, dec_proj, dec_down, head_all = third_all
    patch_all = patch_all.reshape(2, data_size, patch_rows, half_enc).transpose(1, 0, 2, 3)
    patch_all = patch_all.reshape(pix_width, half_enc)
    embed_other = swap(embed_all)
    embed_even = jnp.where(c == 0, embed_all, embed_other)
    embed_odd = jnp.where(c == 0, embed_other, embed_all)
    full_embed = jnp.concatenate([embed_even[0], embed_odd[0], embed_even[1], embed_odd[1]], 1)
    norm_full = norm_all[0].reshape(data_size, norm_room)[:, :norm_share].reshape(-1)
    norm_full = norm_full.astype(FLOAT_TYPE)
    enc_gains = norm_full[: 6 * width_enc].reshape(6, width_enc)
    dec_gains = norm_full[6 * width_enc : 6 * width_enc + 6 * width_dec].reshape(6, width_dec)
    mask_token = norm_full[6 * width_enc + 6 * width_dec : 6 * width_enc + 7 * width_dec]

    seen_rows = jnp.where(
        use_own, seen_of(after(start, marks[0]), own_slot), both(seen_away, "c", c, 1)
    )
    chosen = low(one_hot(visible_row, tokens))
    hidden_row = (1.0 - shown_of(visible_row))[:, None]

    visible_late = after(visible, marks[2])
    counted = jnp.stack([1.0 - shown_of(visible_late[slot]) for slot in range(slot_total)])
    counted = counted * alive.astype(FLOAT_TYPE)[:, None]
    valid_count = jnp.sum(counted[:, :, None] * valid.astype(FLOAT_TYPE))
    valid_count = valid_count * (pix_width // patch_positions)

    def pixels_of(slot, rows):
        place = after(c, marks[1])
        half = pix_width // 2
        cols = [halves_of(rows[:, first : first + half], place) for first in (0, half)]
        return jnp.concatenate(cols + [low(pick(valid, slot))], 1)

    own_pack, away_pack = pixels_of(start, own_slot), pixels_of(away, away_slot)
    pack_moved = shift(after(away_pack, marks[3]), "z", half_step)

    enc_stream = both(product("lp,pd->ld", seen_rows, patch_all), "c", c, 1)
    enc_stream = enc_stream + angles_of(visible_row, width_enc)
    partial, enc_triple, enc_mixture, enc_log = attn_fwd(
        enc_stream, enc_gains, enc_qkv, enc_proj, enc_heads
    )
    enc_middle, partial = mlp_fwd(enc_stream, partial, swap(partial), enc_gains, enc_up, enc_down)
    enc_last, enc_normed, dec_stream = between(
        enc_middle,
        partial,
        swap(partial),
        enc_gains,
        full_embed,
        chosen,
        hidden_row,
        mask_token[None],
        places_of(tokens, width_dec),
    )

    partial, dec_triple, dec_mixture, dec_log = attn_fwd(
        dec_stream, dec_gains, dec_qkv, dec_proj, dec_heads
    )
    dec_middle, partial = mlp_fwd(dec_stream, partial, swap(partial), dec_gains, dec_up, dec_down)

    pixel_pack = jnp.where(use_own, own_pack, after(pack_moved, dec_stream))
    pixel_cols = pixel_pack[:, : pix_width // 2].astype(FLOAT_TYPE)
    valid_cols = pixel_pack[:, pix_width // 2 :].astype(FLOAT_TYPE)
    half_mean = jnp.mean(pixel_cols, -1, keepdims=True)
    half_square = jnp.sum((pixel_cols - half_mean) ** 2, -1, keepdims=True)
    half_both = jnp.concatenate([half_mean, half_square], 1)
    other_both = swap(half_both)
    mean = 0.5 * (half_both[:, :1] + other_both[:, :1])
    gap = half_both[:, :1] - other_both[:, :1]
    variance = (half_both[:, 1:] + other_both[:, 1:]) / pix_width + 0.25 * gap * gap
    target = (pixel_cols - mean) * lax.rsqrt(variance + EPS_PIX)
    half_positions = patch_positions // 2
    front = jnp.where(c == 0, valid_cols[:, :half_positions], valid_cols[:, half_positions:])
    back = jnp.where(c == 0, valid_cols[:, half_positions:], valid_cols[:, :half_positions])
    part_mask = jnp.concatenate([front, back, front], 1) * hidden_row
    goal = jnp.stack([target[:, : pix_width // 4], target[:, pix_width // 4 :]])
    dec_last, dec_normed, pred_low, partial, loss_part = head_loss(
        dec_middle,
        partial,
        swap(partial),
        dec_gains,
        head_all,
        goal,
        part_mask,
    )
    loss_part = jnp.sum(loss_part)

    stream_grad, grad_low, normed_low, hidden_low, upward_low, partial, dec_norms_three = mlp_back(
        (partial, swap(partial)), dec_last, dec_middle, dec_gains, dec_up, dec_down
    )
    dec_tail = Collect(
        *share(
            [(normed_low, upward_low), (grad_low, hidden_low), (dec_normed, pred_low)], rows_dec
        )
    )
    stream_grad, grad_low, normed_low, triple_grad, partial, dec_norms_two = attn_back(
        stream_grad,
        partial,
        swap(partial),
        dec_middle,
        dec_stream,
        (dec_triple, dec_log),
        dec_gains,
        dec_qkv,
        dec_proj,
        dec_heads,
    )
    normed_low = after(normed_low, *dec_tail.second(triple_grad))
    dec_attn = Collect(*share([(normed_low, triple_grad), (grad_low, dec_mixture)], rows_dec))
    embed_mine, normed_grad, mask_grad, dec_norms_one = decoder_end(
        stream_grad,
        partial,
        swap(partial),
        dec_stream,
        dec_gains,
        chosen,
        hidden_row,
        full_embed,
        c[None],
    )

    stream_grad, grad_low, normed_low, hidden_low, upward_low, partial, enc_norms_three = mlp_back(
        (after(normed_grad, *dec_attn.second(), *dec_tail.third(normed_grad)),), enc_last, enc_middle, enc_gains, enc_up, enc_down
    )
    enc_tail = Collect(
        *share([(normed_low, upward_low), (grad_low, hidden_low), (enc_normed, embed_mine)], rows_enc)
    )
    other_partial = after(swap(partial), *dec_attn.third(*enc_tail.mark))
    stream_grad, grad_low, normed_low, triple_grad, partial, enc_norms_two = attn_back(
        stream_grad,
        partial,
        other_partial,
        enc_middle,
        enc_stream,
        (enc_triple, enc_log),
        enc_gains,
        enc_qkv,
        enc_proj,
        enc_heads,
    )
    other_partial = after(swap(partial), *enc_tail.second(partial))
    patch_right, enc_norms_one = encoder_end(
        stream_grad, partial, other_partial, enc_stream, enc_gains, c[None]
    )
    norm_pieces = jnp.concatenate(
        [
            grads.reshape(-1)
            for grads in (
                enc_norms_one,
                enc_norms_two,
                enc_norms_three,
                dec_norms_one,
                dec_norms_two,
                dec_norms_three,
                mask_grad,
            )
        ]
    )
    norm_total = norm_params.shape[0] * data_size
    norm_grad = jnp.concatenate(
        [norm_pieces, jnp.zeros((norm_total - norm_pieces.shape[0],), FLOAT_TYPE)]
    )
    norm_half = norm_share // 2
    norm_grads = low(norm_grad).reshape(data_size, 2, norm_half).transpose(1, 0, 2)
    norm_grads = jnp.pad(norm_grads, ((0, 0), (0, 0), (0, norm_room - norm_half)))
    enc_attn = Collect(
        *share(
            [(normed_low, triple_grad), (grad_low, enc_mixture)],
            rows_enc,
            (seen_rows, patch_right),
            norm_grads.reshape(2, data_size, rows_enc, LANES),
        )
    )

    enc_tail_sent = enc_tail.third(*enc_attn.second())
    dec_tail_sum, dec_attn_sum = dec_tail.total(*enc_tail_sent), dec_attn.total(*enc_tail_sent)
    enc_tail_sum = enc_tail.total(*enc_attn.third())
    enc_attn_sum = enc_attn.total()
    patch_sum, norm_sum, qkv_sum, proj_sum = columns_of(enc_attn_sum, widths[0])
    up_sum, down_sum, embed_sum = columns_of(enc_tail_sum, widths[1])
    dec_qkv_sum, dec_proj_sum = columns_of(dec_attn_sum, (3 * part_dec, part_dec))
    dec_up_sum, dec_down_sum, head_sum = columns_of(
        dec_tail_sum, (4 * part_dec, 4 * part_dec, head_low.shape[1])
    )
    norm_sum = low(norm_sum.reshape(-1)[:norm_half])
    patch_sum, embed_sum = low(patch_sum), low(embed_sum)
    shared_square = sum(
        jnp.sum(jnp.square(piece.astype(FLOAT_TYPE))) for piece in (patch_sum, embed_sum)
    ) + 0.5 * jnp.sum(jnp.square(norm_sum.astype(FLOAT_TYPE)))
    own_square = sum(
        jnp.sum(jnp.square(piece))
        for piece in (qkv_sum, proj_sum, up_sum, down_sum, dec_attn_sum, dec_tail_sum)
    )
    patch_all = from_all(patch_sum, x, c)
    embed_all = from_all(embed_sum, x, c)
    norm_sum = both(norm_sum, "x", x, 0)
    patch_full = jnp.concatenate([jnp.concatenate([patch_all[n], patch_all[n + 1]], 1) for n in (0, 2)])
    embed_full = jnp.concatenate(embed_all, 1)
    totals = jnp.stack([loss_part, own_square + shared_square, valid_count * 0.25])
    totals = total_over(totals, ("c", "x", "y"))
    totals, patch_full, embed_full, norm_sum = lax.optimization_barrier(
        (totals, patch_full, embed_full, norm_sum)
    )
    totals = total_over(totals, ("z",))
    loss_sum, valid_count = totals[0], totals[2]
    grad_norm = jnp.sqrt(totals[1]) / valid_count
    scale = CLIP / jnp.maximum(grad_norm, CLIP) / valid_count
    grads = (
        jnp.concatenate([qkv_sum, up_sum], 1),
        jnp.concatenate([proj_sum, down_sum], 1),
        jnp.concatenate([dec_qkv_sum, dec_up_sum], 1),
        jnp.concatenate([dec_proj_sum, dec_down_sum], 1),
        patch_full,
        embed_full,
        head_sum,
        norm_sum,
    )
    updated = adam_all(scale, masters, moments, seconds, grads)
    return (loss_sum, valid_count, grad_norm, *updated)


def solution(mesh):
    data, model = mesh.shape["dp"], mesh.shape["mp"]
    inner = Mesh(mesh.devices.reshape(data // 2, 2, model // 2, 2), ("z", "y", "x", "c"))
    data_axes, model_axes = ("z", "y"), ("x", "c")
    rows = P(data_axes)
    into = P(data_axes, None, model_axes)
    out_of = P(None, model_axes, data_axes)
    head = P(data_axes, model_axes)
    weights = (into, out_of, into, out_of, rows, rows, head, rows)
    triples = tuple(spec for spec in weights for _ in range(3))
    return jax.shard_map(
        on_device,
        mesh=inner,
        in_specs=(rows, rows, rows, rows) + triples,
        out_specs=(P(), P(), P()) + triples,
        check_vma=False,
    )
```

time: 593 us -> 521 us (0.88)
  Pallas kernels: 5.81 us -> 127 us
  matrix products: 86.9 us -> 2.2 us
  local copies, waits for them, and re-layouts: 106 us -> 50.8 us
  other arithmetic: 88.5 us -> 54.4 us
  waiting for transfers between devices: 188 us -> 161 us
  starting transfers between devices: 94.2 us -> 105 us
    pallas_call x6 -> x20, Pallas kernels: 5.81 us -> 127 us  [vmem_call(): pl.pallas_call(body, out_shape=shapes, in_specs=[pl.BlockSpec(memory_spac...]
    dot_general x57 -> x3, matrix products: 86.9 us -> 2.2 us  [product(): return jnp.einsum(spec, left, right, preferred_element_type=FLOAT_TYPE)]
    ppermute x46 -> x66, waiting for transfers between devices: 99.8 us -> 74 us  [swap(): return lax.ppermute(values, axis, SWAP)]
    concatenate x8 -> x1, local copies, waits for them, and re-layouts: 24.7 us -> 0.79 us  [on_device(): jnp.concatenate([patch_piece, norm_piece, enc_in_low[:, :3 * part_enc], e...]
    ppermute x46 -> x66, starting transfers between devices: 39.4 us -> 57.7 us  [swap(): return lax.ppermute(values, axis, SWAP)]
    unnamed x335 -> x181, local copies, waits for them, and re-layouts: 29.9 us -> 16.8 us
    reduce_sum x20 -> x1, other arithmetic: 12.5 us -> 1.28 us  [on_device(): loss_part = jnp.sum(loss_part)]
    sub x9 -> x1, other arithmetic: 10 us -> 0.01 us  [on_device(): hidden_row = (1.0 - shown_of(visible_row))[:, None]]
  transfers between devices with their start and end apart: 78 -> 97, of which waited for: 39 -> 40; matrix products, arithmetic and copies ran while one was open for 39% -> 16% of each run, Pallas kernels for 1% -> 16%
where the time goes in v3:
time: 521 us; the launch traced here: 512 us
  waiting for transfers between devices  161 us (31%)
  Pallas kernels  127 us (24%)
  starting transfers between devices  105 us (20%)
  other arithmetic  54.4 us (10%)
  local copies, waits for them, and re-layouts  50.8 us (10%)
  between operations  12.3 us (2%)
    pallas_call x20, Pallas kernels, vmem_call(): pl.pallas_call(body, out_shape=shapes, in_specs=[pl.BlockSpec(memory_spac...  127 us
    ppermute x66, waiting for transfers between devices, swap(): return lax.ppermute(values, axis, SWAP)  74 us
    ppermute x24, waiting for transfers between devices, shift(): lax.ppermute(values, axis, [(i, (i + step) % size) for i in range(size)])  72.8 us
    ppermute x66, starting transfers between devices, swap(): return lax.ppermute(values, axis, SWAP)  57.7 us
    ppermute x24, starting transfers between devices, shift(): lax.ppermute(values, axis, [(i, (i + step) % size) for i in range(size)])  43.7 us
    unnamed x181, local copies, waits for them, and re-layouts  16.8 us
    ppermute x5, waiting for transfers between devices, total_over(): lax.ppermute(values, axis, [(i, i ^ step) for i in range(size)])  13.4 us
    convert_element_type x22, other arithmetic, low(): return values.astype(NARROW_TYPE)  11.8 us
  transfers between devices with their start and end apart: 97, of which 40 were waited for; matrix products, arithmetic and copies ran while one was open for 16% of the time, Pallas kernels for 16%

profile of v3, /device:TPU:0, one launch (start us, length us, event | category | flops | bytes accessed | tf_op | source)
XLA Modules:
  0.0 512.3 jit_solution(2461138370684147235)
XLA Ops:
  22.2 9.9 %constant_dynamic-slice_fusion.5 = (bf16[1,588,1536]{2,0,1:T(2,128)(2,1)S(1)}, bf16[1,588,1536]{2,0,1:T(2,128)(2,1)S(1)}) fusion(bf16[4,588,1536]{2,0,1:T(4,128)(2,1)} %param.29, s32[]{:T(128)S(6)} %select_n.303, s32[]{:T(128)S(6)} %select_n.305), kind=kLoop, calls=%fused_computation.193 | loop fusion | bytes 7225352 | tf_op jit(solution)/shard_map/jit(dynamic_index_in_dim)/dynamic_slice | solution.py:722
  52.7 7.8 %collective-permute-done.3 = bf16[147,768]{1,0:T(8,128)(2,1)S(1)} collective-permute-done((bf16[147,768]{1,0:T(8,128)(2,1)S(1)}, bf16[147,768]{1,0:T(8,128)(2,1)S(1)}, u32[]{:S(2)}, u32[]{:S(2)}) %collective-permute-start.3) | collective-permute-done | bytes 225824 | tf_op jit(solution)/shard_map/ppermute | solution.py:60
  71.3 16.2 %collective-permute-done.21 = bf16[96,1664]{1,0:T(8,128)(2,1)S(1)} collective-permute-done((bf16[96,1664]{1,0:T(8,128)(2,1)S(1)}, bf16[96,1664]{1,0:T(8,128)(2,1)S(1)}, u32[]{:S(2)}, u32[]{:S(2)}) %collective-permute-start.21) | collective-permute-done | bytes 319520 | tf_op jit(solution)/shard_map/ppermute | solution.py:60
  103.7 9.6 %collective-permute-done.24.refs_7_ = bf16[3,96,1664]{2,1,0:T(8,128)(2,1)} collective-permute-done((bf16[3,96,1664]{2,1,0:T(8,128)(2,1)S(1)}, bf16[3,96,1664]{2,1,0:T(8,128)(2,1)}, u32[]{:S(2)}, u32[]{:S(2)}) %collective-permute-start.24) | collective-permute-done | bytes 958496 | tf_op jit(solution)/shard_map/ppermute | solution.py:45
  171.7 10.8 %shard_map.490 = (f32[588,512]{1,0:T(8,128)}, bf16[2,588,384]{2,1,0:T(8,128)(2,1)}, bf16[2,588,128]{2,1,0:T(8,128)(2,1)}, f32[588,8]{1,0:T(8,128)}) custom-call(f32[588,512]{1,0:T(8,128)} %get-tuple-element.224.stream, f32[6,512]{1,0:T(8,128)} %slice_convert_fusion.3.gains.refs_4_, bf16[2,512,384]{2,1,0:T(8,128)(2,1)} %bitcast.234, ...), custom_call_target="tpu_custom_call" | custom-call | flops 2032730112 | bytes 4692352 | tf_op jit(solution)/shard_map/pallas_call | solution.py:83
  182.5 15.3 %collective-permute-done.42 = bf16[588,1024]{1,0:T(8,128)(2,1)} collective-permute-done((bf16[588,1024]{1,0:T(8,128)(2,1)}, bf16[588,1024]{1,0:T(8,128)(2,1)}, u32[]{:S(2)}, u32[]{:S(2)}) %collective-permute-start.42) | collective-permute-done | bytes 1204256 | tf_op jit(solution)/shard_map/ppermute | solution.py:60
  200.6 5.5 %shard_map.491 = (f32[588,512]{1,0:T(8,128)}, f32[588,512]{1,0:T(8,128)}) custom-call(f32[588,512]{1,0:T(8,128)} %get-tuple-element.224.stream, f32[588,512]{1,0:T(8,128)} %get-tuple-element.232.own, f32[588,512]{1,0:T(8,128)} %copy-done.16, f32[6,512]{1,0:T(8,128)} %slice_convert_fusion.3.gains.refs_4_, bf16[2,512,512]{2,1,0:T(8,128)(2,1)} %bitcast.191, ...), custom_call_target="tpu_custom_call" | custom-call | flops 1233125376 | bytes 8130560 | tf_op jit(solution)/shard_map/pallas_call | solution.py:83
  210.6 5.7 %shard_map.492 = (f32[588,512]{1,0:T(8,128)}, bf16[588,512]{1,0:T(8,128)(2,1)}, bf16[2,588,384]{2,1,0:T(8,128)(2,1)}, bf16[588,512]{1,0:T(8,128)(2,1)}, f32[1,384]{1,0:T(1,128)}) custom-call(f32[588,512]{1,0:T(8,128)} %get-tuple-element.235.middle.refs_3_, f32[588,512]{1,0:T(8,128)} %get-tuple-element.236.own, f32[588,512]{1,0:T(8,128)} %copy-done.15, ...), custom_call_target="tpu_custom_call" | custom-call | flops 924844032 | bytes 10434048 | tf_op jit(solution)/shard_map/pallas_call | solution.py:83
  219.4 7.4 %shard_map.493 = (f32[588,512]{1,0:T(8,128)}, bf16[588,512]{1,0:T(8,128)(2,1)}, bf16[588,512]{1,0:T(8,128)(2,1)}, bf16[2,588,512]{2,1,0:T(8,128)(2,1)}, bf16[2,5...) custom-call(bf16[588,512]{1,0:T(8,128)(2,1)} %get-tuple-element.242.refs_0_, ...), custom_call_target="tpu_custom_call" | custom-call | flops 1849688064 | bytes 11145216 | tf_op jit(solution)/shard_map/pallas_call | solution.py:83
  227.2 6.8 %shard_map.496 = (bf16[2,64,1408]{2,1,0:T(8,128)(2,1)}, bf16[2,64,1408]{2,1,0:T(8,128)(2,1)}, bf16[2,64,1408]{2,1,0:T(8,128)(2,1)}, bf16[2,64,1408]{2,1,0:T(8,12...) custom-call(s32[2]{0:T(128)} %pad_add_fusion.1.spot, ...), custom_call_target="tpu_custom_call" | custom-call | flops 1695547392 | bytes 8001536 | tf_op jit(solution)/shard_map/pallas_call | solution.py:83
  238.0 18.7 %shard_map.494 = (f32[588,512]{1,0:T(8,128)}, bf16[588,512]{1,0:T(8,128)(2,1)}, bf16[588,512]{1,0:T(8,128)(2,1)}, bf16[2,588,384]{2,1,0:T(8,128)(2,1)}, bf16[588,512]{1,0:T(8,128)(2,1)}, /*index=5*/f32[2,512]{1,0:T(2,128)}) custom-call(f32[588,512]{1,0:T(8,128)} %get-tuple-element.244.stream_grad, bf16[588,512]{1,0:T(8,128)(2,1)} %get-tuple-element.245.own, ...), custom_call_target="tpu_custom_call" | custom-call | flops 4156981248 | bytes 10717568 | tf_op jit(solution)/shard_map/pallas_call | solution.py:83
  291.3 5.6 %shard_map.498 = (f32[147,768]{1,0:T(8,128)}, bf16[147,768]{1,0:T(8,128)(2,1)}, bf16[147,768]{1,0:T(8,128)(2,1)}, bf16[2,147,768]{2,1,0:T(8,128)(2,1)}, bf16[2,1...) custom-call(f32[147,768]{1,0:T(8,128)} %get-tuple-element.282.refs_0_, ...), custom_call_target="tpu_custom_call" | custom-call | flops 1040449536 | bytes 8130048 | tf_op jit(solution)/shard_map/pallas_call | solution.py:83
  297.0 6.5 %shard_map.500 = (bf16[2,96,1664]{2,1,0:T(8,128)(2,1)}, bf16[2,96,1664]{2,1,0:T(8,128)(2,1)}, bf16[2,96,1664]{2,1,0:T(8,128)(2,1)}, bf16[2,96,1664]{2,1,0:T(8,12...) custom-call(s32[2]{0:T(128)} %pad_add_fusion.1.spot, ...), custom_call_target="tpu_custom_call" | custom-call | flops 751435776 | bytes 6767616 | tf_op jit(solution)/shard_map/pallas_call | solution.py:83
  308.5 6.8 %shard_map.499 = (f32[147,768]{1,0:T(8,128)}, bf16[147,768]{1,0:T(8,128)(2,1)}, bf16[147,768]{1,0:T(8,128)(2,1)}, bf16[2,147,576]{2,1,0:T(8,128)(2,1)}, bf16[147,768]{1,0:T(8,128)(2,1)}, /*index=5*/f32[2,768]{1,0:T(2,128)}) custom-call(f32[147,768]{1,0:T(8,128)} %get-tuple-element.284.stream_grad, bf16[147,768]{1,0:T(8,128)(2,1)} %get-tuple-element.285.own, ...), custom_call_target="tpu_custom_call" | custom-call | flops 595752192 | bytes 6000072 | tf_op jit(solution)/shard_map/pallas_call | solution.py:83
  327.3 5.9 %shard_map.502 = (bf16[2,96,1280]{2,1,0:T(8,128)(2,1)}, bf16[2,96,1280]{2,1,0:T(8,128)(2,1)}, bf16[2,96,1280]{2,1,0:T(8,128)(2,1)}, bf16[2,96,1280]{2,1,0:T(8,12...) custom-call(s32[2]{0:T(128)} %pad_add_fusion.1.spot, ...), custom_call_target="tpu_custom_call" | custom-call | flops 346816512 | bytes 5793024 | tf_op jit(solution)/shard_map/pallas_call | solution.py:83
  351.4 9.2 %collective-permute-done.72 = bf16[2,96,1664]{2,1,0:T(8,128)(2,1)S(1)} collective-permute-done((bf16[2,96,1664]{2,1,0:T(8,128)(2,1)}, bf16[2,96,1664]{2,1,0:T(8,128)(2,1)S(1)}, u32[]{:S(2)}, u32[]{:S(2)}) %collective-permute-start.72) | collective-permute-done | bytes 639008 | tf_op jit(solution)/shard_map/ppermute | solution.py:45
  362.6 11.8 %collective-permute-done.75 = bf16[2,96,1664]{2,1,0:T(8,128)(2,1)S(1)} collective-permute-done((bf16[2,96,1664]{2,1,0:T(8,128)(2,1)}, bf16[2,96,1664]{2,1,0:T(8,128)(2,1)S(1)}, u32[]{:S(2)}, u32[]{:S(2)}) %collective-permute-start.75) | collective-permute-done | bytes 639008 | tf_op jit(solution)/shard_map/ppermute | solution.py:45
  376.8 8.1 %collective-permute-done.63 = bf16[2,96,1280]{2,1,0:T(8,128)(2,1)S(1)} collective-permute-done((bf16[2,96,1280]{2,1,0:T(8,128)(2,1)}, bf16[2,96,1280]{2,1,0:T(8,128)(2,1)S(1)}, u32[]{:S(2)}, u32[]{:S(2)}) %collective-permute-start.63) | collective-permute-done | bytes 491552 | tf_op jit(solution)/shard_map/ppermute | solution.py:45
  385.9 7.4 %collective-permute-done.68 = bf16[2,96,1280]{2,1,0:T(8,128)(2,1)S(1)} collective-permute-done((bf16[2,96,1280]{2,1,0:T(8,128)(2,1)S(1)}, bf16[2,96,1280]{2,1,0:T(8,128)(2,1)S(1)}, u32[]{:S(2)}, u32[]{:S(2)}) %collective-permute-start.68) | collective-permute-done | bytes 491552 | tf_op jit(solution)/shard_map/ppermute | solution.py:45
  398.3 13.9 %collective-permute-done.71 = bf16[96,1280]{1,0:T(8,128)(2,1)S(1)} collective-permute-done((bf16[96,1280]{1,0:T(8,128)(2,1)S(1)}, bf16[96,1280]{1,0:T(8,128)(2,1)S(1)}, u32[]{:S(2)}, u32[]{:S(2)}) %collective-permute-start.71) | collective-permute-done | bytes 245792 | tf_op jit(solution)/shard_map/ppermute | solution.py:60
  419.5 6.2 %collective-permute-done.78 = bf16[96,1664]{1,0:T(8,128)(2,1)S(1)} collective-permute-done((bf16[96,1664]{1,0:T(8,128)(2,1)S(1)}, bf16[96,1664]{1,0:T(8,128)(2,1)S(1)}, u32[]{:S(2)}, u32[]{:S(2)}) %collective-permute-start.78) | collective-permute-done | bytes 319520 | tf_op jit(solution)/shard_map/ppermute | solution.py:60
  425.7 10.6 %collective-permute-start.80 = (bf16[64,512]{1,0:T(8,128)(2,1)S(1)}, bf16[64,512]{1,0:T(8,128)(2,1)S(1)}, u32[]{:S(2)}, u32[]{:S(2)}) collective-permute-start(bf16[64,512]{1,0:T(8,128)(2,1)S(1)} %copy-done.63), channel_id=1, source_target_pairs={{0,16},{8,24},{16,0},{24,8},{1,17},{9,25},{17,1},{25,9},{2,18},{10... | collective-permute-start | bytes 196616 | tf_op jit(solution)/shard_map/ppermute | solution.py:60
  457.4 5.8 %collective-permute-done.83 = bf16[64,1408]{1,0:T(8,128)(2,1)S(1)} collective-permute-done((bf16[64,1408]{1,0:T(8,128)(2,1)S(1)}, bf16[64,1408]{1,0:T(8,128)(2,1)S(1)}, u32[]{:S(2)}, u32[]{:S(2)}) %collective-permute-start.83) | collective-permute-done | bytes 180256 | tf_op jit(solution)/shard_map/ppermute | solution.py:60
  502.6 8.1 %shard_map.503 = (f32[7,96,192]{2,1,0:T(8,128)}, f32[7,96,192]{2,1,0:T(8,128)}, f32[7,96,192]{2,1,0:T(8,128)}, f32[5,192,96]{2,1,0:T(8,128)}, f32[5,192,96]{2,1,...) custom-call(f32[1]{0:T(128)} %bitcast.77.scale, ...), custom_call_target="tpu_custom_call" | custom-call | bytes 14772224 | tf_op jit(solution)/shard_map/pallas_call | solution.py:83
  (536 shorter events, 280.5 us)
Async XLA Ops:
  4.3 35.0 %collective-permute-start.30 = (bf16[1,64,1920]{2,1,0:T(8,128)(2,1)}, bf16[1,64,1920]{2,1,0:T(8,128)(2,1)}, u32[]{:S(2)}, u32[]{:S(2)}) collective-permute-start(bf16[1,64,1920]{2,1,0:T(8,128)(2,1)} %bitcast.35.refs_0_), channel_id=1, source_target_pairs={{0,4},{4,0},{1,5},{5,1},{2,6},{6,2},{3,7},{7,3},{8,12},{12,8},{9,1... | collective-permute-start | bytes 737288 | tf_op jit(solution)/shard_map/ppermute | solution.py:45
  7.3 34.1 %collective-permute-start.29 = (bf16[1,64,1920]{2,1,0:T(8,128)(2,1)}, bf16[1,64,1920]{2,1,0:T(8,128)(2,1)}, u32[]{:S(2)}, u32[]{:S(2)}) collective-permute-start(bf16[1,64,1920]{2,1,0:T(8,128)(2,1)} %bitcast.35.refs_0_), channel_id=1, source_target_pairs={{0,2},{2,0},{1,3},{3,1},{4,6},{6,4},{5,7},{7,5},{8,10},{10,8},{9,1... | collective-permute-start | bytes 737288 | tf_op jit(solution)/shard_map/ppermute | solution.py:45
  12.1 23.4 %collective-permute-start.2 = (bf16[96,1280]{1,0:T(8,128)(2,1)}, bf16[96,1280]{1,0:T(8,128)(2,1)S(1)}, u32[]{:S(2)}, u32[]{:S(2)}) collective-permute-start(bf16[96,1280]{1,0:T(8,128)(2,1)} %concatenate.89), channel_id=1, source_target_pairs={{0,24},{8,0},{16,8},{24,16},{1,25},{9,1},{17,9},{25,17},{2,26},{10... | collective-permute-start | bytes 737288 | tf_op jit(solution)/shard_map/ppermute | solution.py:60
  38.1 23.9 %collective-permute-start.10 = (bf16[3,96,1280]{2,1,0:T(8,128)(2,1)S(1)}, bf16[3,96,1280]{2,1,0:T(8,128)(2,1)}, u32[]{:S(2)}, u32[]{:S(2)}) collective-permute-start(bf16[3,96,1280]{2,1,0:T(8,128)(2,1)S(1)} %pad_maximum_fusion.4.refs_5_), channel_id=1, source_target_pairs={{0,4},{4,0},{1,5},{5,1},{2,6},{6,2},{3,7},{7,3},{8,12},{12,8},{9,1... | collective-permute-start | bytes 2211848 | tf_op jit(solution)/shard_map/ppermute | solution.py:45
  61.9 25.6 %collective-permute-start.21 = (bf16[96,1664]{1,0:T(8,128)(2,1)S(1)}, bf16[96,1664]{1,0:T(8,128)(2,1)S(1)}, u32[]{:S(2)}, u32[]{:S(2)}) collective-permute-start(bf16[96,1664]{1,0:T(8,128)(2,1)S(1)} %copy-done.13), channel_id=1, source_target_pairs={{0,16},{8,24},{16,0},{24,8},{1,17},{9,25},{17,1},{25,9},{2,18},{10... | collective-permute-start | bytes 958472 | tf_op jit(solution)/shard_map/ppermute | solution.py:60
  62.1 26.9 %collective-permute-start.20 = (bf16[96,1664]{1,0:T(8,128)(2,1)S(1)}, bf16[96,1664]{1,0:T(8,128)(2,1)S(1)}, u32[]{:S(2)}, u32[]{:S(2)}) collective-permute-start(bf16[96,1664]{1,0:T(8,128)(2,1)S(1)} %copy-done.13), channel_id=1, source_target_pairs={{0,8},{8,16},{16,24},{24,0},{1,9},{9,17},{17,25},{25,1},{2,10},{10... | collective-permute-start | bytes 958472 | tf_op jit(solution)/shard_map/ppermute | solution.py:60
  65.7 23.4 %collective-permute-start.12 = (bf16[3,48,1280]{2,1,0:T(8,128)(2,1)S(1)}, bf16[3,48,1280]{2,1,0:T(8,128)(2,1)S(1)}, u32[]{:S(2)}, u32[]{:S(2)}) collective-permute-start(bf16[3,48,1280]{2,1,0:T(8,128)(2,1)S(1)} %slice.285), channel_id=1, source_target_pairs={{0,2},{2,0},{1,3},{3,1},{4,6},{6,4},{5,7},{7,5},{8,10},{10,8},{9,1... | collective-permute-start | bytes 1105928 | tf_op jit(solution)/shard_map/ppermute | solution.py:45
  69.9 24.9 %collective-permute-start.8 = (bf16[1,48,1280]{2,1,0:T(8,128)(2,1)}, bf16[1,48,1280]{2,1,0:T(8,128)(2,1)}, u32[]{:S(2)}, u32[]{:S(2)}) collective-permute-start(bf16[1,48,1280]{2,1,0:T(8,128)(2,1)} %slice.283), channel_id=1, source_target_pairs={{0,2},{2,0},{1,3},{3,1},{4,6},{6,4},{5,7},{7,5},{8,10},{10,8},{9,1... | collective-permute-start | bytes 368648 | tf_op jit(solution)/shard_map/ppermute | solution.py:45
  89.2 24.1 %collective-permute-start.24 = (bf16[3,96,1664]{2,1,0:T(8,128)(2,1)S(1)}, bf16[3,96,1664]{2,1,0:T(8,128)(2,1)}, u32[]{:S(2)}, u32[]{:S(2)}) collective-permute-start(bf16[3,96,1664]{2,1,0:T(8,128)(2,1)S(1)} %pad_maximum_fusion.2.refs_5_), channel_id=1, source_target_pairs={{0,4},{4,0},{1,5},{5,1},{2,6},{6,2},{3,7},{7,3},{8,12},{12,8},{9,1... | collective-permute-start | bytes 2875400 | tf_op jit(solution)/shard_map/ppermute | solution.py:45
  89.9 25.4 %collective-permute-start.23 = (bf16[3,96,1664]{2,1,0:T(8,128)(2,1)S(1)}, bf16[3,96,1664]{2,1,0:T(8,128)(2,1)}, u32[]{:S(2)}, u32[]{:S(2)}) collective-permute-start(bf16[3,96,1664]{2,1,0:T(8,128)(2,1)S(1)} %pad_maximum_fusion.2.refs_5_), channel_id=1, source_target_pairs={{0,2},{2,0},{1,3},{3,1},{4,6},{6,4},{5,7},{7,5},{8,10},{10,8},{9,1... | collective-permute-start | bytes 2875400 | tf_op jit(solution)/shard_map/ppermute | solution.py:45
  92.6 35.6 %collective-permute-start.35 = (bf16[64,1920]{1,0:T(8,128)(2,1)}, bf16[64,1920]{1,0:T(8,128)(2,1)}, u32[]{:S(2)}, u32[]{:S(2)}) collective-permute-start(bf16[64,1920]{1,0:T(8,128)(2,1)} %pad_maximum_fusion.9), channel_id=1, source_target_pairs={{0,24},{8,0},{16,8},{24,16},{1,25},{9,1},{17,9},{25,17},{2,26},{10... | collective-permute-start | bytes 737288 | tf_op jit(solution)/shard_map/ppermute | solution.py:60
  94.9 34.6 %collective-permute-start.34 = (bf16[64,1920]{1,0:T(8,128)(2,1)}, bf16[64,1920]{1,0:T(8,128)(2,1)S(1)}, u32[]{:S(2)}, u32[]{:S(2)}) collective-permute-start(bf16[64,1920]{1,0:T(8,128)(2,1)} %pad_maximum_fusion.9), channel_id=1, source_target_pairs={{0,16},{8,24},{16,0},{24,8},{1,17},{9,25},{17,1},{25,9},{2,18},{10... | collective-permute-start | bytes 737288 | tf_op jit(solution)/shard_map/ppermute | solution.py:60
  141.5 56.3 %collective-permute-start.42 = (bf16[588,1024]{1,0:T(8,128)(2,1)}, bf16[588,1024]{1,0:T(8,128)(2,1)}, u32[]{:S(2)}, u32[]{:S(2)}) collective-permute-start(bf16[588,1024]{1,0:T(8,128)(2,1)} %pad_maximum_fusion.1), channel_id=1, source_target_pairs={{0,16},{8,24},{16,0},{24,8},{1,17},{9,25},{17,1},{25,9},{2,18},{10... | collective-permute-start | bytes 3612680 | tf_op jit(solution)/shard_map/ppermute | solution.py:60
  340.2 111.1 %collective-permute-start.81 = (bf16[64,512]{1,0:T(8,128)(2,1)}, bf16[64,512]{1,0:T(8,128)(2,1)S(1)}, u32[]{:S(2)}, u32[]{:S(2)}) collective-permute-start(bf16[64,512]{1,0:T(8,128)(2,1)} %get-tuple-element.447), channel_id=1, source_target_pairs={{0,24},{8,0},{16,8},{24,16},{1,25},{9,1},{17,9},{25,17},{2,26},{10... | collective-permute-start | bytes 196616 | tf_op jit(solution)/shard_map/ppermute | solution.py:60
  347.1 27.3 %collective-permute-start.75 = (bf16[2,96,1664]{2,1,0:T(8,128)(2,1)}, bf16[2,96,1664]{2,1,0:T(8,128)(2,1)S(1)}, u32[]{:S(2)}, u32[]{:S(2)}) collective-permute-start(bf16[2,96,1664]{2,1,0:T(8,128)(2,1)} %add_convert_fusion.2), channel_id=1, source_target_pairs={{0,2},{2,0},{1,3},{3,1},{4,6},{6,4},{5,7},{7,5},{8,10},{10,8},{9,1... | collective-permute-start | bytes 1916936 | tf_op jit(solution)/shard_map/ppermute | solution.py:45
  348.0 27.3 %collective-permute-start.74 = (bf16[2,96,1664]{2,1,0:T(8,128)(2,1)S(1)}, bf16[2,96,1664]{2,1,0:T(8,128)(2,1)S(1)}, u32[]{:S(2)}, u32[]{:S(2)}) collective-permute-start(bf16[2,96,1664]{2,1,0:T(8,128)(2,1)S(1)} %copy-done.24), channel_id=1, source_target_pairs={{0,4},{4,0},{1,5},{5,1},{2,6},{6,2},{3,7},{7,3},{8,12},{12,8},{9,1... | collective-permute-start | bytes 1916936 | tf_op jit(solution)/shard_map/ppermute | solution.py:45
  360.6 24.2 %collective-permute-start.63 = (bf16[2,96,1280]{2,1,0:T(8,128)(2,1)}, bf16[2,96,1280]{2,1,0:T(8,128)(2,1)S(1)}, u32[]{:S(2)}, u32[]{:S(2)}) collective-permute-start(bf16[2,96,1280]{2,1,0:T(8,128)(2,1)} %get-tuple-element.325), channel_id=1, source_target_pairs={{0,2},{2,0},{1,3},{3,1},{4,6},{6,4},{5,7},{7,5},{8,10},{10,8},{9,1... | collective-permute-start | bytes 1474568 | tf_op jit(solution)/shard_map/ppermute | solution.py:45
  361.7 24.2 %collective-permute-start.64 = (bf16[2,96,1280]{2,1,0:T(8,128)(2,1)}, bf16[2,96,1280]{2,1,0:T(8,128)(2,1)S(1)}, u32[]{:S(2)}, u32[]{:S(2)}) collective-permute-start(bf16[2,96,1280]{2,1,0:T(8,128)(2,1)} %get-tuple-element.326), channel_id=1, source_target_pairs={{0,4},{4,0},{1,5},{5,1},{2,6},{6,2},{3,7},{7,3},{8,12},{12,8},{9,1... | collective-permute-start | bytes 1474568 | tf_op jit(solution)/shard_map/ppermute | solution.py:45
  384.9 69.9 %collective-permute-start.79 = (bf16[64,512]{1,0:T(8,128)(2,1)S(1)}, bf16[64,512]{1,0:T(8,128)(2,1)S(1)}, u32[]{:S(2)}, u32[]{:S(2)}) collective-permute-start(bf16[64,512]{1,0:T(8,128)(2,1)S(1)} %copy-done.64), channel_id=1, source_target_pairs={{0,8},{8,16},{16,24},{24,0},{1,9},{9,17},{17,25},{25,1},{2,10},{10... | collective-permute-start | bytes 196616 | tf_op jit(solution)/shard_map/ppermute | solution.py:60
  412.1 24.1 %collective-permute-start.76 = (bf16[96,1664]{1,0:T(8,128)(2,1)S(1)}, bf16[96,1664]{1,0:T(8,128)(2,1)S(1)}, u32[]{:S(2)}, u32[]{:S(2)}) collective-permute-start(bf16[96,1664]{1,0:T(8,128)(2,1)S(1)} %get-tuple-element.418), channel_id=1, source_target_pairs={{0,8},{8,16},{16,24},{24,0},{1,9},{9,17},{17,25},{25,1},{2,10},{10... | collective-permute-start | bytes 958472 | tf_op jit(solution)/shard_map/ppermute | solution.py:60
  416.1 28.3 %collective-permute-start.77 = (bf16[96,1664]{1,0:T(8,128)(2,1)S(1)}, bf16[96,1664]{1,0:T(8,128)(2,1)S(1)}, u32[]{:S(2)}, u32[]{:S(2)}) collective-permute-start(bf16[96,1664]{1,0:T(8,128)(2,1)S(1)} %get-tuple-element.419), channel_id=1, source_target_pairs={{0,16},{8,24},{16,0},{24,8},{1,17},{9,25},{17,1},{25,9},{2,18},{10... | collective-permute-start | bytes 958472 | tf_op jit(solution)/shard_map/ppermute | solution.py:60
  425.7 29.1 %collective-permute-start.80 = (bf16[64,512]{1,0:T(8,128)(2,1)S(1)}, bf16[64,512]{1,0:T(8,128)(2,1)S(1)}, u32[]{:S(2)}, u32[]{:S(2)}) collective-permute-start(bf16[64,512]{1,0:T(8,128)(2,1)S(1)} %copy-done.63), channel_id=1, source_target_pairs={{0,16},{8,24},{16,0},{24,8},{1,17},{9,25},{17,1},{25,9},{2,18},{10... | collective-permute-start | bytes 196616 | tf_op jit(solution)/shard_map/ppermute | solution.py:60
  454.8 34.7 %collective-permute-start.88 = (bf16[96,384]{1,0:T(8,128)(2,1)S(1)}, bf16[96,384]{1,0:T(8,128)(2,1)S(1)}, u32[]{:S(2)}, u32[]{:S(2)}) collective-permute-start(bf16[96,384]{1,0:T(8,128)(2,1)S(1)} %get-tuple-element.394), channel_id=1, source_target_pairs={{0,1},{1,0},{2,3},{3,2},{4,5},{5,4},{6,7},{7,6},{8,9},{9,8},{10,11... | collective-permute-start | bytes 221192 | tf_op jit(solution)/shard_map/ppermute | solution.py:45
  454.8 34.7 %collective-permute-start.90 = (bf16[96,384]{1,0:T(8,128)(2,1)S(1)}, bf16[96,384]{1,0:T(8,128)(2,1)S(1)}, u32[]{:S(2)}, u32[]{:S(2)}) collective-permute-start(bf16[96,384]{1,0:T(8,128)(2,1)S(1)} %get-tuple-element.394), channel_id=1, source_target_pairs={{0,3},{1,2},{2,1},{3,0},{4,7},{5,6},{6,5},{7,4},{8,11},{9,10},{10,... | collective-permute-start | bytes 221192 | tf_op jit(solution)/shard_map/ppermute | solution.py:689
  (156 other events, 1778.9 us)

commit v4 on v3

--- a/solution.py
+++ b/solution.py
@@ -142,16 +142,17 @@
         return [whole.reshape(2, 8 * rows, -1) for whole in wholes]
 
 
-def spread_all(blobs, widths, arrived):
+def spread_all(blobs, widths, picked):
     sizes = tuple(lax.axis_size(axis) for axis in ("x", "z", "y"))
     if sizes != (2, 4, 2):
         wholes = [lax.all_gather(blob, ("x", "z", "y")) for blob in blobs]
         wholes = [whole.reshape(2, -1, whole.shape[-1]) for whole in wholes]
         pieces = [columns_of(whole, width) for whole, width in zip(wholes, widths)]
         return pieces, [wholes[0]] * 4
-    first, second, third = (Spread(blob) for blob in blobs)
+    first = Spread(blobs[0])
     first.along_z()
-    second.along_z(*first.moved, arrived)
+    second, third = (Spread(blob, picked) for blob in blobs[1:])
+    second.along_z(*first.moved)
     first.round_plane()
     third.along_z(*first.far[:2])
     second.moved = [after(moved, *first.far[:2]) for moved in second.moved]
@@ -159,7 +160,7 @@
     third.moved = [after(moved, *second.far[:2]) for moved in third.moved]
     third.round_plane(*second.far)
     pieces = [group.whole(width) for group, width in zip((first, second, third), widths)]
-    return pieces, [first.stack, first.far[0], first.far[2], third.stack]
+    return pieces, [first.stack, first.far[0], first.far[2], second.far[0]]
 
 
 def share(pieces, rows, patch=None, norms=None):
@@ -256,13 +257,14 @@
 
 
 class Collect:
-    def __init__(self, *cuts):
+    def __init__(self, cuts, *earlier):
         self.direct = None
-        self.mark = ()
+        self.corner = self.early = self.late = self.moved = ()
         if len(cuts) == 1:
             self.direct = lax.psum_scatter(cuts[0], ("x", "z", "y"), scatter_dimension=0)
             return
-        self.own, self.by_y, self.by_x, corner = cuts[:2], cuts[2:4], cuts[4:6], cuts[6:]
+        cuts = lax.optimization_barrier((*cuts, *earlier))
+        self.own, self.by_y, self.by_x, corner = cuts[:2], cuts[2:4], cuts[4:6], cuts[6:8]
         self.corner = (swap(corner[0], "x"), swap(corner[1], "y"))
         self.early = (swap(self.by_x[0], "x"), swap(self.by_y[1], "y"))
 
@@ -287,10 +289,10 @@
         self.moved = [shift(part, "z", step) for step, part in enumerate(parts[1:], 1)]
         return tuple(parts)
 
-    def total(self, *earlier):
+    def terms(self, *earlier):
         if self.direct is not None:
-            return self.direct.astype(FLOAT_TYPE)
-        return add(self.mine, *lax.optimization_barrier((*self.moved, *earlier))[:3])
+            return (self.direct,)
+        return self.mine, *lax.optimization_barrier((*self.moved, *earlier))[:3]
 
 
 def dot_nn(left, right):
@@ -635,7 +637,74 @@
     return [weight, moment, second]
 
 
-def adam_all(scale, masters, moments, seconds, grads):
+def lane_is(number):
+    return lax.broadcasted_iota(jnp.int32, (1, LANES), 1) == number
+
+
+def sum_early(groups, embed_width):
+    count = sum(len(group) for group in groups)
+
+    def body(*refs):
+        outs = refs[count:]
+        used, square = 0, 0.0
+        for number, group in enumerate(groups):
+            total = add(*(ref[...] for ref in refs[used : used + len(group)]))
+            used += len(group)
+            if number == len(groups) - 1:
+                embed = low(total[:, total.shape[1] - embed_width :])
+                outs[number + 1][...] = embed
+                total = total[:, : total.shape[1] - embed_width]
+                embed = embed.astype(FLOAT_TYPE)
+                square = square + jnp.sum(embed * embed, keepdims=True)
+            outs[number][...] = total
+            square = square + jnp.sum(total * total, keepdims=True)
+        outs[-1][...] = square
+
+    outs = []
+    for number, group in enumerate(groups):
+        rows, columns = group[0].shape
+        outs.append(((rows, columns - embed_width * (number == len(groups) - 1)), FLOAT_TYPE))
+    outs += [((groups[-1][0].shape[0], embed_width), NARROW_TYPE), ((1, 1), FLOAT_TYPE)]
+    flat = [term for group in groups for term in group]
+    *sums, embed, square = vmem_call(body, outs, *flat)
+    return sums, embed, square
+
+
+def sum_late(terms, embed, square, loss_part, valid_count, patch_width):
+    count = len(terms)
+    rows, columns = terms[0].shape
+    split = patch_width + LANES
+
+    def body(*refs):
+        embed, square, loss, valid, rest, exchanged, totals = refs[count:]
+        total = add(*(ref[...] for ref in refs[:count]))
+        kept = total[:, split:]
+        rest[...] = kept
+        sent = low(total[:, :split])
+        exchanged[:, :split] = sent
+        exchanged[:, split:] = embed[...]
+        sent = sent.astype(FLOAT_TYPE)
+        squares = sent * sent
+        gathered = (
+            square[...]
+            + jnp.sum(kept * kept, keepdims=True)
+            + jnp.sum(squares[:, :patch_width], keepdims=True)
+            + 0.5 * jnp.sum(squares[:, patch_width:], keepdims=True)
+        )
+        loss = jnp.sum(loss[...], keepdims=True)
+        totals[...] = jnp.where(
+            lane_is(0), loss, jnp.where(lane_is(1), 0.25 * valid[...], jnp.where(lane_is(2), gathered, 0.0))
+        )
+
+    outs = [
+        ((rows, columns - split), FLOAT_TYPE),
+        ((rows, split + embed.shape[1]), NARROW_TYPE),
+        ((1, LANES), FLOAT_TYPE),
+    ]
+    return vmem_call(body, outs, *terms, embed, square, loss_part, valid_count.reshape(1, 1))
+
+
+def adam_all(place, totals, masters, moments, seconds, sums, exchanged, norm_sum):
     orders = ((1, 0, 2), None, (1, 0, 2), (0, 2, 1))
     shapes = [array.shape for array in masters]
 
@@ -653,51 +722,65 @@
         [view(array, number) for array in (masters[number], moments[number], seconds[number])]
         for number in range(8)
     ]
-    grads = [view(grad, 7) if number == 7 else grad for number, grad in enumerate(grads)]
-
-    def body(scale, *refs):
-        arrays, gradients, outs = refs[:24], refs[24:32], refs[32:]
-        factor = scale[0]
-        for number in range(8):
-            ins, news = arrays[3 * number : 3 * number + 3], outs[3 * number : 3 * number + 3]
+    flat = [array for triple in triples for array in triple]
+    part_enc, part_dec = shapes[0][2], shapes[2][2]
+    patch_rows, patch_width = shapes[4][0] // 2, shapes[4][1] // 2
+    embed_width = shapes[5][1] // 4
+
+    def body(place, totals, *refs):
+        arrays, refs = refs[:24], refs[24:]
+        (dec_attn, dec_tail, enc_tail, enc_attn, *parts, norm_sum), refs = refs[:9], refs[9:]
+        scalars, outs = refs[0], refs[1:]
+        loss, count, square = (
+            jnp.sum(jnp.where(lane_is(n), totals[...], 0.0), keepdims=True) for n in range(3)
+        )
+        grad_norm = jnp.sqrt(square) / count
+        factor = CLIP / jnp.maximum(grad_norm, CLIP) / count
+        scalars[...] = jnp.where(lane_is(0), loss, jnp.where(lane_is(1), count, grad_norm))
+
+        def update(number, where, grad):
             step_rate = LR_NORM if number == 7 else LR_MATRIX
             decay_rate = 0.0 if number == 7 else DECAY
-            blocks = ins[0].shape[0] if number < 4 else 1
-            for block in range(blocks):
-                if number < 4:
-                    width = ins[0].shape[1] if number == 1 else ins[0].shape[2]
-                    grad = gradients[number][:, block * width : (block + 1) * width]
-                    grad = grad.T if number == 1 else grad
-                    values = [ref[block] for ref in ins]
-                else:
-                    grad = gradients[number][...].astype(FLOAT_TYPE)
-                    values = [ref[...] for ref in ins]
-                results = adam_update(*values, grad * factor, step_rate, decay_rate)
-                for ref, result in zip(news, results):
-                    if number < 4:
-                        ref[block] = result
-                    else:
-                        ref[...] = result
-
-    flat = [array for triple in triples for array in triple]
-    outs = [(array.shape, FLOAT_TYPE) for array in flat]
-    results = vmem_call(body, outs, *flat, *grads, scalars=(scale[None],))
-    return [unview(result, index // 3) for index, result in enumerate(results)]
-
-
-def from_all(piece, x, c):
-    there = [piece, swap(piece, "c"), swap(piece, "x"), lax.ppermute(piece, ("x", "c"), ACROSS)]
-    ordered = []
-    for number in range(4):
-        at_x, at_c = x ^ (number // 2), c ^ (number % 2)
-        ordered.append(
-            jnp.where(
-                at_x == 0,
-                jnp.where(at_c == 0, there[0], there[1]),
-                jnp.where(at_c == 0, there[2], there[3]),
-            )
-        )
-    return ordered
+            values = (ref[where] for ref in arrays[3 * number : 3 * number + 3])
+            results = adam_update(*values, grad * factor, step_rate, decay_rate)
+            for ref, result in zip(outs[3 * number : 3 * number + 3], results):
+                ref[where] = result
+
+        def piece(at_x, at_c, columns):
+            far_x, far_c = place[0] != at_x, place[1] != at_c
+            cuts = [part[:, columns] for part in parts]
+            rows = [jnp.where(far_c, cuts[n + 1], cuts[n]) for n in (0, 2)]
+            return jnp.where(far_x, rows[1], rows[0]).astype(FLOAT_TYPE)
+
+        for number, attn, tail, width in (
+            (0, enc_attn, enc_tail, part_enc),
+            (2, dec_attn, dec_tail, part_dec),
+        ):
+            for block in range(7):
+                source, first = (attn, block) if block < 3 else (tail, block - 3)
+                update(number, block, source[:, first * width : (first + 1) * width])
+            for block in range(5):
+                source, first = (attn, 3) if block == 0 else (tail, 3 + block)
+                grad = source[:, first * width : (first + 1) * width]
+                update(number + 1, block, grad.T if number == 0 else grad)
+        for at_x in (0, 1):
+            for at_c in (0, 1):
+                grad = piece(at_x, at_c, slice(0, patch_width))
+                rows = slice(at_x * patch_rows, (at_x + 1) * patch_rows)
+                columns = slice(at_c * patch_width, (at_c + 1) * patch_width)
+                update(4, (rows, columns), grad)
+                first = patch_width + LANES
+                grad = piece(at_x, at_c, slice(first, first + embed_width))
+                number = 2 * at_x + at_c
+                update(5, (slice(None), slice(number * embed_width, (number + 1) * embed_width)), grad)
+        update(6, Ellipsis, dec_tail[:, 8 * part_dec :])
+        update(7, Ellipsis, norm_sum[...].astype(FLOAT_TYPE))
+
+    outs = [((1, LANES), FLOAT_TYPE)] + [(array.shape, FLOAT_TYPE) for array in flat]
+    scalars, *results = vmem_call(
+        body, outs, totals, *flat, *sums, *exchanged, view(norm_sum, 7), scalars=(place,)
+    )
+    return scalars, [unview(result, index // 3) for index, result in enumerate(results)]
 
 
 def both(piece, axis, place, dimension):
@@ -848,7 +931,7 @@
     seen_away = shift(halves_of(seen_of(away, away_slot), c), "z", half_step)
 
     (first_all, second_all, third_all), marks = spread_all(
-        (first_blob, second_blob, third_blob), widths, seen_away
+        (first_blob, second_blob, third_blob), widths, own_slot
     )
 
     patch_all, norm_all, enc_qkv, enc_proj = first_all
@@ -935,15 +1018,12 @@
         goal,
         part_mask,
     )
-    loss_part = jnp.sum(loss_part)
 
     stream_grad, grad_low, normed_low, hidden_low, upward_low, partial, dec_norms_three = mlp_back(
         (partial, swap(partial)), dec_last, dec_middle, dec_gains, dec_up, dec_down
     )
     dec_tail = Collect(
-        *share(
-            [(normed_low, upward_low), (grad_low, hidden_low), (dec_normed, pred_low)], rows_dec
-        )
+        share([(normed_low, upward_low), (grad_low, hidden_low), (dec_normed, pred_low)], rows_dec)
     )
     stream_grad, grad_low, normed_low, triple_grad, partial, dec_norms_two = attn_back(
         stream_grad,
@@ -958,7 +1038,9 @@
         dec_heads,
     )
     normed_low = after(normed_low, *dec_tail.second(triple_grad))
-    dec_attn = Collect(*share([(normed_low, triple_grad), (grad_low, dec_mixture)], rows_dec))
+    dec_attn = Collect(
+        share([(normed_low, triple_grad), (grad_low, dec_mixture)], rows_dec), *dec_tail.late
+    )
     embed_mine, normed_grad, mask_grad, dec_norms_one = decoder_end(
         stream_grad,
         partial,
@@ -972,12 +1054,13 @@
     )
 
     stream_grad, grad_low, normed_low, hidden_low, upward_low, partial, enc_norms_three = mlp_back(
-        (after(normed_grad, *dec_attn.second(), *dec_tail.third(normed_grad)),), enc_last, enc_middle, enc_gains, enc_up, enc_down
+        (after(normed_grad, *dec_attn.second(), *dec_tail.third()),), enc_last, enc_middle, enc_gains, enc_up, enc_down
     )
     enc_tail = Collect(
-        *share([(normed_low, upward_low), (grad_low, hidden_low), (enc_normed, embed_mine)], rows_enc)
-    )
-    other_partial = after(swap(partial), *dec_attn.third(*enc_tail.mark))
+        share([(normed_low, upward_low), (grad_low, hidden_low), (enc_normed, embed_mine)], rows_enc),
+        *dec_attn.late,
+    )
+    other_partial = after(swap(partial), *dec_attn.third(), *dec_tail.moved)
     stream_grad, grad_low, normed_low, triple_grad, partial, enc_norms_two = attn_back(
         stream_grad,
         partial,
@@ -990,7 +1073,7 @@
         enc_proj,
         enc_heads,
     )
-    other_partial = after(swap(partial), *enc_tail.second(partial))
+    other_partial = after(swap(partial), *enc_tail.second(), *dec_attn.moved)
     patch_right, enc_norms_one = encoder_end(
         stream_grad, partial, other_partial, enc_stream, enc_gains, c[None]
     )
@@ -1016,59 +1099,42 @@
     norm_grads = low(norm_grad).reshape(data_size, 2, norm_half).transpose(1, 0, 2)
     norm_grads = jnp.pad(norm_grads, ((0, 0), (0, 0), (0, norm_room - norm_half)))
     enc_attn = Collect(
-        *share(
+        share(
             [(normed_low, triple_grad), (grad_low, enc_mixture)],
             rows_enc,
             (seen_rows, patch_right),
             norm_grads.reshape(2, data_size, rows_enc, LANES),
-        )
-    )
-
-    enc_tail_sent = enc_tail.third(*enc_attn.second())
-    dec_tail_sum, dec_attn_sum = dec_tail.total(*enc_tail_sent), dec_attn.total(*enc_tail_sent)
-    enc_tail_sum = enc_tail.total(*enc_attn.third())
-    enc_attn_sum = enc_attn.total()
-    patch_sum, norm_sum, qkv_sum, proj_sum = columns_of(enc_attn_sum, widths[0])
-    up_sum, down_sum, embed_sum = columns_of(enc_tail_sum, widths[1])
-    dec_qkv_sum, dec_proj_sum = columns_of(dec_attn_sum, (3 * part_dec, part_dec))
-    dec_up_sum, dec_down_sum, head_sum = columns_of(
-        dec_tail_sum, (4 * part_dec, 4 * part_dec, head_low.shape[1])
-    )
-    norm_sum = low(norm_sum.reshape(-1)[:norm_half])
-    patch_sum, embed_sum = low(patch_sum), low(embed_sum)
-    shared_square = sum(
-        jnp.sum(jnp.square(piece.astype(FLOAT_TYPE))) for piece in (patch_sum, embed_sum)
-    ) + 0.5 * jnp.sum(jnp.square(norm_sum.astype(FLOAT_TYPE)))
-    own_square = sum(
-        jnp.sum(jnp.square(piece))
-        for piece in (qkv_sum, proj_sum, up_sum, down_sum, dec_attn_sum, dec_tail_sum)
-    )
-    patch_all = from_all(patch_sum, x, c)
-    embed_all = from_all(embed_sum, x, c)
-    norm_sum = both(norm_sum, "x", x, 0)
-    patch_full = jnp.concatenate([jnp.concatenate([patch_all[n], patch_all[n + 1]], 1) for n in (0, 2)])
-    embed_full = jnp.concatenate(embed_all, 1)
-    totals = jnp.stack([loss_part, own_square + shared_square, valid_count * 0.25])
+        ),
+        *enc_tail.late,
+    )
+
+    enc_tail_sent = enc_tail.third()
+    enc_attn_sent = enc_attn.second(*enc_tail_sent)
+    early_sums, embed_sum, square = sum_early(
+        [group.terms(*enc_attn_sent) for group in (dec_attn, dec_tail, enc_tail)], quarter_dec
+    )
+    enc_attn.third(*enc_tail.moved)
+    late_sum, exchanged, totals = sum_late(
+        enc_attn.terms(), embed_sum, square, loss_part, valid_count, half_enc
+    )
+    exchanged = [
+        exchanged,
+        swap(exchanged, "c"),
+        swap(exchanged, "x"),
+        lax.ppermute(exchanged, ("x", "c"), ACROSS),
+    ]
+    norm_cuts = [
+        part[:, half_enc : half_enc + LANES].reshape(-1)[:norm_half]
+        for part in (exchanged[0], exchanged[2])
+    ]
+    norm_sum = jnp.where(x == 0, jnp.concatenate(norm_cuts), jnp.concatenate(norm_cuts[::-1]))
     totals = total_over(totals, ("c", "x", "y"))
-    totals, patch_full, embed_full, norm_sum = lax.optimization_barrier(
-        (totals, patch_full, embed_full, norm_sum)
-    )
+    totals, *exchanged = lax.optimization_barrier((totals, *exchanged))
     totals = total_over(totals, ("z",))
-    loss_sum, valid_count = totals[0], totals[2]
-    grad_norm = jnp.sqrt(totals[1]) / valid_count
-    scale = CLIP / jnp.maximum(grad_norm, CLIP) / valid_count
-    grads = (
-        jnp.concatenate([qkv_sum, up_sum], 1),
-        jnp.concatenate([proj_sum, down_sum], 1),
-        jnp.concatenate([dec_qkv_sum, dec_up_sum], 1),
-        jnp.concatenate([dec_proj_sum, dec_down_sum], 1),
-        patch_full,
-        embed_full,
-        head_sum,
-        norm_sum,
-    )
-    updated = adam_all(scale, masters, moments, seconds, grads)
-    return (loss_sum, valid_count, grad_norm, *updated)
+    scalars, updated = adam_all(
+        jnp.stack([x, c]), totals, masters, moments, seconds, [*early_sums, late_sum], exchanged, norm_sum
+    )
+    return (scalars[0, 0], scalars[0, 1], scalars[0, 2], *updated)
 
 
 def solution(mesh):

time: 521 us -> 472 us (0.906)
  waiting for transfers between devices: 161 us -> 137 us
  starting transfers between devices: 105 us -> 92.2 us
  other arithmetic: 54.4 us -> 43.9 us
  between operations: 12.3 us -> 3.16 us
  Pallas kernels: 127 us -> 133 us
    ppermute x66 -> x63, waiting for transfers between devices: 74 us -> 52 us  [swap(): return lax.ppermute(values, axis, SWAP)]
    ppermute x66 -> x63, starting transfers between devices: 57.7 us -> 48.6 us  [swap(): return lax.ppermute(values, axis, SWAP)]
    ppermute x24, starting transfers between devices: 43.7 us -> 36.3 us  [shift(): lax.ppermute(values, axis, [(i, (i + step) % size) for i in range(size)])]
    pallas_call x20 -> x22, Pallas kernels: 127 us -> 133 us  [vmem_call(): pl.pallas_call(body, out_shape=shapes, in_specs=[pl.BlockSpec(memory_spac...]
    ppermute x5, starting transfers between devices: 1.73 us -> 7.06 us  [total_over(): lax.ppermute(values, axis, [(i, i ^ step) for i in range(size)])]
    unnamed x181 -> x191, local copies, waits for them, and re-layouts: 16.8 us -> 17.6 us
  transfers between devices with their start and end apart: 97 -> 93, of which waited for: 40 -> 31; matrix products, arithmetic and copies ran while one was open for 16% -> 16% of each run, Pallas kernels for 16% -> 20%
where the time goes in v4:
time: 472 us; the launch traced here: 464 us
  waiting for transfers between devices  137 us (29%)
  Pallas kernels  133 us (28%)
  starting transfers between devices  92.2 us (20%)
  local copies, waits for them, and re-layouts  51.9 us (11%)
  other arithmetic  43.9 us (9%)
    pallas_call x22, Pallas kernels, vmem_call(): pl.pallas_call(body, out_shape=shapes, in_specs=[pl.BlockSpec(memory_spac...  133 us
    ppermute x24, waiting for transfers between devices, shift(): lax.ppermute(values, axis, [(i, (i + step) % size) for i in range(size)])  76.4 us
    ppermute x63, waiting for transfers between devices, swap(): return lax.ppermute(values, axis, SWAP)  52 us
    ppermute x63, starting transfers between devices, swap(): return lax.ppermute(values, axis, SWAP)  48.6 us
    ppermute x24, starting transfers between devices, shift(): lax.ppermute(values, axis, [(i, (i + step) % size) for i in range(size)])  36.3 us
    unnamed x191, local copies, waits for them, and re-layouts  17.6 us
    dynamic_slice x4, local copies, waits for them, and re-layouts, pick(): return lax.dynamic_index_in_dim(array, index, axis, keepdims=False)  12.3 us
    convert_element_type x22, other arithmetic, low(): return values.astype(NARROW_TYPE)  11.2 us
  transfers between devices with their start and end apart: 93, of which 31 were waited for; matrix products, arithmetic and copies ran while one was open for 16% of the time, Pallas kernels for 20%

profile of v4, /device:TPU:0, one launch (start us, length us, event | category | flops | bytes accessed | tf_op | source)
XLA Modules:
  0.0 463.7 jit_solution(3525201455182495140)
XLA Ops:
  23.2 10.7 %constant_dynamic-slice_fusion.5 = (bf16[1,588,1536]{2,0,1:T(2,128)(2,1)S(1)}, bf16[1,588,1536]{2,0,1:T(2,128)(2,1)}) fusion(bf16[4,588,1536]{2,0,1:T(4,128)(2,1)} %param.29, s32[]{:T(128)S(6)} %select_n.203, s32[]{:T(128)S(6)} %select_n.206), kind=kLoop, calls=%fused_computation.157 | loop fusion | bytes 7225352 | tf_op jit(solution)/shard_map/jit(dynamic_index_in_dim)/dynamic_slice | solution.py:805
  69.8 19.3 %collective-permute-done.21 = bf16[96,1664]{1,0:T(8,128)(2,1)S(1)} collective-permute-done((bf16[96,1664]{1,0:T(8,128)(2,1)S(1)}, bf16[96,1664]{1,0:T(8,128)(2,1)S(1)}, u32[]{:S(2)}, u32[]{:S(2)}) %collective-permute-start.21) | collective-permute-done | bytes 319520 | tf_op jit(solution)/shard_map/ppermute | solution.py:60
  108.0 13.8 %collective-permute-done.8.refs_4_ = bf16[1,48,1280]{2,1,0:T(8,128)(2,1)S(1)} collective-permute-done((bf16[1,48,1280]{2,1,0:T(8,128)(2,1)}, bf16[1,48,1280]{2,1,0:T(8,128)(2,1)S(1)}, u32[]{:S(2)}, u32[]{:S(2)}) %collective-permute-start.8) | collective-permute-done | bytes 122912 | tf_op jit(solution)/shard_map/ppermute | solution.py:45
  131.9 5.8 %collective-permute-start.33 = (bf16[64,1920]{1,0:T(8,128)(2,1)}, bf16[64,1920]{1,0:T(8,128)(2,1)}, u32[]{:S(2)}, u32[]{:S(2)}) collective-permute-start(bf16[64,1920]{1,0:T(8,128)(2,1)} %pad_maximum_fusion.7), channel_id=1, source_target_pairs={{0,8},{8,16},{16,24},{24,0},{1,9},{9,17},{17,25},{25,1},{2,10},{10... | collective-permute-start | bytes 737288 | tf_op jit(solution)/shard_map/ppermute | solution.py:60
  144.3 5.1 %shard_map.485 = (f32[147,768]{1,0:T(8,128)}, bf16[2,147,576]{2,1,0:T(8,128)(2,1)}, bf16[2,147,192]{2,1,0:T(8,128)(2,1)}, f32[147,6]{1,0:T(8,128)}) custom-call(f32[147,768]{1,0:T(8,128)} %fusion.4.stream, f32[6,768]{1,0:T(8,128)} %reshape.330.gains.refs_3_, bf16[2,768,576]{2,1,0:T(8,128)(2,1)} %bitcast.171, bf16[2,768,192]{2,1,0:T(8,128)(2,1)} %bitcast.176), custom_call_target="tpu_custom_call" | custom-call | flops 446390784 | bytes 3736008 | tf_op jit(solution)/shard_map/pallas_call | solution.py:83
  156.9 5.1 %shard_map.486 = (bf16[2,4,2,96,768]{4,3,2,1,0:T(8,128)(2,1)}, bf16[2,4,2,96,768]{4,3,2,1,0:T(8,128)(2,1)}, bf16[2,4,2,96,128]{4,3,2,1,0:T(8,128)(2,1)}) custom-call(s32[3]{0:T(128)} %pad_add_fusion.2.spot, bf16[1,96,1664]{2,1,0:T(8,128)(2,1)} %bitcast.179, bf16[1,96,1664]{2,1,0:T(8,128)(2,1)} %copy-done.20, bf16[1,96,1664]{2,1,0:T(8,128)(2,1)} %copy-done.19, ...), custom_call_target="tpu_custom_call" | custom-call | bytes 10223616 | tf_op jit(solution)/shard_map/pallas_call | solution.py:83
  165.3 5.1 %shard_map.487 = (f32[147,768]{1,0:T(8,128)}, f32[147,768]{1,0:T(8,128)}) custom-call(f32[147,768]{1,0:T(8,128)} %fusion.4.stream, f32[147,768]{1,0:T(8,128)} %get-tuple-element.249.own, f32[147,768]{1,0:T(8,128)} %collective-permute-done.15.other, f32[6,768]{1,0:T(8,128)} %reshape.330.gains.refs_3_, bf16[2,768,768]{2,1,0:T(8,128)(2,1)} %bitcast.167, ...), custom_call_target="tpu_custom_call" | custom-call | flops 693633024 | bytes 6994944 | tf_op jit(solution)/shard_map/pallas_call | solution.py:83
  181.8 24.4 %collective-permute-done.42 = bf16[588,1024]{1,0:T(8,128)(2,1)} collective-permute-done((bf16[588,1024]{1,0:T(8,128)(2,1)}, bf16[588,1024]{1,0:T(8,128)(2,1)}, u32[]{:S(2)}, u32[]{:S(2)}) %collective-permute-start.42) | collective-permute-done | bytes 1204256 | tf_op jit(solution)/shard_map/ppermute | solution.py:60
  212.3 10.8 %shard_map.490 = (f32[588,512]{1,0:T(8,128)}, bf16[2,588,384]{2,1,0:T(8,128)(2,1)}, bf16[2,588,128]{2,1,0:T(8,128)(2,1)}, f32[588,8]{1,0:T(8,128)}) custom-call(f32[588,512]{1,0:T(8,128)} %get-tuple-element.261.stream, f32[6,512]{1,0:T(8,128)} %slice_convert_fusion.1.gains.refs_4_, bf16[2,512,384]{2,1,0:T(8,128)(2,1)} %bitcast.222, ...), custom_call_target="tpu_custom_call" | custom-call | flops 2032730112 | bytes 4692352 | tf_op jit(solution)/shard_map/pallas_call | solution.py:83
  227.2 5.5 %shard_map.491 = (f32[588,512]{1,0:T(8,128)}, f32[588,512]{1,0:T(8,128)}) custom-call(f32[588,512]{1,0:T(8,128)} %get-tuple-element.261.stream, f32[588,512]{1,0:T(8,128)} %get-tuple-element.270.own, f32[588,512]{1,0:T(8,128)} %copy-done.14, f32[6,512]{1,0:T(8,128)} %slice_convert_fusion.1.gains.refs_4_, bf16[2,512,512]{2,1,0:T(8,128)(2,1)} %bitcast.183, ...), custom_call_target="tpu_custom_call" | custom-call | flops 1233125376 | bytes 8130560 | tf_op jit(solution)/shard_map/pallas_call | solution.py:83
  236.9 5.7 %shard_map.492 = (f32[588,512]{1,0:T(8,128)}, bf16[588,512]{1,0:T(8,128)(2,1)}, bf16[2,588,384]{2,1,0:T(8,128)(2,1)}, bf16[588,512]{1,0:T(8,128)(2,1)}, f32[1,384]{1,0:T(1,128)}) custom-call(f32[588,512]{1,0:T(8,128)} %get-tuple-element.273.middle.refs_3_, f32[588,512]{1,0:T(8,128)} %get-tuple-element.274.own, f32[588,512]{1,0:T(8,128)} %copy-done.13, ...), custom_call_target="tpu_custom_call" | custom-call | flops 924844032 | bytes 10434048 | tf_op jit(solution)/shard_map/pallas_call | solution.py:83
  245.7 7.3 %shard_map.493 = (f32[588,512]{1,0:T(8,128)}, bf16[588,512]{1,0:T(8,128)(2,1)}, bf16[588,512]{1,0:T(8,128)(2,1)}, bf16[2,588,512]{2,1,0:T(8,128)(2,1)}, bf16[2,5...) custom-call(bf16[588,512]{1,0:T(8,128)(2,1)} %get-tuple-element.279.refs_0_, ...), custom_call_target="tpu_custom_call" | custom-call | flops 1849688064 | bytes 11145216 | tf_op jit(solution)/shard_map/pallas_call | solution.py:83
  253.4 6.8 %shard_map.496 = (bf16[2,64,1408]{2,1,0:T(8,128)(2,1)}, bf16[2,64,1408]{2,1,0:T(8,128)(2,1)}, bf16[2,64,1408]{2,1,0:T(8,128)(2,1)}, bf16[2,64,1408]{2,1,0:T(8,12...) custom-call(s32[2]{0:T(128)} %pad_add_fusion.1.spot, ...), custom_call_target="tpu_custom_call" | custom-call | flops 1695547392 | bytes 8001536 | tf_op jit(solution)/shard_map/pallas_call | solution.py:83
  265.1 18.7 %shard_map.494 = (f32[588,512]{1,0:T(8,128)}, bf16[588,512]{1,0:T(8,128)(2,1)}, bf16[588,512]{1,0:T(8,128)(2,1)}, bf16[2,588,384]{2,1,0:T(8,128)(2,1)}, bf16[588,512]{1,0:T(8,128)(2,1)}, /*index=5*/f32[2,512]{1,0:T(2,128)}) custom-call(f32[588,512]{1,0:T(8,128)} %get-tuple-element.281.stream_grad, bf16[588,512]{1,0:T(8,128)(2,1)} %get-tuple-element.282.own, ...), custom_call_target="tpu_custom_call" | custom-call | flops 4156981248 | bytes 10717568 | tf_op jit(solution)/shard_map/pallas_call | solution.py:83
  307.6 5.6 %shard_map.498 = (f32[147,768]{1,0:T(8,128)}, bf16[147,768]{1,0:T(8,128)(2,1)}, bf16[147,768]{1,0:T(8,128)(2,1)}, bf16[2,147,768]{2,1,0:T(8,128)(2,1)}, bf16[2,1...) custom-call(f32[147,768]{1,0:T(8,128)} %get-tuple-element.327.refs_0_, ...), custom_call_target="tpu_custom_call" | custom-call | flops 1040449536 | bytes 8130048 | tf_op jit(solution)/shard_map/pallas_call | solution.py:83
  313.2 6.5 %shard_map.500 = (bf16[2,96,1664]{2,1,0:T(8,128)(2,1)}, bf16[2,96,1664]{2,1,0:T(8,128)(2,1)}, bf16[2,96,1664]{2,1,0:T(8,128)(2,1)}, bf16[2,96,1664]{2,1,0:T(8,12...) custom-call(s32[2]{0:T(128)} %pad_add_fusion.1.spot, ...), custom_call_target="tpu_custom_call" | custom-call | flops 751435776 | bytes 6767616 | tf_op jit(solution)/shard_map/pallas_call | solution.py:83
  325.9 6.1 %collective-permute-done.64 = bf16[2,96,1664]{2,1,0:T(8,128)(2,1)S(1)} collective-permute-done((bf16[2,96,1664]{2,1,0:T(8,128)(2,1)}, bf16[2,96,1664]{2,1,0:T(8,128)(2,1)S(1)}, u32[]{:S(2)}, u32[]{:S(2)}) %collective-permute-start.64) | collective-permute-done | bytes 639008 | tf_op jit(solution)/shard_map/ppermute | solution.py:45
  344.1 6.6 %shard_map.499 = (f32[147,768]{1,0:T(8,128)}, bf16[147,768]{1,0:T(8,128)(2,1)}, bf16[147,768]{1,0:T(8,128)(2,1)}, bf16[2,147,576]{2,1,0:T(8,128)(2,1)}, bf16[147,768]{1,0:T(8,128)(2,1)}, /*index=5*/f32[2,768]{1,0:T(2,128)}) custom-call(f32[147,768]{1,0:T(8,128)} %get-tuple-element.329.stream_grad, bf16[147,768]{1,0:T(8,128)(2,1)} %get-tuple-element.330.own, ...), custom_call_target="tpu_custom_call" | custom-call | flops 595752192 | bytes 6000072 | tf_op jit(solution)/shard_map/pallas_call | solution.py:83
  359.4 5.9 %shard_map.502 = (bf16[2,96,1280]{2,1,0:T(8,128)(2,1)}, bf16[2,96,1280]{2,1,0:T(8,128)(2,1)}, bf16[2,96,1280]{2,1,0:T(8,128)(2,1)}, bf16[2,96,1280]{2,1,0:T(8,12...) custom-call(s32[2]{0:T(128)} %pad_add_fusion.1.spot, ...), custom_call_target="tpu_custom_call" | custom-call | flops 346816512 | bytes 5793024 | tf_op jit(solution)/shard_map/pallas_call | solution.py:83
  375.9 6.9 %collective-permute-done.73 = bf16[2,96,1280]{2,1,0:T(8,128)(2,1)S(1)} collective-permute-done((bf16[2,96,1280]{2,1,0:T(8,128)(2,1)}, bf16[2,96,1280]{2,1,0:T(8,128)(2,1)S(1)}, u32[]{:S(2)}, u32[]{:S(2)}) %collective-permute-start.73) | collective-permute-done | bytes 491552 | tf_op jit(solution)/shard_map/ppermute | solution.py:45
  389.6 14.6 %collective-permute-done.80.refs_10_ = bf16[96,1664]{1,0:T(8,128)(2,1)} collective-permute-done((bf16[96,1664]{1,0:T(8,128)(2,1)}, bf16[96,1664]{1,0:T(8,128)(2,1)}, u32[]{:S(2)}, u32[]{:S(2)}) %collective-permute-start.80) | collective-permute-done | bytes 319520 | tf_op jit(solution)/shard_map/ppermute | solution.py:60
  416.5 5.7 %collective-permute-done.84.refs_3_ = bf16[96,1280]{1,0:T(8,128)(2,1)S(1)} collective-permute-done((bf16[96,1280]{1,0:T(8,128)(2,1)S(1)}, bf16[96,1280]{1,0:T(8,128)(2,1)S(1)}, u32[]{:S(2)}, u32[]{:S(2)}) %collective-permute-start.84) | collective-permute-done | bytes 245792 | tf_op jit(solution)/shard_map/ppermute | solution.py:60
  422.2 7.0 %collective-permute-done.83.refs_2_ = bf16[96,1280]{1,0:T(8,128)(2,1)S(1)} collective-permute-done((bf16[96,1280]{1,0:T(8,128)(2,1)S(1)}, bf16[96,1280]{1,0:T(8,128)(2,1)S(1)}, u32[]{:S(2)}, u32[]{:S(2)}) %collective-permute-start.83) | collective-permute-done | bytes 245792 | tf_op jit(solution)/shard_map/ppermute | solution.py:60
  453.5 8.5 %shard_map.505 = (f32[1,128]{1,0:T(1,128)}, f32[7,96,192]{2,1,0:T(8,128)}, f32[7,96,192]{2,1,0:T(8,128)}, f32[7,96,192]{2,1,0:T(8,128)}, f32[5,192,96]{2,1,0:T(8...) custom-call(s32[2]{0:T(128)} %pad_add_fusion.place, ...), custom_call_target="tpu_custom_call" | custom-call | bytes 14871552 | tf_op jit(solution)/shard_map/pallas_call | solution.py:83
  (518 shorter events, 243.0 us)
Async XLA Ops:
  8.2 33.9 %collective-permute-start.2 = (bf16[96,1280]{1,0:T(8,128)(2,1)}, bf16[96,1280]{1,0:T(8,128)(2,1)}, u32[]{:S(2)}, u32[]{:S(2)}) collective-permute-start(bf16[96,1280]{1,0:T(8,128)(2,1)} %concatenate.67), channel_id=1, source_target_pairs={{0,24},{8,0},{16,8},{24,16},{1,25},{9,1},{17,9},{25,17},{2,26},{10... | collective-permute-start | bytes 737288 | tf_op jit(solution)/shard_map/ppermute | solution.py:60
  13.2 29.4 %collective-permute-start.1 = (bf16[96,1280]{1,0:T(8,128)(2,1)}, bf16[96,1280]{1,0:T(8,128)(2,1)}, u32[]{:S(2)}, u32[]{:S(2)}) collective-permute-start(bf16[96,1280]{1,0:T(8,128)(2,1)} %concatenate.67), channel_id=1, source_target_pairs={{0,16},{8,24},{16,0},{24,8},{1,17},{9,25},{17,1},{25,9},{2,18},{10... | collective-permute-start | bytes 737288 | tf_op jit(solution)/shard_map/ppermute | solution.py:60
  13.2 29.9 %collective-permute-start = (bf16[96,1280]{1,0:T(8,128)(2,1)}, bf16[96,1280]{1,0:T(8,128)(2,1)}, u32[]{:S(2)}, u32[]{:S(2)}) collective-permute-start(bf16[96,1280]{1,0:T(8,128)(2,1)} %concatenate.67), channel_id=1, source_target_pairs={{0,8},{8,16},{16,24},{24,0},{1,9},{9,17},{17,25},{25,1},{2,10},{10... | collective-permute-start | bytes 737288 | tf_op jit(solution)/shard_map/ppermute | solution.py:60
  14.2 31.8 %collective-permute-start.6 = (bf16[1,96,1280]{2,1,0:T(8,128)(2,1)}, bf16[1,96,1280]{2,1,0:T(8,128)(2,1)}, u32[]{:S(2)}, u32[]{:S(2)}) collective-permute-start(bf16[1,96,1280]{2,1,0:T(8,128)(2,1)} %bitcast.15.refs_0_), channel_id=1, source_target_pairs={{0,4},{4,0},{1,5},{5,1},{2,6},{6,2},{3,7},{7,3},{8,12},{12,8},{9,1... | collective-permute-start | bytes 737288 | tf_op jit(solution)/shard_map/ppermute | solution.py:45
  15.8 32.5 %collective-permute-start.5 = (bf16[1,96,1280]{2,1,0:T(8,128)(2,1)}, bf16[1,96,1280]{2,1,0:T(8,128)(2,1)}, u32[]{:S(2)}, u32[]{:S(2)}) collective-permute-start(bf16[1,96,1280]{2,1,0:T(8,128)(2,1)} %bitcast.15.refs_0_), channel_id=1, source_target_pairs={{0,2},{2,0},{1,3},{3,1},{4,6},{6,4},{5,7},{7,5},{8,10},{10,8},{9,1... | collective-permute-start | bytes 737288 | tf_op jit(solution)/shard_map/ppermute | solution.py:45
  57.0 32.1 %collective-permute-start.21 = (bf16[96,1664]{1,0:T(8,128)(2,1)S(1)}, bf16[96,1664]{1,0:T(8,128)(2,1)S(1)}, u32[]{:S(2)}, u32[]{:S(2)}) collective-permute-start(bf16[96,1664]{1,0:T(8,128)(2,1)S(1)} %copy-done.11), channel_id=1, source_target_pairs={{0,16},{8,24},{16,0},{24,8},{1,17},{9,25},{17,1},{25,9},{2,18},{10... | collective-permute-start | bytes 958472 | tf_op jit(solution)/shard_map/ppermute | solution.py:60
  57.7 34.4 %collective-permute-start.20 = (bf16[96,1664]{1,0:T(8,128)(2,1)S(1)}, bf16[96,1664]{1,0:T(8,128)(2,1)S(1)}, u32[]{:S(2)}, u32[]{:S(2)}) collective-permute-start(bf16[96,1664]{1,0:T(8,128)(2,1)S(1)} %copy-done.11), channel_id=1, source_target_pairs={{0,8},{8,16},{16,24},{24,0},{1,9},{9,17},{17,25},{25,1},{2,10},{10... | collective-permute-start | bytes 958472 | tf_op jit(solution)/shard_map/ppermute | solution.py:60
  64.5 27.1 %collective-permute-start.3 = (bf16[147,768]{1,0:T(8,128)(2,1)S(1)}, bf16[147,768]{1,0:T(8,128)(2,1)S(1)}, u32[]{:S(2)}, u32[]{:S(2)}) collective-permute-start(bf16[147,768]{1,0:T(8,128)(2,1)S(1)} %slice_select_fusion.6), channel_id=1, source_target_pairs={{0,16},{8,24},{16,0},{24,8},{1,17},{9,25},{17,1},{25,9},{2,18},{10... | collective-permute-start | bytes 677384 | tf_op jit(solution)/shard_map/ppermute | solution.py:60
  92.4 39.5 %collective-permute-start.24 = (bf16[3,96,1664]{2,1,0:T(8,128)(2,1)S(1)}, bf16[3,96,1664]{2,1,0:T(8,128)(2,1)}, u32[]{:S(2)}, u32[]{:S(2)}) collective-permute-start(bf16[3,96,1664]{2,1,0:T(8,128)(2,1)S(1)} %pad_maximum_fusion.2.refs_5_), channel_id=1, source_target_pairs={{0,4},{4,0},{1,5},{5,1},{2,6},{6,2},{3,7},{7,3},{8,12},{12,8},{9,1... | collective-permute-start | bytes 2875400 | tf_op jit(solution)/shard_map/ppermute | solution.py:45
  92.9 45.8 %collective-permute-start.23 = (bf16[3,96,1664]{2,1,0:T(8,128)(2,1)S(1)}, bf16[3,96,1664]{2,1,0:T(8,128)(2,1)}, u32[]{:S(2)}, u32[]{:S(2)}) collective-permute-start(bf16[3,96,1664]{2,1,0:T(8,128)(2,1)S(1)} %pad_maximum_fusion.2.refs_5_), channel_id=1, source_target_pairs={{0,2},{2,0},{1,3},{3,1},{4,6},{6,4},{5,7},{7,5},{8,10},{10,8},{9,1... | collective-permute-start | bytes 2875400 | tf_op jit(solution)/shard_map/ppermute | solution.py:45
  103.6 45.8 %collective-permute-start.35 = (bf16[64,1920]{1,0:T(8,128)(2,1)}, bf16[64,1920]{1,0:T(8,128)(2,1)}, u32[]{:S(2)}, u32[]{:S(2)}) collective-permute-start(bf16[64,1920]{1,0:T(8,128)(2,1)} %pad_maximum_fusion.7), channel_id=1, source_target_pairs={{0,24},{8,0},{16,8},{24,16},{1,25},{9,1},{17,9},{25,17},{2,26},{10... | collective-permute-start | bytes 737288 | tf_op jit(solution)/shard_map/ppermute | solution.py:60
  121.8 29.1 %collective-permute-start.34 = (bf16[64,1920]{1,0:T(8,128)(2,1)}, bf16[64,1920]{1,0:T(8,128)(2,1)}, u32[]{:S(2)}, u32[]{:S(2)}) collective-permute-start(bf16[64,1920]{1,0:T(8,128)(2,1)} %pad_maximum_fusion.7), channel_id=1, source_target_pairs={{0,16},{8,24},{16,0},{24,8},{1,17},{9,25},{17,1},{25,9},{2,18},{10... | collective-permute-start | bytes 737288 | tf_op jit(solution)/shard_map/ppermute | solution.py:60
  152.3 53.9 %collective-permute-start.42 = (bf16[588,1024]{1,0:T(8,128)(2,1)}, bf16[588,1024]{1,0:T(8,128)(2,1)}, u32[]{:S(2)}, u32[]{:S(2)}) collective-permute-start(bf16[588,1024]{1,0:T(8,128)(2,1)} %pad_maximum_fusion.1), channel_id=1, source_target_pairs={{0,16},{8,24},{16,0},{24,8},{1,17},{9,25},{17,1},{25,9},{2,18},{10... | collective-permute-start | bytes 3612680 | tf_op jit(solution)/shard_map/ppermute | solution.py:60
  164.1 42.2 %collective-permute-start.32 = (bf16[1,32,1920]{2,1,0:T(8,128)(2,1)}, bf16[1,32,1920]{2,1,0:T(8,128)(2,1)S(1)}, u32[]{:S(2)}, u32[]{:S(2)}) collective-permute-start(bf16[1,32,1920]{2,1,0:T(8,128)(2,1)} %slice.262), channel_id=1, source_target_pairs={{0,2},{2,0},{1,3},{3,1},{4,6},{6,4},{5,7},{7,5},{8,10},{10,8},{9,1... | collective-permute-start | bytes 368648 | tf_op jit(solution)/shard_map/ppermute | solution.py:45
  173.3 32.9 %collective-permute-start.39 = (bf16[3,32,1920]{2,1,0:T(8,128)(2,1)S(1)}, bf16[3,32,1920]{2,1,0:T(8,128)(2,1)S(1)}, u32[]{:S(2)}, u32[]{:S(2)}) collective-permute-start(bf16[3,32,1920]{2,1,0:T(8,128)(2,1)S(1)} %slice.264), channel_id=1, source_target_pairs={{0,2},{2,0},{1,3},{3,1},{4,6},{6,4},{5,7},{7,5},{8,10},{10,8},{9,1... | collective-permute-start | bytes 1105928 | tf_op jit(solution)/shard_map/ppermute | solution.py:45
  174.5 31.8 %collective-permute-start.38 = (bf16[3,32,1920]{2,1,0:T(8,128)(2,1)S(1)}, bf16[3,32,1920]{2,1,0:T(8,128)(2,1)S(1)}, u32[]{:S(2)}, u32[]{:S(2)}) collective-permute-start(bf16[3,32,1920]{2,1,0:T(8,128)(2,1)S(1)} %slice.263), channel_id=1, source_target_pairs={{0,4},{4,0},{1,5},{5,1},{2,6},{6,2},{3,7},{7,3},{8,12},{12,8},{9,1... | collective-permute-start | bytes 1105928 | tf_op jit(solution)/shard_map/ppermute | solution.py:45
  176.0 30.2 %collective-permute-start.31 = (bf16[1,32,1920]{2,1,0:T(8,128)(2,1)S(1)}, bf16[1,32,1920]{2,1,0:T(8,128)(2,1)S(1)}, u32[]{:S(2)}, u32[]{:S(2)}) collective-permute-start(bf16[1,32,1920]{2,1,0:T(8,128)(2,1)S(1)} %copy-done.67), channel_id=1, source_target_pairs={{0,4},{4,0},{1,5},{5,1},{2,6},{6,2},{3,7},{7,3},{8,12},{12,8},{9,1... | collective-permute-start | bytes 368648 | tf_op jit(solution)/shard_map/ppermute | solution.py:45
  261.6 34.5 %collective-permute-start.53 = (bf16[2,64,1408]{2,1,0:T(8,128)(2,1)}, bf16[2,64,1408]{2,1,0:T(8,128)(2,1)S(1)}, u32[]{:S(2)}, u32[]{:S(2)}) collective-permute-start(bf16[2,64,1408]{2,1,0:T(8,128)(2,1)} %get-tuple-element.320), channel_id=1, source_target_pairs={{0,2},{2,0},{1,3},{3,1},{4,6},{6,4},{5,7},{7,5},{8,10},{10,8},{9,1... | collective-permute-start | bytes 1081352 | tf_op jit(solution)/shard_map/ppermute | solution.py:45
  263.1 33.5 %collective-permute-start.54 = (bf16[2,64,1408]{2,1,0:T(8,128)(2,1)}, bf16[2,64,1408]{2,1,0:T(8,128)(2,1)S(1)}, u32[]{:S(2)}, u32[]{:S(2)}) collective-permute-start(bf16[2,64,1408]{2,1,0:T(8,128)(2,1)} %get-tuple-element.321), channel_id=1, source_target_pairs={{0,4},{4,0},{1,5},{5,1},{2,6},{6,2},{3,7},{7,3},{8,12},{12,8},{9,1... | collective-permute-start | bytes 1081352 | tf_op jit(solution)/shard_map/ppermute | solution.py:45
  296.1 28.0 %collective-permute-start.56 = (bf16[2,64,512]{2,1,0:T(8,128)(2,1)}, bf16[2,64,512]{2,1,0:T(8,128)(2,1)S(1)}, u32[]{:S(2)}, u32[]{:S(2)}) collective-permute-start(bf16[2,64,512]{2,1,0:T(8,128)(2,1)} %get-tuple-element.332), channel_id=1, source_target_pairs={{0,2},{2,0},{1,3},{3,1},{4,6},{6,4},{5,7},{7,5},{8,10},{10,8},{9,1... | collective-permute-start | bytes 393224 | tf_op jit(solution)/shard_map/ppermute | solution.py:45
  296.6 28.4 %collective-permute-start.57 = (bf16[2,64,512]{2,1,0:T(8,128)(2,1)}, bf16[2,64,512]{2,1,0:T(8,128)(2,1)S(1)}, u32[]{:S(2)}, u32[]{:S(2)}) collective-permute-start(bf16[2,64,512]{2,1,0:T(8,128)(2,1)} %get-tuple-element.333), channel_id=1, source_target_pairs={{0,4},{4,0},{1,5},{5,1},{2,6},{6,2},{3,7},{7,3},{8,12},{12,8},{9,1... | collective-permute-start | bytes 393224 | tf_op jit(solution)/shard_map/ppermute | solution.py:45
  337.5 27.8 %collective-permute-start.75 = (bf16[2,96,1664]{2,1,0:T(8,128)(2,1)}, bf16[2,96,1664]{2,1,0:T(8,128)(2,1)S(1)}, u32[]{:S(2)}, u32[]{:S(2)}) collective-permute-start(bf16[2,96,1664]{2,1,0:T(8,128)(2,1)} %get-tuple-element.392), channel_id=1, source_target_pairs={{0,2},{2,0},{1,3},{3,1},{4,6},{6,4},{5,7},{7,5},{8,10},{10,8},{9,1... | collective-permute-start | bytes 1916936 | tf_op jit(solution)/shard_map/ppermute | solution.py:45
  338.3 27.0 %collective-permute-start.76 = (bf16[2,96,1664]{2,1,0:T(8,128)(2,1)}, bf16[2,96,1664]{2,1,0:T(8,128)(2,1)S(1)}, u32[]{:S(2)}, u32[]{:S(2)}) collective-permute-start(bf16[2,96,1664]{2,1,0:T(8,128)(2,1)} %get-tuple-element.393), channel_id=1, source_target_pairs={{0,4},{4,0},{1,5},{5,1},{2,6},{6,2},{3,7},{7,3},{8,12},{12,8},{9,1... | collective-permute-start | bytes 1916936 | tf_op jit(solution)/shard_map/ppermute | solution.py:45
  374.4 29.8 %collective-permute-start.71 = (bf16[2,96,1280]{2,1,0:T(8,128)(2,1)}, bf16[2,96,1280]{2,1,0:T(8,128)(2,1)S(1)}, u32[]{:S(2)}, u32[]{:S(2)}) collective-permute-start(bf16[2,96,1280]{2,1,0:T(8,128)(2,1)} %get-tuple-element.386), channel_id=1, source_target_pairs={{0,2},{2,0},{1,3},{3,1},{4,6},{6,4},{5,7},{7,5},{8,10},{10,8},{9,1... | collective-permute-start | bytes 1474568 | tf_op jit(solution)/shard_map/ppermute | solution.py:45
  (157 other events, 1650.7 us)

commit v5 on v4

--- a/solution.py
+++ b/solution.py
@@ -27,7 +27,9 @@
 SWAP = [(0, 1), (1, 0)]
 ACROSS = [(0, 3), (1, 2), (2, 1), (3, 0)]
 LANES = 128
-VMEM_ROOM = 56 * 2**20
+NORM_ROWS = 64
+VMEM_ROOM = 16 * 2**20
+WIDE_ROOM = 56 * 2**20
 SQRT_HALF = 0.5**0.5
 DENSITY = (2.0 * np.pi) ** -0.5
 DATA = ("z", "y")
@@ -77,7 +79,7 @@
     return lax.optimization_barrier((value,) + others)[0]
 
 
-def vmem_call(body, outs, *ins, scalars=(), scratch=(), flops=0):
+def vmem_call(body, outs, *ins, scalars=(), scratch=(), flops=0, room=VMEM_ROOM):
     shapes = [jax.ShapeDtypeStruct(shape, kind) for shape, kind in outs]
     moved = sum(int(np.prod(a.shape)) * a.dtype.itemsize for a in [*ins, *shapes])
     return pl.pallas_call(
@@ -87,80 +89,150 @@
         + [pl.BlockSpec(memory_space=pltpu.VMEM)] * len(ins),
         out_specs=[pl.BlockSpec(memory_space=pltpu.VMEM)] * len(shapes),
         scratch_shapes=list(scratch),
-        compiler_params=pltpu.CompilerParams(vmem_limit_bytes=VMEM_ROOM),
+        compiler_params=pltpu.CompilerParams(vmem_limit_bytes=room),
         cost_estimate=pl.CostEstimate(flops=flops, bytes_accessed=moved, transcendentals=0),
     )(*scalars, *ins)
 
 
 class Spread:
-    def __init__(self, blob, *earlier):
-        self.half = blob.shape[0] // 2
-        self.blob = after(blob, *earlier)
-        self.near = self.plane(self.blob[None])
-
-    def plane(self, part):
-        from_x, from_y = swap(part, "x"), swap(part, "y")
-        corner = (swap(from_x[:, : self.half], "y"), swap(from_y[:, self.half :], "x"))
-        return from_x, from_y, *corner
+    def __init__(self, blob, favour):
+        self.favour = favour
+        self.blob = blob
+        self.near = self.sides(blob[None])
+
+    def sides(self, part):
+        return swap(part, "x"), swap(part, "y")
+
+    def corners(self, from_x, from_y, favour):
+        low_part, high_part = from_y[:favour], from_x[favour:]
+        return [
+            swap(part, axis) for part, axis in ((low_part, "x"), (high_part, "y")) if part.shape[0]
+        ]
+
+    def near_corners(self, *earlier):
+        sides = lax.optimization_barrier((*self.near, *earlier))[:2]
+        self.near = (*self.near, *self.corners(*sides, self.favour - 1))
 
     def along_z(self, *earlier):
         blob = after(self.blob, *earlier)
         self.moved = [shift(blob, "z", step) for step in (1, 2, 3)]
 
-    def round_plane(self, *earlier):
-        self.stack = after(jnp.stack(self.moved), *earlier)
-        self.far = self.plane(self.stack)
+    def far_sides(self, *earlier):
+        self.stack = after(jnp.stack(lax.optimization_barrier((*self.moved, *earlier))[:3]), *earlier)
+        self.far = self.sides(self.stack)
+
+    def far_corners(self, *earlier):
+        sides = lax.optimization_barrier((*self.far, *earlier))[:2]
+        self.far = (*self.far, *self.corners(*sides, self.favour))
 
     def whole(self, widths):
         rows = self.blob.shape[0]
         x, y, z = (lax.axis_index(axis) for axis in ("x", "y", "z"))
         starts = np.cumsum([0, *widths])
 
+        parts = [(self.blob[None], 0, 0, (0,)), (self.stack, 0, 0, (1, 2, 3))]
+        for sides, steps, favour in (
+            (self.near, (0,), self.favour - 1),
+            (self.far, (1, 2, 3), self.favour),
+        ):
+            parts += [(sides[0], 1, 0, steps), (sides[1], 0, 1, steps)]
+            corners = [part for part in (steps[:favour], steps[favour:]) if part]
+            parts += [(part, 1, 1, cut) for part, cut in zip(sides[2:], corners)]
+        count = len(parts)
+
         def body(spot, *refs):
             here_x, here_y, here_z = spot[0], spot[1], spot[2]
-            outs = refs[10:]
-            for group in (0, 5):
-                own, from_x, from_y, low_corner, high_corner = refs[group : group + 5]
-                for number in range(own.shape[0]):
-                    level = lax.rem(here_z - number + 3 if group else here_z + 4, 4)
-                    for ref, at_x, at_y, first in (
-                        (own, here_x, here_y, 0),
-                        (from_x, 1 - here_x, here_y, 0),
-                        (from_y, here_x, 1 - here_y, 0),
-                        (low_corner, 1 - here_x, 1 - here_y, 0),
-                        (high_corner, 1 - here_x, 1 - here_y, self.half),
-                    ):
-                        count = ref.shape[1]
-                        for out, start, width in zip(outs, starts, widths):
-                            out[at_x, level, at_y, first : first + count, :] = ref[
-                                number, :, start : start + width
-                            ]
-
-        parts = (self.blob[None], *self.near, self.stack, *self.far)
+            outs = refs[count:]
+            for ref, (_, far_x, far_y, steps) in zip(refs, parts):
+                at_x = 1 - here_x if far_x else here_x
+                at_y = 1 - here_y if far_y else here_y
+                for number, step in enumerate(steps):
+                    level = lax.rem(here_z + (4 - step), 4)
+                    for out, first, width in zip(outs, starts, widths):
+                        out[at_x, level, at_y] = ref[number, :, first : first + width]
+
         outs = [((2, 4, 2, rows, width), self.blob.dtype) for width in widths]
-        wholes = vmem_call(body, outs, *parts, scalars=(jnp.stack([x, y, z]),))
+        wholes = vmem_call(
+            body, outs, *(part[0] for part in parts), scalars=(jnp.stack([x, y, z]),)
+        )
         return [whole.reshape(2, 8 * rows, -1) for whole in wholes]
 
 
-def spread_all(blobs, widths, picked):
+def pack_first(place, enc_in, enc_out, patch, norms):
+    rows, width = enc_in.shape[1:]
+    half_rows, half_columns = patch.shape[0] // 2, patch.shape[1] // 2
+    columns = half_columns + LANES + 4 * width
+
+    def body(place, enc_in, enc_out, patch, norms, blob):
+        cuts = [
+            jnp.where(place[1] == 0, patch[cut, :half_columns], patch[cut, half_columns:])
+            for cut in (slice(0, half_rows), slice(half_rows, 2 * half_rows))
+        ]
+        blob[:, :half_columns] = low(jnp.where(place[0] == 0, *cuts))
+        start = half_columns
+        blob[:, start : start + LANES] = jnp.zeros((rows, LANES), NARROW_TYPE)
+        blob[: norms.shape[0], start : start + LANES] = low(norms[...])
+        start += LANES
+        for block in range(3):
+            blob[:, start : start + width] = low(enc_in[block])
+            start += width
+        blob[:, start:] = low(enc_out[0].T)
+
+    return vmem_call(
+        body, [((rows, columns), NARROW_TYPE)], enc_in, enc_out, patch, norms, scalars=(place,)
+    )[0]
+
+
+def pack_rest(place, enc_in, enc_out, dec_in, dec_out, embed, head):
+    rows, width = enc_in.shape[1:]
+    rows_dec, width_dec = dec_in.shape[1:]
+    quarter = embed.shape[1] // 4
+
+    def body(place, enc_in, enc_out, dec_in, dec_out, embed, head, second, third):
+        for block in range(4):
+            second[:, block * width : (block + 1) * width] = low(enc_in[3 + block])
+            second[:, (4 + block) * width : (5 + block) * width] = low(enc_out[1 + block].T)
+        cuts = [embed[:, n * quarter : (n + 1) * quarter] for n in range(4)]
+        pairs = [jnp.where(place[1] == 0, cuts[n], cuts[n + 1]) for n in (0, 2)]
+        second[:, 8 * width :] = low(jnp.where(place[0] == 0, *pairs))
+        for block in range(7):
+            third[:, block * width_dec : (block + 1) * width_dec] = low(dec_in[block])
+        for block in range(5):
+            third[:, (7 + block) * width_dec : (8 + block) * width_dec] = low(dec_out[block])
+        third[:, 12 * width_dec :] = low(head[...])
+
+    outs = [
+        ((rows, 8 * width + quarter), NARROW_TYPE),
+        ((rows_dec, 12 * width_dec + head.shape[1]), NARROW_TYPE),
+    ]
+    return vmem_call(body, outs, enc_in, enc_out, dec_in, dec_out, embed, head, scalars=(place,))
+
+
+def spread_all(blobs, widths, arrived, last):
     sizes = tuple(lax.axis_size(axis) for axis in ("x", "z", "y"))
     if sizes != (2, 4, 2):
         wholes = [lax.all_gather(blob, ("x", "z", "y")) for blob in blobs]
         wholes = [whole.reshape(2, -1, whole.shape[-1]) for whole in wholes]
         pieces = [columns_of(whole, width) for whole, width in zip(wholes, widths)]
-        return pieces, [wholes[0]] * 4
-    first = Spread(blobs[0])
+        marks = [wholes[0]] * 4
+        return pieces, marks, last(marks)
+    first = Spread(blobs[0], 2)
     first.along_z()
-    second, third = (Spread(blob, picked) for blob in blobs[1:])
+    second, third = (Spread(blob, favour) for blob, favour in ((blobs[1], 1), (blobs[2], 2)))
+    for group in (first, second, third):
+        group.near_corners()
     second.along_z(*first.moved)
-    first.round_plane()
-    third.along_z(*first.far[:2])
-    second.moved = [after(moved, *first.far[:2]) for moved in second.moved]
-    second.round_plane(*first.far)
-    third.moved = [after(moved, *second.far[:2]) for moved in third.moved]
-    third.round_plane(*second.far)
+    third.along_z(*first.moved)
+    first.far_sides(*first.near, *second.near[:2], *third.near[:2], arrived)
+    first.far_corners(*second.near[2:], *third.near[2:])
+    second.far_sides(*first.far, *third.moved)
+    second.far_corners()
+    third.far_sides(*second.far)
+    marks = (first.stack, first.far[0], first.far[2], third.moved[2])
+    moved = last(marks)
+    third.far_corners(moved)
     pieces = [group.whole(width) for group, width in zip((first, second, third), widths)]
-    return pieces, [first.stack, first.far[0], first.far[2], second.far[0]]
+    return pieces, marks, moved
 
 
 def share(pieces, rows, patch=None, norms=None):
@@ -173,7 +245,9 @@
             cut = low(product("ld,lc->dc", *patch)).reshape(2 * levels, 2, rows, -1)
             cuts.append(cut.transpose(1, 0, 2, 3).reshape(2, 2 * levels * rows, -1))
         if norms is not None:
-            cuts.append(norms.reshape(2, 2 * levels * rows, -1))
+            norms = low(norms[:, :4]).reshape(2 * levels, 2, -1).transpose(1, 0, 2)
+            norms = jnp.pad(norms, ((0, 0), (0, 0), (0, rows * LANES - norms.shape[2])))
+            cuts.append(norms.reshape(2, 2 * levels * rows, LANES))
         cuts += [low(product("ld,xlc->xdc", left, right)) for left, right in pieces]
         return (jnp.concatenate(cuts, 2).reshape(4 * levels, rows, -1),)
     extra = []
@@ -216,13 +290,16 @@
             used, column = 2, width
         if norms is not None:
             source = ins[used]
-            count = source.shape[2]
             for far_x in (0, 1):
                 for far_y in (0, 1):
                     at_x, at_y = spot[0] ^ far_x, spot[1] ^ far_y
                     for level in range(levels):
+                        values = source[2 * (2 * level + at_y) + at_x]
+                        values = jnp.concatenate(
+                            [values, jnp.zeros((rows - values.shape[0], LANES), FLOAT_TYPE)]
+                        )
                         window = (slice(None), slice(column, column + LANES))
-                        put(far_x, far_y, level, window, source[at_x, 2 * level + at_y])
+                        put(far_x, far_y, level, window, low(values))
             used, column = used + 1, column + LANES
         for number, (_, right) in enumerate(pieces):
             left_ref, right_ref = ins[used + 2 * number], ins[used + 2 * number + 1]
@@ -611,19 +688,30 @@
     )
 
 
-def encoder_end(stream_grad, own, other, stream, gains, place):
+def encoder_end(stream_grad, own, other, stream, gains, place, norms, mask_grad):
     length, features = stream.shape
     half = features // 2
-
-    def body(place, stream_grad, own, other, stream, gains, grad_mine, norm_grads):
+    width_dec = mask_grad.shape[1]
+    rows = (6 * features + 7 * width_dec) // LANES
+
+    def body(place, stream_grad, own, other, stream, gains, *refs):
+        norms, (mask, grad_mine, gathered) = refs[:5], refs[5:]
         upstream = own[...].astype(FLOAT_TYPE) + other[...].astype(FLOAT_TYPE)
         input_grad, sums = norm_back(upstream, stream[...], gains, 0)
-        norm_grads[0:1, :], norm_grads[1:2, :] = sums
         grad = low(stream_grad[...] + input_grad)
         grad_mine[...] = jnp.where(place[0] == 0, grad[:, :half], grad[:, half:])
-
-    outs = [((length, half), NARROW_TYPE), ((2, features), FLOAT_TYPE)]
-    return vmem_call(body, outs, stream_grad, own, other, stream, gains, scalars=(place,))
+        gathered[...] = jnp.zeros_like(gathered)
+        row = 0
+        for source in (*sums, *(ref[n : n + 1, :] for ref in norms for n in (0, 1)), mask[...]):
+            for start in range(0, source.shape[1], LANES):
+                gathered[row // 4, row % 4 : row % 4 + 1, :] = source[:, start : start + LANES]
+                row += 1
+
+    groups = max(rows, NORM_ROWS) // 4
+    outs = [((length, half), NARROW_TYPE), ((groups, 8, LANES), FLOAT_TYPE)]
+    return vmem_call(
+        body, outs, stream_grad, own, other, stream, gains, *norms, mask_grad, scalars=(place,)
+    )
 
 
 def adam_update(weight, moment, second, gradient, step_rate, decay_rate):
@@ -670,17 +758,16 @@
     return sums, embed, square
 
 
-def sum_late(terms, embed, square, loss_part, valid_count, patch_width):
-    count = len(terms)
+def sum_late(terms, first_terms, embed, square, loss_part, valid_count, patch_width):
+    count, both_count = len(terms), len(terms) + len(first_terms)
     rows, columns = terms[0].shape
-    split = patch_width + LANES
+    split = first_terms[0].shape[1]
 
     def body(*refs):
-        embed, square, loss, valid, rest, exchanged, totals = refs[count:]
-        total = add(*(ref[...] for ref in refs[:count]))
-        kept = total[:, split:]
+        embed, square, loss, valid, rest, exchanged, totals = refs[both_count:]
+        kept = add(*(ref[...] for ref in refs[:count]))
         rest[...] = kept
-        sent = low(total[:, :split])
+        sent = low(add(*(ref[...] for ref in refs[count:both_count])))
         exchanged[:, :split] = sent
         exchanged[:, split:] = embed[...]
         sent = sent.astype(FLOAT_TYPE)
@@ -697,11 +784,13 @@
         )
 
     outs = [
-        ((rows, columns - split), FLOAT_TYPE),
+        ((rows, columns), FLOAT_TYPE),
         ((rows, split + embed.shape[1]), NARROW_TYPE),
         ((1, LANES), FLOAT_TYPE),
     ]
-    return vmem_call(body, outs, *terms, embed, square, loss_part, valid_count.reshape(1, 1))
+    return vmem_call(
+        body, outs, *terms, *first_terms, embed, square, loss_part, valid_count.reshape(1, 1)
+    )
 
 
 def adam_all(place, totals, masters, moments, seconds, sums, exchanged, norm_sum):
@@ -778,7 +867,7 @@
 
     outs = [((1, LANES), FLOAT_TYPE)] + [(array.shape, FLOAT_TYPE) for array in flat]
     scalars, *results = vmem_call(
-        body, outs, totals, *flat, *sums, *exchanged, view(norm_sum, 7), scalars=(place,)
+        body, outs, totals, *flat, *sums, *exchanged, view(norm_sum, 7), scalars=(place,), room=WIDE_ROOM
     )
     return scalars, [unview(result, index // 3) for index, result in enumerate(results)]
 
@@ -886,30 +975,23 @@
 
     patch_rows = patch_embed.shape[0] // 2
     half_enc, quarter_dec = width_enc // 2, width_dec // 4
-    patch_piece = lax.dynamic_slice(
-        low(patch_embed), (x * patch_rows, c * half_enc), (patch_rows, half_enc)
-    )
-    embed_piece = lax.dynamic_slice(
-        low(decoder_embed), (0, (2 * x + c) * quarter_dec), (rows_enc, quarter_dec)
-    )
     norm_share, norm_room = norm_params.shape[0], rows_enc * LANES
-    norm_piece = jnp.pad(low(norm_params), (0, norm_room - norm_share)).reshape(rows_enc, LANES)
-    enc_in_low = low(encoder_in).reshape(rows_enc, -1)
-    enc_out_low = low(encoder_out).transpose(2, 0, 1).reshape(rows_enc, -1)
-    dec_in_low = low(decoder_in).reshape(rows_dec, -1)
-    dec_out_low = low(decoder_out).transpose(2, 0, 1).reshape(rows_dec, -1)
-    head_low = low(pixel_head)
-    first_blob = jnp.concatenate(
-        [patch_piece, norm_piece, enc_in_low[:, : 3 * part_enc], enc_out_low[:, :part_enc]], 1
-    )
-    second_blob = jnp.concatenate(
-        [enc_in_low[:, 3 * part_enc :], enc_out_low[:, part_enc:], embed_piece], 1
-    )
-    third_blob = jnp.concatenate([dec_in_low, dec_out_low, head_low], 1)
+    place = jnp.stack([x, c])
+    enc_in_blocks = encoder_in.transpose(1, 0, 2)
+    first_blob = pack_first(place, enc_in_blocks, encoder_out, patch_embed, norm_params.reshape(-1, LANES))
+    second_blob, third_blob = pack_rest(
+        after(place, first_blob),
+        enc_in_blocks,
+        encoder_out,
+        decoder_in.transpose(1, 0, 2),
+        decoder_out.transpose(0, 2, 1),
+        decoder_embed,
+        pixel_head,
+    )
     widths = (
         (half_enc, LANES, 3 * part_enc, part_enc),
         (4 * part_enc, 4 * part_enc, quarter_dec),
-        (3 * part_dec, 4 * part_dec, part_dec, 4 * part_dec, head_low.shape[1]),
+        (3 * part_dec, 4 * part_dec, part_dec, 4 * part_dec, pixel_head.shape[1]),
     )
 
     buf_rows = data_size * -(-(slot_total * vis_count) // data_size)
@@ -920,19 +1002,36 @@
     def shown_of(visible_row):
         return jnp.any(one_hot(visible_row, tokens), axis=0).astype(FLOAT_TYPE)
 
-    start = after(x, first_blob)
-    away = slot_total - 1 - start
-    own_slot, away_slot = pick(pixels, start), pick(pixels, away)
-
-    def seen_of(slot, rows):
-        return low(product("vt,tp->vp", low(one_hot(pick(visible, slot), tokens)), rows))
-
-    visible_row = jnp.where(use_own, pick(visible, start), shift(pick(visible, away), "z", half_step))
-    seen_away = shift(halves_of(seen_of(away, away_slot), c), "z", half_step)
-
-    (first_all, second_all, third_all), marks = spread_all(
-        (first_blob, second_blob, third_blob), widths, own_slot
-    )
+    away = slot_total - 1 - x
+    visible_moved = shift(pick(visible, away), "z", half_step)
+    visible_row = jnp.where(use_own, pick(visible, x), visible_moved)
+
+    def packs_of(marks):
+        start = after(x, marks[0])
+        own_slot, away_slot = pick(pixels, start), pick(pixels, slot_total - 1 - start)
+
+        def seen_of(slot, rows):
+            return low(product("vt,tp->vp", low(one_hot(pick(visible, slot), tokens)), rows))
+
+        seen_away = shift(halves_of(seen_of(away, away_slot), c), "z", half_step)
+        seen_away = both(seen_away, "c", c, 1)
+        seen.append(jnp.where(use_own, seen_of(x, own_slot), seen_away))
+
+        def pixels_of(slot, rows):
+            place = after(c, marks[1])
+            half = pix_width // 2
+            cols = [halves_of(rows[:, first : first + half], place) for first in (0, half)]
+            return jnp.concatenate(cols + [low(pick(valid, slot))], 1)
+
+        seen.append(pixels_of(start, own_slot))
+        away_pack = pixels_of(slot_total - 1 - start, away_slot)
+        return shift(after(away_pack, marks[3]), "z", half_step)
+
+    seen = []
+    (first_all, second_all, third_all), marks, pack_moved = spread_all(
+        (first_blob, second_blob, third_blob), widths, visible_moved, packs_of
+    )
+    seen_rows, own_pack = seen
 
     patch_all, norm_all, enc_qkv, enc_proj = first_all
     enc_up, enc_down, embed_all = second_all
@@ -949,9 +1048,6 @@
     dec_gains = norm_full[6 * width_enc : 6 * width_enc + 6 * width_dec].reshape(6, width_dec)
     mask_token = norm_full[6 * width_enc + 6 * width_dec : 6 * width_enc + 7 * width_dec]
 
-    seen_rows = jnp.where(
-        use_own, seen_of(after(start, marks[0]), own_slot), both(seen_away, "c", c, 1)
-    )
     chosen = low(one_hot(visible_row, tokens))
     hidden_row = (1.0 - shown_of(visible_row))[:, None]
 
@@ -960,15 +1056,6 @@
     counted = counted * alive.astype(FLOAT_TYPE)[:, None]
     valid_count = jnp.sum(counted[:, :, None] * valid.astype(FLOAT_TYPE))
     valid_count = valid_count * (pix_width // patch_positions)
-
-    def pixels_of(slot, rows):
-        place = after(c, marks[1])
-        half = pix_width // 2
-        cols = [halves_of(rows[:, first : first + half], place) for first in (0, half)]
-        return jnp.concatenate(cols + [low(pick(valid, slot))], 1)
-
-    own_pack, away_pack = pixels_of(start, own_slot), pixels_of(away, away_slot)
-    pack_moved = shift(after(away_pack, marks[3]), "z", half_step)
 
     enc_stream = both(product("lp,pd->ld", seen_rows, patch_all), "c", c, 1)
     enc_stream = enc_stream + angles_of(visible_row, width_enc)
@@ -993,7 +1080,7 @@
     )
     dec_middle, partial = mlp_fwd(dec_stream, partial, swap(partial), dec_gains, dec_up, dec_down)
 
-    pixel_pack = jnp.where(use_own, own_pack, after(pack_moved, dec_stream))
+    pixel_pack = jnp.where(use_own, own_pack, after(pack_moved, dec_triple))
     pixel_cols = pixel_pack[:, : pix_width // 2].astype(FLOAT_TYPE)
     valid_cols = pixel_pack[:, pix_width // 2 :].astype(FLOAT_TYPE)
     half_mean = jnp.mean(pixel_cols, -1, keepdims=True)
@@ -1073,49 +1160,47 @@
         enc_proj,
         enc_heads,
     )
-    other_partial = after(swap(partial), *enc_tail.second(), *dec_attn.moved)
-    patch_right, enc_norms_one = encoder_end(
-        stream_grad, partial, other_partial, enc_stream, enc_gains, c[None]
-    )
-    norm_pieces = jnp.concatenate(
-        [
-            grads.reshape(-1)
-            for grads in (
-                enc_norms_one,
-                enc_norms_two,
-                enc_norms_three,
-                dec_norms_one,
-                dec_norms_two,
-                dec_norms_three,
-                mask_grad,
-            )
-        ]
-    )
-    norm_total = norm_params.shape[0] * data_size
-    norm_grad = jnp.concatenate(
-        [norm_pieces, jnp.zeros((norm_total - norm_pieces.shape[0],), FLOAT_TYPE)]
+    enc_tail_late = enc_tail.second(triple_grad)
+    normed_low = after(normed_low, *enc_tail_late)
+    enc_attn = Collect(
+        share([(normed_low, triple_grad), (grad_low, enc_mixture)], rows_enc), *enc_tail.late
+    )
+    other_partial = after(swap(partial), *enc_tail_late, *dec_attn.moved)
+    patch_right, norm_grads = encoder_end(
+        stream_grad,
+        partial,
+        other_partial,
+        enc_stream,
+        enc_gains,
+        c[None],
+        (enc_norms_two, enc_norms_three, dec_norms_one, dec_norms_two, dec_norms_three),
+        mask_grad,
     )
     norm_half = norm_share // 2
-    norm_grads = low(norm_grad).reshape(data_size, 2, norm_half).transpose(1, 0, 2)
-    norm_grads = jnp.pad(norm_grads, ((0, 0), (0, 0), (0, norm_room - norm_half)))
-    enc_attn = Collect(
+    enc_attn_late = enc_attn.second()
+    enc_first = Collect(
         share(
-            [(normed_low, triple_grad), (grad_low, enc_mixture)],
+            [],
             rows_enc,
             (seen_rows, patch_right),
-            norm_grads.reshape(2, data_size, rows_enc, LANES),
+            norm_grads,
         ),
-        *enc_tail.late,
+        *enc_attn_late,
     )
 
     enc_tail_sent = enc_tail.third()
-    enc_attn_sent = enc_attn.second(*enc_tail_sent)
+    enc_attn_sent = enc_attn.third(*enc_tail_sent)
+    enc_first_late = enc_first.second(*enc_tail.moved)
     early_sums, embed_sum, square = sum_early(
-        [group.terms(*enc_attn_sent) for group in (dec_attn, dec_tail, enc_tail)], quarter_dec
-    )
-    enc_attn.third(*enc_tail.moved)
+        [
+            group.terms(*enc_attn_sent, *enc_first_late)
+            for group in (dec_attn, dec_tail, enc_tail)
+        ],
+        quarter_dec,
+    )
+    enc_first_sent = enc_first.third()
     late_sum, exchanged, totals = sum_late(
-        enc_attn.terms(), embed_sum, square, loss_part, valid_count, half_enc
+        enc_attn.terms(*enc_first_sent), enc_first.terms(), embed_sum, square, loss_part, valid_count, half_enc
     )
     exchanged = [
         exchanged,

time: 472 us -> 426 us (0.903)
  Pallas kernels: 133 us -> 77.9 us
  other arithmetic: 43.9 us -> 30.4 us
  starting transfers between devices: 92.2 us -> 102 us
  local copies, waits for them, and re-layouts: 51.9 us -> 59.9 us
  waiting for transfers between devices: 137 us -> 144 us
    pallas_call x22 -> x25, Pallas kernels: 133 us -> 77.9 us  [vmem_call(): pl.pallas_call(body, out_shape=shapes, in_specs=[pl.BlockSpec(memory_spac...]
    unnamed x191 -> x308, local copies, waits for them, and re-layouts: 17.6 us -> 41.4 us
    ppermute x63 -> x66, starting transfers between devices: 48.6 us -> 61.9 us  [swap(): return lax.ppermute(values, axis, SWAP)]
    slice x16 -> x6, local copies, waits for them, and re-layouts: 9.31 us -> 2.16 us  [corners(): low_part, high_part = (from_y[:favour], from_x[favour:])]
    ppermute x63 -> x66, waiting for transfers between devices: 52 us -> 58.1 us  [swap(): return lax.ppermute(values, axis, SWAP)]
    ppermute x5, waiting for transfers between devices: 8.59 us -> 14.1 us  [total_over(): lax.ppermute(values, axis, [(i, i ^ step) for i in range(size)])]
    convert_element_type x22, other arithmetic: 11.2 us -> 6.24 us  [low(): return values.astype(NARROW_TYPE)]
    ppermute x24 -> x27, waiting for transfers between devices: 76.4 us -> 72.2 us  [shift(): lax.ppermute(values, axis, [(i, (i + step) % size) for i in range(size)])]
  transfers between devices with their start and end apart: 93 -> 99, of which waited for: 31 -> 36; matrix products, arithmetic and copies ran while one was open for 16% -> 12% of each run, Pallas kernels for 20% -> 12%
where the time goes in v5:
time: 426 us; the launch traced here: 421 us
  waiting for transfers between devices  144 us (34%)
  starting transfers between devices  102 us (24%)
  Pallas kernels  77.9 us (18%)
  local copies, waits for them, and re-layouts  59.9 us (14%)
  other arithmetic  30.4 us (7%)
    pallas_call x25, Pallas kernels, vmem_call(): pl.pallas_call(body, out_shape=shapes, in_specs=[pl.BlockSpec(memory_spac...  77.9 us
    ppermute x27, waiting for transfers between devices, shift(): lax.ppermute(values, axis, [(i, (i + step) % size) for i in range(size)])  72.2 us
    ppermute x66, starting transfers between devices, swap(): return lax.ppermute(values, axis, SWAP)  61.9 us
    ppermute x66, waiting for transfers between devices, swap(): return lax.ppermute(values, axis, SWAP)  58.1 us
    unnamed x308, local copies, waits for them, and re-layouts  41.4 us
    ppermute x27, starting transfers between devices, shift(): lax.ppermute(values, axis, [(i, (i + step) % size) for i in range(size)])  36.7 us
    ppermute x5, waiting for transfers between devices, total_over(): lax.ppermute(values, axis, [(i, i ^ step) for i in range(size)])  14.1 us
    dynamic_slice x4, local copies, waits for them, and re-layouts, pick(): return lax.dynamic_index_in_dim(array, index, axis, keepdims=False)  11.6 us
  transfers between devices with their start and end apart: 99, of which 36 were waited for; matrix products, arithmetic and copies ran while one was open for 12% of the time, Pallas kernels for 12%

profile of v5, /device:TPU:0, one launch (start us, length us, event | category | flops | bytes accessed | tf_op | source)
XLA Modules:
  0.0 421.1 jit_solution(17306366683939605930)
XLA Ops:
  9.9 3.6 collective-permute-start.2
  28.1 7.8 %collective-permute-done.1 = bf16[96,1280]{1,0:T(8,128)(2,1)S(1)} collective-permute-done((bf16[96,1280]{1,0:T(8,128)(2,1)S(1)}, bf16[96,1280]{1,0:T(8,128)(2,1)S(1)}, u32[]{:S(2)}, u32[]{:S(2)}) %collective-permute-start.1) | collective-permute-done | bytes 245792 | tf_op jit(solution)/shard_map/ppermute | solution.py:62
  49.7 13.3 %collective-permute-done.15.refs_4_ = bf16[1,96,1664]{2,1,0:T(8,128)(2,1)} collective-permute-done((bf16[1,96,1664]{2,1,0:T(8,128)(2,1)S(1)}, bf16[1,96,1664]{2,1,0:T(8,128)(2,1)}, u32[]{:S(2)}, u32[]{:S(2)}) %collective-permute-start.15) | collective-permute-done | bytes 319520 | tf_op jit(solution)/shard_map/ppermute | solution.py:47
  63.7 3.8 collective-permute-start.23
  68.8 10.0 %constant_dynamic-slice_fusion.3 = (bf16[1,588,1536]{2,0,1:T(2,128)(2,1)S(1)}, bf16[1,588,1536]{2,0,1:T(2,128)(2,1)S(1)}) fusion(bf16[4,588,1536]{2,0,1:T(4,128)(2,1)} %param.29, s32[]{:T(128)S(6)} %select_n.206, s32[]{:T(128)S(6)} %select_n.208), kind=kLoop, calls=%fused_computation.166 | loop fusion | bytes 7225352 | tf_op jit(solution)/shard_map/jit(dynamic_index_in_dim)/dynamic_slice | solution.py:894
  81.5 15.9 %collective-permute-done.22 = bf16[96,1664]{1,0:T(8,128)(2,1)S(1)} collective-permute-done((bf16[96,1664]{1,0:T(8,128)(2,1)S(1)}, bf16[96,1664]{1,0:T(8,128)(2,1)S(1)}, u32[]{:S(2)}, u32[]{:S(2)}) %collective-permute-start.22) | collective-permute-done | bytes 319520 | tf_op jit(solution)/shard_map/ppermute | solution.py:62
  105.2 5.6 %collective-permute-done.11 = bf16[147,768]{1,0:T(8,128)(2,1)S(1)} collective-permute-done((bf16[147,768]{1,0:T(8,128)(2,1)S(1)}, bf16[147,768]{1,0:T(8,128)(2,1)S(1)}, u32[]{:S(2)}, u32[]{:S(2)}) %collective-permute-start.11) | collective-permute-done | bytes 225824 | tf_op jit(solution)/shard_map/ppermute | solution.py:62
  114.3 7.6 %collective-permute-done.28.refs_6_ = bf16[3,96,1664]{2,1,0:T(8,128)(2,1)S(1)} collective-permute-done((bf16[3,96,1664]{2,1,0:T(8,128)(2,1)S(1)}, bf16[3,96,1664]{2,1,0:T(8,128)(2,1)S(1)}, u32[]{:S(2)}, u32[]{:S(2)}) %collective-permute-start.28) | collective-permute-done | bytes 958496 | tf_op jit(solution)/shard_map/ppermute | solution.py:47
  133.2 3.9 collective-permute-done.30.refs_8_
  162.2 13.4 %collective-permute-done.35 = bf16[588,1024]{1,0:T(8,128)(2,1)} collective-permute-done((bf16[588,1024]{1,0:T(8,128)(2,1)}, bf16[588,1024]{1,0:T(8,128)(2,1)}, u32[]{:S(2)}, u32[]{:S(2)}) %collective-permute-start.35) | collective-permute-done | bytes 1204256 | tf_op jit(solution)/shard_map/ppermute | solution.py:62
  192.1 8.4 %shard_map.492 = (f32[588,512]{1,0:T(8,128)S(1)}, bf16[2,588,384]{2,1,0:T(8,128)(2,1)S(1)}, bf16[2,588,128]{2,1,0:T(8,128)(2,1)S(1)}, f32[588,8]{1,0:T(8,128)S(1)}) custom-call(f32[588,512]{1,0:T(8,128)S(1)} %get-tuple-element.313.stream, f32[6,512]{1,0:T(8,128)S(1)} %slice_convert_fusion.1.gains.refs_4_, bf16[2,512,384]{2,1,0:T(8,128)(2,1)S(1)} %bitcast.177, ...), custom_call_target="tpu_custom_call" | custom-call | flops 2032730112 | bytes 4692352 | tf_op jit(solution)/shard_map/pallas_call | solution.py:85
  224.3 5.1 %shard_map.495 = (f32[588,512]{1,0:T(8,128)S(1)}, bf16[588,512]{1,0:T(8,128)(2,1)S(1)}, bf16[588,512]{1,0:T(8,128)(2,1)S(1)}, bf16[2,588,512]{2,1,0:T(8,128)(2,1...) custom-call(bf16[588,512]{1,0:T(8,128)(2,1)} %get-tuple-element.332.refs_0_, ...), custom_call_target="tpu_custom_call" | custom-call | flops 1849688064 | bytes 11145216 | tf_op jit(solution)/shard_map/pallas_call | solution.py:85
  237.4 15.2 %shard_map.496 = (f32[588,512]{1,0:T(8,128)S(1)}, bf16[588,512]{1,0:T(8,128)(2,1)S(1)}, bf16[588,512]{1,0:T(8,128)(2,1)S(1)}, bf16[2,588,384]{2,1,0:T(8,128)(2,1...) custom-call(f32[588,512]{1,0:T(8,128)S(1)} %get-tuple-element.334.stream_grad, ...), custom_call_target="tpu_custom_call" | custom-call | flops 4156981248 | bytes 10717568 | tf_op jit(solution)/shard_map/pallas_call | solution.py:85
  258.8 3.9 collective-permute-done.47
  283.4 4.4 %collective-permute-done.57.refs_5_ = bf16[64,1408]{1,0:T(8,128)(2,1)S(1)} collective-permute-done((bf16[64,1408]{1,0:T(8,128)(2,1)S(1)}, bf16[64,1408]{1,0:T(8,128)(2,1)S(1)}, u32[]{:S(2)}, u32[]{:S(2)}) %collective-permute-start.57) | collective-permute-done | bytes 180256 | tf_op jit(solution)/shard_map/ppermute | solution.py:62
  288.5 4.3 %collective-permute-done.58.refs_6_ = bf16[64,1408]{1,0:T(8,128)(2,1)S(1)} collective-permute-done((bf16[64,1408]{1,0:T(8,128)(2,1)S(1)}, bf16[64,1408]{1,0:T(8,128)(2,1)S(1)}, u32[]{:S(2)}, u32[]{:S(2)}) %collective-permute-start.58) | collective-permute-done | bytes 180256 | tf_op jit(solution)/shard_map/ppermute | solution.py:62
  303.4 3.8 collective-permute-done.77.refs_2_
  315.5 6.1 %collective-permute-done.63 = bf16[2,96,1664]{2,1,0:T(8,128)(2,1)S(1)} collective-permute-done((bf16[2,96,1664]{2,1,0:T(8,128)(2,1)S(1)}, bf16[2,96,1664]{2,1,0:T(8,128)(2,1)S(1)}, u32[]{:S(2)}, u32[]{:S(2)}) %collective-permute-start.63) | collective-permute-done | bytes 639008 | tf_op jit(solution)/shard_map/ppermute | solution.py:47
  321.6 4.8 %collective-permute-done.62 = bf16[2,96,1664]{2,1,0:T(8,128)(2,1)S(1)} collective-permute-done((bf16[2,96,1664]{2,1,0:T(8,128)(2,1)S(1)}, bf16[2,96,1664]{2,1,0:T(8,128)(2,1)S(1)}, u32[]{:S(2)}, u32[]{:S(2)}) %collective-permute-start.62) | collective-permute-done | bytes 639008 | tf_op jit(solution)/shard_map/ppermute | solution.py:47
  343.7 4.3 %collective-permute-done.83.refs_9_ = bf16[96,1664]{1,0:T(8,128)(2,1)S(1)} collective-permute-done((bf16[96,1664]{1,0:T(8,128)(2,1)}, bf16[96,1664]{1,0:T(8,128)(2,1)S(1)}, u32[]{:S(2)}, u32[]{:S(2)}) %collective-permute-start.83) | collective-permute-done | bytes 319520 | tf_op jit(solution)/shard_map/ppermute | solution.py:62
  348.7 8.4 %collective-permute-done.84.refs_10_ = bf16[96,1664]{1,0:T(8,128)(2,1)S(1)} collective-permute-done((bf16[96,1664]{1,0:T(8,128)(2,1)}, bf16[96,1664]{1,0:T(8,128)(2,1)S(1)}, u32[]{:S(2)}, u32[]{:S(2)}) %collective-permute-start.84) | collective-permute-done | bytes 319520 | tf_op jit(solution)/shard_map/ppermute | solution.py:62
  377.9 4.6 %collective-permute-start.89 = (bf16[96,512]{1,0:T(8,128)(2,1)}, bf16[96,512]{1,0:T(8,128)(2,1)S(1)}, u32[]{:S(2)}, u32[]{:S(2)}) collective-permute-start(bf16[96,512]{1,0:T(8,128)(2,1)} %get-tuple-element.572), channel_id=1, source_target_pairs={{0,16},{8,24},{16,0},{24,8},{1,17},{9,25},{17,1},{25,9},{2,18},{10... | collective-permute-start | bytes 294920 | tf_op jit(solution)/shard_map/ppermute | solution.py:62
  395.4 3.6 collective-permute-done.92
  411.1 8.4 %shard_map.508 = (f32[1,128]{1,0:T(1,128)}, f32[7,96,192]{2,1,0:T(8,128)}, f32[7,96,192]{2,1,0:T(8,128)}, f32[7,96,192]{2,1,0:T(8,128)}, f32[5,192,96]{2,1,0:T(8...) custom-call(s32[2]{0:T(128)} %copy-done.105, ...), custom_call_target="tpu_custom_call" | custom-call | bytes 14871552 | tf_op jit(solution)/shard_map/pallas_call | solution.py:85
  (615 shorter events, 247.4 us)
Async XLA Ops:
  38.9 24.8 %collective-permute-start.14 = (bf16[3,96,1280]{2,1,0:T(8,128)(2,1)S(1)}, bf16[3,96,1280]{2,1,0:T(8,128)(2,1)S(1)}, u32[]{:S(2)}, u32[]{:S(2)}) collective-permute-start(bf16[3,96,1280]{2,1,0:T(8,128)(2,1)S(1)} %pad_maximum_fusion.4.refs_1_), channel_id=1, source_target_pairs={{0,4},{4,0},{1,5},{5,1},{2,6},{6,2},{3,7},{7,3},{8,12},{12,8},{9,1... | collective-permute-start | bytes 2211848 | tf_op jit(solution)/shard_map/ppermute | solution.py:47
  40.5 27.0 %collective-permute-start.13 = (bf16[3,96,1280]{2,1,0:T(8,128)(2,1)S(1)}, bf16[3,96,1280]{2,1,0:T(8,128)(2,1)S(1)}, u32[]{:S(2)}, u32[]{:S(2)}) collective-permute-start(bf16[3,96,1280]{2,1,0:T(8,128)(2,1)S(1)} %pad_maximum_fusion.4.refs_1_), channel_id=1, source_target_pairs={{0,2},{2,0},{1,3},{3,1},{4,6},{6,4},{5,7},{7,5},{8,10},{10,8},{9,1... | collective-permute-start | bytes 2211848 | tf_op jit(solution)/shard_map/ppermute | solution.py:47
  41.8 25.8 %collective-permute-start.26 = (bf16[64,1920]{1,0:T(8,128)(2,1)S(1)}, bf16[64,1920]{1,0:T(8,128)(2,1)}, u32[]{:S(2)}, u32[]{:S(2)}) collective-permute-start(bf16[64,1920]{1,0:T(8,128)(2,1)S(1)} %get-tuple-element.301), channel_id=1, source_target_pairs={{0,24},{8,0},{16,8},{24,16},{1,25},{9,1},{17,9},{25,17},{2,26},{10... | collective-permute-start | bytes 737288 | tf_op jit(solution)/shard_map/ppermute | solution.py:62
  45.2 23.1 %collective-permute-start.25 = (bf16[64,1920]{1,0:T(8,128)(2,1)S(1)}, bf16[64,1920]{1,0:T(8,128)(2,1)}, u32[]{:S(2)}, u32[]{:S(2)}) collective-permute-start(bf16[64,1920]{1,0:T(8,128)(2,1)S(1)} %get-tuple-element.301), channel_id=1, source_target_pairs={{0,16},{8,24},{16,0},{24,8},{1,17},{9,25},{17,1},{25,9},{2,18},{10... | collective-permute-start | bytes 737288 | tf_op jit(solution)/shard_map/ppermute | solution.py:62
  67.5 29.9 %collective-permute-start.22 = (bf16[96,1664]{1,0:T(8,128)(2,1)S(1)}, bf16[96,1664]{1,0:T(8,128)(2,1)S(1)}, u32[]{:S(2)}, u32[]{:S(2)}) collective-permute-start(bf16[96,1664]{1,0:T(8,128)(2,1)S(1)} %get-tuple-element.300), channel_id=1, source_target_pairs={{0,16},{8,24},{16,0},{24,8},{1,17},{9,25},{17,1},{25,9},{2,18},{10... | collective-permute-start | bytes 958472 | tf_op jit(solution)/shard_map/ppermute | solution.py:62
  67.6 29.8 %collective-permute-start.21 = (bf16[96,1664]{1,0:T(8,128)(2,1)S(1)}, bf16[96,1664]{1,0:T(8,128)(2,1)S(1)}, u32[]{:S(2)}, u32[]{:S(2)}) collective-permute-start(bf16[96,1664]{1,0:T(8,128)(2,1)S(1)} %get-tuple-element.300), channel_id=1, source_target_pairs={{0,8},{8,16},{16,24},{24,0},{1,9},{9,17},{17,25},{25,1},{2,10},{10... | collective-permute-start | bytes 958472 | tf_op jit(solution)/shard_map/ppermute | solution.py:62
  68.3 29.9 %collective-permute-start.17 = (bf16[2,96,1280]{2,1,0:T(8,128)(2,1)S(1)}, bf16[2,96,1280]{2,1,0:T(8,128)(2,1)S(1)}, u32[]{:S(2)}, u32[]{:S(2)}) collective-permute-start(bf16[2,96,1280]{2,1,0:T(8,128)(2,1)S(1)} %slice.158), channel_id=1, source_target_pairs={{0,2},{2,0},{1,3},{3,1},{4,6},{6,4},{5,7},{7,5},{8,10},{10,8},{9,1... | collective-permute-start | bytes 1474568 | tf_op jit(solution)/shard_map/ppermute | solution.py:47
  99.1 22.8 %collective-permute-start.28 = (bf16[3,96,1664]{2,1,0:T(8,128)(2,1)S(1)}, bf16[3,96,1664]{2,1,0:T(8,128)(2,1)S(1)}, u32[]{:S(2)}, u32[]{:S(2)}) collective-permute-start(bf16[3,96,1664]{2,1,0:T(8,128)(2,1)S(1)} %pad_maximum_fusion.2.refs_1_), channel_id=1, source_target_pairs={{0,4},{4,0},{1,5},{5,1},{2,6},{6,2},{3,7},{7,3},{8,12},{12,8},{9,1... | collective-permute-start | bytes 2875400 | tf_op jit(solution)/shard_map/ppermute | solution.py:47
  99.2 22.8 %collective-permute-start.27 = (bf16[3,96,1664]{2,1,0:T(8,128)(2,1)S(1)}, bf16[3,96,1664]{2,1,0:T(8,128)(2,1)S(1)}, u32[]{:S(2)}, u32[]{:S(2)}) collective-permute-start(bf16[3,96,1664]{2,1,0:T(8,128)(2,1)S(1)} %pad_maximum_fusion.2.refs_1_), channel_id=1, source_target_pairs={{0,2},{2,0},{1,3},{3,1},{4,6},{6,4},{5,7},{7,5},{8,10},{10,8},{9,1... | collective-permute-start | bytes 2875400 | tf_op jit(solution)/shard_map/ppermute | solution.py:47
  127.2 48.4 %collective-permute-start.35 = (bf16[588,1024]{1,0:T(8,128)(2,1)}, bf16[588,1024]{1,0:T(8,128)(2,1)}, u32[]{:S(2)}, u32[]{:S(2)}) collective-permute-start(bf16[588,1024]{1,0:T(8,128)(2,1)} %pad_maximum_fusion.1), channel_id=1, source_target_pairs={{0,16},{8,24},{16,0},{24,8},{1,17},{9,25},{17,1},{25,9},{2,18},{10... | collective-permute-start | bytes 3612680 | tf_op jit(solution)/shard_map/ppermute | solution.py:62
  139.4 36.3 %collective-permute-start.34 = (bf16[3,64,1920]{2,1,0:T(8,128)(2,1)}, bf16[3,64,1920]{2,1,0:T(8,128)(2,1)}, u32[]{:S(2)}, u32[]{:S(2)}) collective-permute-start(bf16[3,64,1920]{2,1,0:T(8,128)(2,1)} %pad_maximum_fusion.5.refs_1_), channel_id=1, source_target_pairs={{0,4},{4,0},{1,5},{5,1},{2,6},{6,2},{3,7},{7,3},{8,12},{12,8},{9,1... | collective-permute-start | bytes 2211848 | tf_op jit(solution)/shard_map/ppermute | solution.py:47
  140.8 34.9 %collective-permute-start.33 = (bf16[3,64,1920]{2,1,0:T(8,128)(2,1)}, bf16[3,64,1920]{2,1,0:T(8,128)(2,1)}, u32[]{:S(2)}, u32[]{:S(2)}) collective-permute-start(bf16[3,64,1920]{2,1,0:T(8,128)(2,1)} %pad_maximum_fusion.5.refs_1_), channel_id=1, source_target_pairs={{0,2},{2,0},{1,3},{3,1},{4,6},{6,4},{5,7},{7,5},{8,10},{10,8},{9,1... | collective-permute-start | bytes 2211848 | tf_op jit(solution)/shard_map/ppermute | solution.py:47
  152.7 25.9 %collective-permute-start.32 = (bf16[2,768,128]{2,1,0:T(8,128)(2,1)}, bf16[2,768,128]{2,1,0:T(8,128)(2,1)}, u32[]{:S(2)}, u32[]{:S(2)}) collective-permute-start(bf16[2,768,128]{2,1,0:T(8,128)(2,1)} %bitcast.29), channel_id=1, source_target_pairs={{0,1},{1,0},{2,3},{3,2},{4,5},{5,4},{6,7},{7,6},{8,9},{9,8},{10,11... | collective-permute-start | bytes 1179656 | tf_op jit(solution)/shard_map/ppermute | solution.py:47
  162.1 20.3 %collective-permute-start.31 = (f32[147,768]{1,0:T(8,128)S(1)}, f32[147,768]{1,0:T(8,128)S(1)}, u32[]{:S(2)}, u32[]{:S(2)}) collective-permute-start(f32[147,768]{1,0:T(8,128)S(1)} %get-tuple-element.311.own), channel_id=1, source_target_pairs={{0,1},{1,0},{2,3},{3,2},{4,5},{5,4},{6,7},{7,6},{8,9},{9,8},{10,11... | collective-permute-start | bytes 1354760 | tf_op jit(solution)/shard_map/ppermute | solution.py:47
  233.1 19.5 %collective-permute-start.44 = (bf16[2,64,1408]{2,1,0:T(8,128)(2,1)S(1)}, bf16[2,64,1408]{2,1,0:T(8,128)(2,1)S(1)}, u32[]{:S(2)}, u32[]{:S(2)}) collective-permute-start(bf16[2,64,1408]{2,1,0:T(8,128)(2,1)S(1)} %get-tuple-element.348), channel_id=1, source_target_pairs={{0,2},{2,0},{1,3},{3,1},{4,6},{6,4},{5,7},{7,5},{8,10},{10,8},{9,1... | collective-permute-start | bytes 1081352 | tf_op jit(solution)/shard_map/ppermute | solution.py:47
  237.1 29.3 %collective-permute-start.50 = (bf16[2,64,1408]{2,1,0:T(8,128)(2,1)S(1)}, bf16[2,64,1408]{2,1,0:T(8,128)(2,1)S(1)}, u32[]{:S(2)}, u32[]{:S(2)}) collective-permute-start(bf16[2,64,1408]{2,1,0:T(8,128)(2,1)S(1)} %get-tuple-element.372), channel_id=1, source_target_pairs={{0,2},{2,0},{1,3},{3,1},{4,6},{6,4},{5,7},{7,5},{8,10},{10,8},{9,1... | collective-permute-start | bytes 1081352 | tf_op jit(solution)/shard_map/ppermute | solution.py:47
  237.4 30.6 %collective-permute-start.51 = (bf16[2,64,1408]{2,1,0:T(8,128)(2,1)S(1)}, bf16[2,64,1408]{2,1,0:T(8,128)(2,1)S(1)}, u32[]{:S(2)}, u32[]{:S(2)}) collective-permute-start(bf16[2,64,1408]{2,1,0:T(8,128)(2,1)S(1)} %get-tuple-element.373), channel_id=1, source_target_pairs={{0,4},{4,0},{1,5},{5,1},{2,6},{6,2},{3,7},{7,3},{8,12},{12,8},{9,1... | collective-permute-start | bytes 1081352 | tf_op jit(solution)/shard_map/ppermute | solution.py:47
  293.6 21.8 %collective-permute-start.70 = (bf16[2,96,1664]{2,1,0:T(8,128)(2,1)S(1)}, bf16[2,96,1664]{2,1,0:T(8,128)(2,1)S(1)}, u32[]{:S(2)}, u32[]{:S(2)}) collective-permute-start(bf16[2,96,1664]{2,1,0:T(8,128)(2,1)S(1)} %get-tuple-element.437), channel_id=1, source_target_pairs={{0,2},{2,0},{1,3},{3,1},{4,6},{6,4},{5,7},{7,5},{8,10},{10,8},{9,1... | collective-permute-start | bytes 1916936 | tf_op jit(solution)/shard_map/ppermute | solution.py:47
  299.0 22.6 %collective-permute-start.63 = (bf16[2,96,1664]{2,1,0:T(8,128)(2,1)S(1)}, bf16[2,96,1664]{2,1,0:T(8,128)(2,1)S(1)}, u32[]{:S(2)}, u32[]{:S(2)}) collective-permute-start(bf16[2,96,1664]{2,1,0:T(8,128)(2,1)S(1)} %add_convert_fusion.2), channel_id=1, source_target_pairs={{0,2},{2,0},{1,3},{3,1},{4,6},{6,4},{5,7},{7,5},{8,10},{10,8},{9,1... | collective-permute-start | bytes 1916936 | tf_op jit(solution)/shard_map/ppermute | solution.py:47
  300.4 26.1 %collective-permute-start.62 = (bf16[2,96,1664]{2,1,0:T(8,128)(2,1)S(1)}, bf16[2,96,1664]{2,1,0:T(8,128)(2,1)S(1)}, u32[]{:S(2)}, u32[]{:S(2)}) collective-permute-start(bf16[2,96,1664]{2,1,0:T(8,128)(2,1)S(1)} %add_convert_fusion.3), channel_id=1, source_target_pairs={{0,4},{4,0},{1,5},{5,1},{2,6},{6,2},{3,7},{7,3},{8,12},{12,8},{9,1... | collective-permute-start | bytes 1916936 | tf_op jit(solution)/shard_map/ppermute | solution.py:47
  333.4 23.7 %collective-permute-start.84 = (bf16[96,1664]{1,0:T(8,128)(2,1)}, bf16[96,1664]{1,0:T(8,128)(2,1)S(1)}, u32[]{:S(2)}, u32[]{:S(2)}) collective-permute-start(bf16[96,1664]{1,0:T(8,128)(2,1)} %get-tuple-element.556), channel_id=1, source_target_pairs={{0,16},{8,24},{16,0},{24,8},{1,17},{9,25},{17,1},{25,9},{2,18},{10... | collective-permute-start | bytes 958472 | tf_op jit(solution)/shard_map/ppermute | solution.py:62
  335.7 22.1 %collective-permute-start.81 = (bf16[2,96,512]{2,1,0:T(8,128)(2,1)}, bf16[2,96,512]{2,1,0:T(8,128)(2,1)}, u32[]{:S(2)}, u32[]{:S(2)}) collective-permute-start(bf16[2,96,512]{2,1,0:T(8,128)(2,1)} %get-tuple-element.472), channel_id=1, source_target_pairs={{0,2},{2,0},{1,3},{3,1},{4,6},{6,4},{5,7},{7,5},{8,10},{10,8},{9,1... | collective-permute-start | bytes 589832 | tf_op jit(solution)/shard_map/ppermute | solution.py:47
  336.7 22.9 %collective-permute-start.82 = (bf16[2,96,512]{2,1,0:T(8,128)(2,1)}, bf16[2,96,512]{2,1,0:T(8,128)(2,1)}, u32[]{:S(2)}, u32[]{:S(2)}) collective-permute-start(bf16[2,96,512]{2,1,0:T(8,128)(2,1)} %get-tuple-element.473), channel_id=1, source_target_pairs={{0,4},{4,0},{1,5},{5,1},{2,6},{6,2},{3,7},{7,3},{8,12},{12,8},{9,1... | collective-permute-start | bytes 589832 | tf_op jit(solution)/shard_map/ppermute | solution.py:47
  342.9 19.0 %collective-permute-start.64 = (bf16[2,96,768]{2,1,0:T(8,128)(2,1)S(1)}, bf16[2,96,768]{2,1,0:T(8,128)(2,1)S(1)}, u32[]{:S(2)}, u32[]{:S(2)}) collective-permute-start(bf16[2,96,768]{2,1,0:T(8,128)(2,1)S(1)} %get-tuple-element.428), channel_id=1, source_target_pairs={{0,2},{2,0},{1,3},{3,1},{4,6},{6,4},{5,7},{7,5},{8,10},{10,8},{9,1... | collective-permute-start | bytes 884744 | tf_op jit(solution)/shard_map/ppermute | solution.py:47
  (227 other events, 1959.1 us)

commit v6 on v5

--- a/solution.py
+++ b/solution.py
@@ -208,13 +208,14 @@
     return vmem_call(body, outs, enc_in, enc_out, dec_in, dec_out, embed, head, scalars=(place,))
 
 
-def spread_all(blobs, widths, arrived, last):
+def spread_all(blobs, widths, arrived, early, last):
     sizes = tuple(lax.axis_size(axis) for axis in ("x", "z", "y"))
     if sizes != (2, 4, 2):
         wholes = [lax.all_gather(blob, ("x", "z", "y")) for blob in blobs]
         wholes = [whole.reshape(2, -1, whole.shape[-1]) for whole in wholes]
         pieces = [columns_of(whole, width) for whole, width in zip(wholes, widths)]
         marks = [wholes[0]] * 4
+        early(wholes[0])
         return pieces, marks, last(marks)
     first = Spread(blobs[0], 2)
     first.along_z()
@@ -223,14 +224,15 @@
         group.near_corners()
     second.along_z(*first.moved)
     third.along_z(*first.moved)
-    first.far_sides(*first.near, *second.near[:2], *third.near[:2], arrived)
-    first.far_corners(*second.near[2:], *third.near[2:])
+    first.far_sides(*first.near, *second.near, *third.near, arrived)
+    picked = early(first.stack)
+    first.far_corners(picked)
     second.far_sides(*first.far, *third.moved)
     second.far_corners()
     third.far_sides(*second.far)
     marks = (first.stack, first.far[0], first.far[2], third.moved[2])
     moved = last(marks)
-    third.far_corners(moved)
+    third.far_corners()
     pieces = [group.whole(width) for group, width in zip((first, second, third), widths)]
     return pieces, marks, moved
 
@@ -1006,16 +1008,23 @@
     visible_moved = shift(pick(visible, away), "z", half_step)
     visible_row = jnp.where(use_own, pick(visible, x), visible_moved)
 
-    def packs_of(marks):
-        start = after(x, marks[0])
+    seen, packs = [], []
+
+    def pick_slots(mark):
+        start = after(x, mark)
         own_slot, away_slot = pick(pixels, start), pick(pixels, slot_total - 1 - start)
+        packs.extend((start, own_slot, away_slot))
 
         def seen_of(slot, rows):
             return low(product("vt,tp->vp", low(one_hot(pick(visible, slot), tokens)), rows))
 
-        seen_away = shift(halves_of(seen_of(away, away_slot), c), "z", half_step)
-        seen_away = both(seen_away, "c", c, 1)
+        sent = halves_of(seen_of(away, away_slot), c)
+        seen_away = both(shift(sent, "z", half_step), "c", c, 1)
         seen.append(jnp.where(use_own, seen_of(x, own_slot), seen_away))
+        return sent
+
+    def move_pack(marks):
+        start, own_slot, away_slot = packs
 
         def pixels_of(slot, rows):
             place = after(c, marks[1])
@@ -1027,9 +1036,8 @@
         away_pack = pixels_of(slot_total - 1 - start, away_slot)
         return shift(after(away_pack, marks[3]), "z", half_step)
 
-    seen = []
     (first_all, second_all, third_all), marks, pack_moved = spread_all(
-        (first_blob, second_blob, third_blob), widths, visible_moved, packs_of
+        (first_blob, second_blob, third_blob), widths, visible_moved, pick_slots, move_pack
     )
     seen_rows, own_pack = seen
 

time: 426 us -> 411 us (0.965)
  waiting for transfers between devices: 144 us -> 114 us
  starting transfers between devices: 102 us -> 114 us
    ppermute x27, waiting for transfers between devices: 72.2 us -> 53.4 us  [shift(): lax.ppermute(values, axis, [(i, (i + step) % size) for i in range(size)])]
    ppermute x27, starting transfers between devices: 36.7 us -> 51.6 us  [shift(): lax.ppermute(values, axis, [(i, (i + step) % size) for i in range(size)])]
    ppermute x66, waiting for transfers between devices: 58.1 us -> 49.2 us  [swap(): return lax.ppermute(values, axis, SWAP)]
    unnamed x308 -> x320, local copies, waits for them, and re-layouts: 41.4 us -> 43.2 us
  transfers between devices with their start and end apart: 99 -> 99, of which waited for: 36 -> 39; matrix products, arithmetic and copies ran while one was open for 12% -> 13% of each run, Pallas kernels for 12% -> 15%
where the time goes in v6:
time: 411 us; the launch traced here: 405 us
  starting transfers between devices  114 us (28%)
  waiting for transfers between devices  114 us (28%)
  Pallas kernels  77 us (19%)
  local copies, waits for them, and re-layouts  61.4 us (15%)
  other arithmetic  31.2 us (8%)
    pallas_call x25, Pallas kernels, vmem_call(): pl.pallas_call(body, out_shape=shapes, in_specs=[pl.BlockSpec(memory_spac...  77 us
    ppermute x66, starting transfers between devices, swap(): return lax.ppermute(values, axis, SWAP)  58.6 us
    ppermute x27, waiting for transfers between devices, shift(): lax.ppermute(values, axis, [(i, (i + step) % size) for i in range(size)])  53.4 us
    ppermute x27, starting transfers between devices, shift(): lax.ppermute(values, axis, [(i, (i + step) % size) for i in range(size)])  51.6 us
    ppermute x66, waiting for transfers between devices, swap(): return lax.ppermute(values, axis, SWAP)  49.2 us
    unnamed x320, local copies, waits for them, and re-layouts  43.2 us
    ppermute x5, waiting for transfers between devices, total_over(): lax.ppermute(values, axis, [(i, i ^ step) for i in range(size)])  11.7 us
    dynamic_slice x4, local copies, waits for them, and re-layouts, pick(): return lax.dynamic_index_in_dim(array, index, axis, keepdims=False)  11.3 us
  transfers between devices with their start and end apart: 99, of which 39 were waited for; matrix products, arithmetic and copies ran while one was open for 13% of the time, Pallas kernels for 15%

profile of v6, /device:TPU:0, one launch (start us, length us, event | category | flops | bytes accessed | tf_op | source)
XLA Modules:
  0.0 404.7 jit_solution(5902539103892497505)
XLA Ops:
  18.0 3.6 collective-permute-start.2
  24.2 3.7 collective-permute-done.9.refs_2_
  35.6 5.2 %collective-permute-done.1 = bf16[96,1280]{1,0:T(8,128)(2,1)S(1)} collective-permute-done((bf16[96,1280]{1,0:T(8,128)(2,1)S(1)}, bf16[96,1280]{1,0:T(8,128)(2,1)S(1)}, u32[]{:S(2)}, u32[]{:S(2)}) %collective-permute-start.1) | collective-permute-done | bytes 245792 | tf_op jit(solution)/shard_map/ppermute | solution.py:62
  51.6 9.8 %constant_dynamic-slice_fusion.3 = (bf16[1,588,1536]{2,0,1:T(2,128)(2,1)S(1)}, bf16[1,588,1536]{2,0,1:T(2,128)(2,1)S(1)}) fusion(bf16[4,588,1536]{2,0,1:T(4,128)(2,1)} %param.29, s32[]{:T(128)S(6)} %select_n.206, s32[]{:T(128)S(6)} %select_n.208), kind=kLoop, calls=%fused_computation.166 | loop fusion | bytes 7225352 | tf_op jit(solution)/shard_map/jit(dynamic_index_in_dim)/dynamic_slice | solution.py:896
  62.4 3.8 collective-permute-done.16.refs_6_
  76.3 3.4 collective-permute-done.23
  79.7 16.1 %collective-permute-done.22 = bf16[96,1664]{1,0:T(8,128)(2,1)S(1)} collective-permute-done((bf16[96,1664]{1,0:T(8,128)(2,1)S(1)}, bf16[96,1664]{1,0:T(8,128)(2,1)S(1)}, u32[]{:S(2)}, u32[]{:S(2)}) %collective-permute-start.22) | collective-permute-done | bytes 319520 | tf_op jit(solution)/shard_map/ppermute | solution.py:62
  105.9 6.1 %collective-permute-done.13 = bf16[147,768]{1,0:T(8,128)(2,1)S(1)} collective-permute-done((bf16[147,768]{1,0:T(8,128)(2,1)S(1)}, bf16[147,768]{1,0:T(8,128)(2,1)S(1)}, u32[]{:S(2)}, u32[]{:S(2)}) %collective-permute-start.13) | collective-permute-done | bytes 225824 | tf_op jit(solution)/shard_map/ppermute | solution.py:62
  121.9 6.5 %collective-permute-start.39 = (bf16[588,1024]{1,0:T(8,128)(2,1)}, bf16[588,1024]{1,0:T(8,128)(2,1)}, u32[]{:S(2)}, u32[]{:S(2)}) collective-permute-start(bf16[588,1024]{1,0:T(8,128)(2,1)} %pad_maximum_fusion.1), channel_id=1, source_target_pairs={{0,16},{8,24},{16,0},{24,8},{1,17},{9,25},{17,1},{25,9},{2,18},{10... | collective-permute-start | bytes 3612680 | tf_op jit(solution)/shard_map/ppermute | solution.py:62
  166.9 4.0 %collective-permute-done.36.refs_8_ = bf16[1,64,1920]{2,1,0:T(8,128)(2,1)S(1)} collective-permute-done((bf16[1,64,1920]{2,1,0:T(8,128)(2,1)S(1)}, bf16[1,64,1920]{2,1,0:T(8,128)(2,1)S(1)}, u32[]{:S(2)}, u32[]{:S(2)}) %collective-permute-start.36) | collective-permute-done | bytes 245792 | tf_op jit(solution)/shard_map/ppermute | solution.py:47
  175.9 8.4 %shard_map.492 = (f32[588,512]{1,0:T(8,128)S(1)}, bf16[2,588,384]{2,1,0:T(8,128)(2,1)S(1)}, bf16[2,588,128]{2,1,0:T(8,128)(2,1)S(1)}, f32[588,8]{1,0:T(8,128)S(1)}) custom-call(f32[588,512]{1,0:T(8,128)S(1)} %get-tuple-element.313.stream, f32[6,512]{1,0:T(8,128)S(1)} %slice_convert_fusion.1.gains.refs_4_, bf16[2,512,384]{2,1,0:T(8,128)(2,1)S(1)} %bitcast.177, ...), custom_call_target="tpu_custom_call" | custom-call | flops 2032730112 | bytes 4692352 | tf_op jit(solution)/shard_map/pallas_call | solution.py:85
  209.0 5.0 %shard_map.495 = (f32[588,512]{1,0:T(8,128)S(1)}, bf16[588,512]{1,0:T(8,128)(2,1)S(1)}, bf16[588,512]{1,0:T(8,128)(2,1)S(1)}, bf16[2,588,512]{2,1,0:T(8,128)(2,1...) custom-call(bf16[588,512]{1,0:T(8,128)(2,1)} %get-tuple-element.332.refs_0_, ...), custom_call_target="tpu_custom_call" | custom-call | flops 1849688064 | bytes 11145216 | tf_op jit(solution)/shard_map/pallas_call | solution.py:85
  221.8 15.1 %shard_map.496 = (f32[588,512]{1,0:T(8,128)S(1)}, bf16[588,512]{1,0:T(8,128)(2,1)S(1)}, bf16[588,512]{1,0:T(8,128)(2,1)S(1)}, bf16[2,588,384]{2,1,0:T(8,128)(2,1...) custom-call(f32[588,512]{1,0:T(8,128)S(1)} %get-tuple-element.334.stream_grad, ...), custom_call_target="tpu_custom_call" | custom-call | flops 4156981248 | bytes 10717568 | tf_op jit(solution)/shard_map/pallas_call | solution.py:85
  240.3 6.3 %collective-permute-done.47 = bf16[2,64,1408]{2,1,0:T(8,128)(2,1)S(1)} collective-permute-done((bf16[2,64,1408]{2,1,0:T(8,128)(2,1)S(1)}, bf16[2,64,1408]{2,1,0:T(8,128)(2,1)S(1)}, u32[]{:S(2)}, u32[]{:S(2)}) %collective-permute-start.47) | collective-permute-done | bytes 360480 | tf_op jit(solution)/shard_map/ppermute | solution.py:47
  278.9 3.5 shard_map.501
  299.7 7.1 %collective-permute-done.63 = bf16[2,96,1664]{2,1,0:T(8,128)(2,1)S(1)} collective-permute-done((bf16[2,96,1664]{2,1,0:T(8,128)(2,1)S(1)}, bf16[2,96,1664]{2,1,0:T(8,128)(2,1)S(1)}, u32[]{:S(2)}, u32[]{:S(2)}) %collective-permute-start.63) | collective-permute-done | bytes 639008 | tf_op jit(solution)/shard_map/ppermute | solution.py:47
  306.9 3.8 collective-permute-done.62
  314.4 3.5 collective-permute-start.85
  322.9 4.6 %collective-permute-done.85.refs_11_ = bf16[96,1664]{1,0:T(8,128)(2,1)S(1)} collective-permute-done((bf16[96,1664]{1,0:T(8,128)(2,1)}, bf16[96,1664]{1,0:T(8,128)(2,1)S(1)}, u32[]{:S(2)}, u32[]{:S(2)}) %collective-permute-start.85) | collective-permute-done | bytes 319520 | tf_op jit(solution)/shard_map/ppermute | solution.py:62
  329.0 3.5 collective-permute-done.83.refs_9_
  332.9 8.4 %collective-permute-done.84.refs_10_ = bf16[96,1664]{1,0:T(8,128)(2,1)S(1)} collective-permute-done((bf16[96,1664]{1,0:T(8,128)(2,1)}, bf16[96,1664]{1,0:T(8,128)(2,1)S(1)}, u32[]{:S(2)}, u32[]{:S(2)}) %collective-permute-start.84) | collective-permute-done | bytes 319520 | tf_op jit(solution)/shard_map/ppermute | solution.py:62
  363.1 4.7 %collective-permute-start.89 = (bf16[96,512]{1,0:T(8,128)(2,1)S(1)}, bf16[96,512]{1,0:T(8,128)(2,1)S(1)}, u32[]{:S(2)}, u32[]{:S(2)}) collective-permute-start(bf16[96,512]{1,0:T(8,128)(2,1)S(1)} %get-tuple-element.572), channel_id=1, source_target_pairs={{0,16},{8,24},{16,0},{24,8},{1,17},{9,25},{17,1},{25,9},{2,18},{10... | collective-permute-start | bytes 294920 | tf_op jit(solution)/shard_map/ppermute | solution.py:62
  386.6 3.3 collective-permute-done.97
  394.8 8.4 %shard_map.508 = (f32[1,128]{1,0:T(1,128)}, f32[7,96,192]{2,1,0:T(8,128)}, f32[7,96,192]{2,1,0:T(8,128)}, f32[7,96,192]{2,1,0:T(8,128)}, f32[5,192,96]{2,1,0:T(8...) custom-call(s32[2]{0:T(128)} %copy-done.109, ...), custom_call_target="tpu_custom_call" | custom-call | bytes 14871552 | tf_op jit(solution)/shard_map/pallas_call | solution.py:85
  (627 shorter events, 253.4 us)
Async XLA Ops:
  11.3 19.0 %collective-permute-start.7 = (bf16[1,96,1664]{2,1,0:T(8,128)(2,1)S(1)}, bf16[1,96,1664]{2,1,0:T(8,128)(2,1)S(1)}, u32[]{:S(2)}, u32[]{:S(2)}) collective-permute-start(bf16[1,96,1664]{2,1,0:T(8,128)(2,1)S(1)} %bitcast.168), channel_id=1, source_target_pairs={{0,4},{4,0},{1,5},{5,1},{2,6},{6,2},{3,7},{7,3},{8,12},{12,8},{9,1... | collective-permute-start | bytes 958472 | tf_op jit(solution)/shard_map/ppermute | solution.py:47
  12.8 20.3 %collective-permute-start.6 = (bf16[1,96,1664]{2,1,0:T(8,128)(2,1)S(1)}, bf16[1,96,1664]{2,1,0:T(8,128)(2,1)S(1)}, u32[]{:S(2)}, u32[]{:S(2)}) collective-permute-start(bf16[1,96,1664]{2,1,0:T(8,128)(2,1)S(1)} %bitcast.169), channel_id=1, source_target_pairs={{0,2},{2,0},{1,3},{3,1},{4,6},{6,4},{5,7},{7,5},{8,10},{10,8},{9,1... | collective-permute-start | bytes 958472 | tf_op jit(solution)/shard_map/ppermute | solution.py:47
  21.6 19.3 %collective-permute-start.1 = (bf16[96,1280]{1,0:T(8,128)(2,1)S(1)}, bf16[96,1280]{1,0:T(8,128)(2,1)S(1)}, u32[]{:S(2)}, u32[]{:S(2)}) collective-permute-start(bf16[96,1280]{1,0:T(8,128)(2,1)S(1)} %shard_map.484), channel_id=1, source_target_pairs={{0,16},{8,24},{16,0},{24,8},{1,17},{9,25},{17,1},{25,9},{2,18},{10... | collective-permute-start | bytes 737288 | tf_op jit(solution)/shard_map/ppermute | solution.py:62
  41.5 30.3 %collective-permute-start.26 = (bf16[64,1920]{1,0:T(8,128)(2,1)S(1)}, bf16[64,1920]{1,0:T(8,128)(2,1)S(1)}, u32[]{:S(2)}, u32[]{:S(2)}) collective-permute-start(bf16[64,1920]{1,0:T(8,128)(2,1)S(1)} %get-tuple-element.301), channel_id=1, source_target_pairs={{0,24},{8,0},{16,8},{24,16},{1,25},{9,1},{17,9},{25,17},{2,26},{10... | collective-permute-start | bytes 737288 | tf_op jit(solution)/shard_map/ppermute | solution.py:62
  45.3 27.0 %collective-permute-start.25 = (bf16[64,1920]{1,0:T(8,128)(2,1)S(1)}, bf16[64,1920]{1,0:T(8,128)(2,1)}, u32[]{:S(2)}, u32[]{:S(2)}) collective-permute-start(bf16[64,1920]{1,0:T(8,128)(2,1)S(1)} %get-tuple-element.301), channel_id=1, source_target_pairs={{0,16},{8,24},{16,0},{24,8},{1,17},{9,25},{17,1},{25,9},{2,18},{10... | collective-permute-start | bytes 737288 | tf_op jit(solution)/shard_map/ppermute | solution.py:62
  46.0 26.7 %collective-permute-start.24 = (bf16[64,1920]{1,0:T(8,128)(2,1)S(1)}, bf16[64,1920]{1,0:T(8,128)(2,1)}, u32[]{:S(2)}, u32[]{:S(2)}) collective-permute-start(bf16[64,1920]{1,0:T(8,128)(2,1)S(1)} %get-tuple-element.301), channel_id=1, source_target_pairs={{0,8},{8,16},{16,24},{24,0},{1,9},{9,17},{17,25},{25,1},{2,10},{10... | collective-permute-start | bytes 737288 | tf_op jit(solution)/shard_map/ppermute | solution.py:62
  67.6 29.0 %collective-permute-start.17 = (bf16[2,96,1280]{2,1,0:T(8,128)(2,1)S(1)}, bf16[2,96,1280]{2,1,0:T(8,128)(2,1)S(1)}, u32[]{:S(2)}, u32[]{:S(2)}) collective-permute-start(bf16[2,96,1280]{2,1,0:T(8,128)(2,1)S(1)} %slice.158), channel_id=1, source_target_pairs={{0,2},{2,0},{1,3},{3,1},{4,6},{6,4},{5,7},{7,5},{8,10},{10,8},{9,1... | collective-permute-start | bytes 1474568 | tf_op jit(solution)/shard_map/ppermute | solution.py:47
  71.7 24.1 %collective-permute-start.22 = (bf16[96,1664]{1,0:T(8,128)(2,1)S(1)}, bf16[96,1664]{1,0:T(8,128)(2,1)S(1)}, u32[]{:S(2)}, u32[]{:S(2)}) collective-permute-start(bf16[96,1664]{1,0:T(8,128)(2,1)S(1)} %get-tuple-element.300), channel_id=1, source_target_pairs={{0,16},{8,24},{16,0},{24,8},{1,17},{9,25},{17,1},{25,9},{2,18},{10... | collective-permute-start | bytes 958472 | tf_op jit(solution)/shard_map/ppermute | solution.py:62
  72.3 23.5 %collective-permute-start.21 = (bf16[96,1664]{1,0:T(8,128)(2,1)S(1)}, bf16[96,1664]{1,0:T(8,128)(2,1)S(1)}, u32[]{:S(2)}, u32[]{:S(2)}) collective-permute-start(bf16[96,1664]{1,0:T(8,128)(2,1)S(1)} %get-tuple-element.300), channel_id=1, source_target_pairs={{0,8},{8,16},{16,24},{24,0},{1,9},{9,17},{17,25},{25,1},{2,10},{10... | collective-permute-start | bytes 958472 | tf_op jit(solution)/shard_map/ppermute | solution.py:62
  72.8 23.0 %collective-permute-start.18 = (bf16[1,96,1280]{2,1,0:T(8,128)(2,1)S(1)}, bf16[1,96,1280]{2,1,0:T(8,128)(2,1)S(1)}, u32[]{:S(2)}, u32[]{:S(2)}) collective-permute-start(bf16[1,96,1280]{2,1,0:T(8,128)(2,1)S(1)} %slice.159), channel_id=1, source_target_pairs={{0,4},{4,0},{1,5},{5,1},{2,6},{6,2},{3,7},{7,3},{8,12},{12,8},{9,1... | collective-permute-start | bytes 737288 | tf_op jit(solution)/shard_map/ppermute | solution.py:47
  97.5 18.5 %collective-permute-start.28 = (bf16[3,96,1664]{2,1,0:T(8,128)(2,1)S(1)}, bf16[3,96,1664]{2,1,0:T(8,128)(2,1)S(1)}, u32[]{:S(2)}, u32[]{:S(2)}) collective-permute-start(bf16[3,96,1664]{2,1,0:T(8,128)(2,1)S(1)} %pad_maximum_fusion.2.refs_1_), channel_id=1, source_target_pairs={{0,4},{4,0},{1,5},{5,1},{2,6},{6,2},{3,7},{7,3},{8,12},{12,8},{9,1... | collective-permute-start | bytes 2875400 | tf_op jit(solution)/shard_map/ppermute | solution.py:47
  121.9 64.8 %collective-permute-start.39 = (bf16[588,1024]{1,0:T(8,128)(2,1)}, bf16[588,1024]{1,0:T(8,128)(2,1)}, u32[]{:S(2)}, u32[]{:S(2)}) collective-permute-start(bf16[588,1024]{1,0:T(8,128)(2,1)} %pad_maximum_fusion.1), channel_id=1, source_target_pairs={{0,16},{8,24},{16,0},{24,8},{1,17},{9,25},{17,1},{25,9},{2,18},{10... | collective-permute-start | bytes 3612680 | tf_op jit(solution)/shard_map/ppermute | solution.py:62
  134.4 24.8 %collective-permute-start.34 = (bf16[3,64,1920]{2,1,0:T(8,128)(2,1)}, bf16[3,64,1920]{2,1,0:T(8,128)(2,1)}, u32[]{:S(2)}, u32[]{:S(2)}) collective-permute-start(bf16[3,64,1920]{2,1,0:T(8,128)(2,1)} %pad_maximum_fusion.5.refs_1_), channel_id=1, source_target_pairs={{0,4},{4,0},{1,5},{5,1},{2,6},{6,2},{3,7},{7,3},{8,12},{12,8},{9,1... | collective-permute-start | bytes 2211848 | tf_op jit(solution)/shard_map/ppermute | solution.py:47
  135.8 23.3 %collective-permute-start.33 = (bf16[3,64,1920]{2,1,0:T(8,128)(2,1)}, bf16[3,64,1920]{2,1,0:T(8,128)(2,1)}, u32[]{:S(2)}, u32[]{:S(2)}) collective-permute-start(bf16[3,64,1920]{2,1,0:T(8,128)(2,1)} %pad_maximum_fusion.5.refs_1_), channel_id=1, source_target_pairs={{0,2},{2,0},{1,3},{3,1},{4,6},{6,4},{5,7},{7,5},{8,10},{10,8},{9,1... | collective-permute-start | bytes 2211848 | tf_op jit(solution)/shard_map/ppermute | solution.py:47
  217.6 19.4 %collective-permute-start.44 = (bf16[2,64,1408]{2,1,0:T(8,128)(2,1)S(1)}, bf16[2,64,1408]{2,1,0:T(8,128)(2,1)S(1)}, u32[]{:S(2)}, u32[]{:S(2)}) collective-permute-start(bf16[2,64,1408]{2,1,0:T(8,128)(2,1)S(1)} %get-tuple-element.348), channel_id=1, source_target_pairs={{0,2},{2,0},{1,3},{3,1},{4,6},{6,4},{5,7},{7,5},{8,10},{10,8},{9,1... | collective-permute-start | bytes 1081352 | tf_op jit(solution)/shard_map/ppermute | solution.py:47
  218.1 18.9 %collective-permute-start.45 = (bf16[2,64,1408]{2,1,0:T(8,128)(2,1)S(1)}, bf16[2,64,1408]{2,1,0:T(8,128)(2,1)S(1)}, u32[]{:S(2)}, u32[]{:S(2)}) collective-permute-start(bf16[2,64,1408]{2,1,0:T(8,128)(2,1)S(1)} %get-tuple-element.349), channel_id=1, source_target_pairs={{0,4},{4,0},{1,5},{5,1},{2,6},{6,2},{3,7},{7,3},{8,12},{12,8},{9,1... | collective-permute-start | bytes 1081352 | tf_op jit(solution)/shard_map/ppermute | solution.py:47
  218.6 30.3 %collective-permute-start.50 = (bf16[2,64,1408]{2,1,0:T(8,128)(2,1)S(1)}, bf16[2,64,1408]{2,1,0:T(8,128)(2,1)S(1)}, u32[]{:S(2)}, u32[]{:S(2)}) collective-permute-start(bf16[2,64,1408]{2,1,0:T(8,128)(2,1)S(1)} %get-tuple-element.372), channel_id=1, source_target_pairs={{0,2},{2,0},{1,3},{3,1},{4,6},{6,4},{5,7},{7,5},{8,10},{10,8},{9,1... | collective-permute-start | bytes 1081352 | tf_op jit(solution)/shard_map/ppermute | solution.py:47
  219.7 29.8 %collective-permute-start.51 = (bf16[2,64,1408]{2,1,0:T(8,128)(2,1)S(1)}, bf16[2,64,1408]{2,1,0:T(8,128)(2,1)S(1)}, u32[]{:S(2)}, u32[]{:S(2)}) collective-permute-start(bf16[2,64,1408]{2,1,0:T(8,128)(2,1)S(1)} %get-tuple-element.373), channel_id=1, source_target_pairs={{0,4},{4,0},{1,5},{5,1},{2,6},{6,2},{3,7},{7,3},{8,12},{12,8},{9,1... | collective-permute-start | bytes 1081352 | tf_op jit(solution)/shard_map/ppermute | solution.py:47
  277.3 21.9 %collective-permute-start.70 = (bf16[2,96,1664]{2,1,0:T(8,128)(2,1)S(1)}, bf16[2,96,1664]{2,1,0:T(8,128)(2,1)S(1)}, u32[]{:S(2)}, u32[]{:S(2)}) collective-permute-start(bf16[2,96,1664]{2,1,0:T(8,128)(2,1)S(1)} %get-tuple-element.437), channel_id=1, source_target_pairs={{0,2},{2,0},{1,3},{3,1},{4,6},{6,4},{5,7},{7,5},{8,10},{10,8},{9,1... | collective-permute-start | bytes 1916936 | tf_op jit(solution)/shard_map/ppermute | solution.py:47
  284.1 22.8 %collective-permute-start.63 = (bf16[2,96,1664]{2,1,0:T(8,128)(2,1)S(1)}, bf16[2,96,1664]{2,1,0:T(8,128)(2,1)S(1)}, u32[]{:S(2)}, u32[]{:S(2)}) collective-permute-start(bf16[2,96,1664]{2,1,0:T(8,128)(2,1)S(1)} %add_convert_fusion.2), channel_id=1, source_target_pairs={{0,2},{2,0},{1,3},{3,1},{4,6},{6,4},{5,7},{7,5},{8,10},{10,8},{9,1... | collective-permute-start | bytes 1916936 | tf_op jit(solution)/shard_map/ppermute | solution.py:47
  284.7 25.9 %collective-permute-start.62 = (bf16[2,96,1664]{2,1,0:T(8,128)(2,1)S(1)}, bf16[2,96,1664]{2,1,0:T(8,128)(2,1)S(1)}, u32[]{:S(2)}, u32[]{:S(2)}) collective-permute-start(bf16[2,96,1664]{2,1,0:T(8,128)(2,1)S(1)} %add_convert_fusion.3), channel_id=1, source_target_pairs={{0,4},{4,0},{1,5},{5,1},{2,6},{6,2},{3,7},{7,3},{8,12},{12,8},{9,1... | collective-permute-start | bytes 1916936 | tf_op jit(solution)/shard_map/ppermute | solution.py:47
  317.8 23.5 %collective-permute-start.84 = (bf16[96,1664]{1,0:T(8,128)(2,1)}, bf16[96,1664]{1,0:T(8,128)(2,1)S(1)}, u32[]{:S(2)}, u32[]{:S(2)}) collective-permute-start(bf16[96,1664]{1,0:T(8,128)(2,1)} %get-tuple-element.556), channel_id=1, source_target_pairs={{0,16},{8,24},{16,0},{24,8},{1,17},{9,25},{17,1},{25,9},{2,18},{10... | collective-permute-start | bytes 958472 | tf_op jit(solution)/shard_map/ppermute | solution.py:62
  319.3 23.9 %collective-permute-start.81 = (bf16[2,96,512]{2,1,0:T(8,128)(2,1)}, bf16[2,96,512]{2,1,0:T(8,128)(2,1)}, u32[]{:S(2)}, u32[]{:S(2)}) collective-permute-start(bf16[2,96,512]{2,1,0:T(8,128)(2,1)} %get-tuple-element.472), channel_id=1, source_target_pairs={{0,2},{2,0},{1,3},{3,1},{4,6},{6,4},{5,7},{7,5},{8,10},{10,8},{9,1... | collective-permute-start | bytes 589832 | tf_op jit(solution)/shard_map/ppermute | solution.py:47
  321.3 22.5 %collective-permute-start.82 = (bf16[2,96,512]{2,1,0:T(8,128)(2,1)}, bf16[2,96,512]{2,1,0:T(8,128)(2,1)}, u32[]{:S(2)}, u32[]{:S(2)}) collective-permute-start(bf16[2,96,512]{2,1,0:T(8,128)(2,1)} %get-tuple-element.473), channel_id=1, source_target_pairs={{0,4},{4,0},{1,5},{5,1},{2,6},{6,2},{3,7},{7,3},{8,12},{12,8},{9,1... | collective-permute-start | bytes 589832 | tf_op jit(solution)/shard_map/ppermute | solution.py:47
  (233 other events, 2034.4 us)
